TPU v7x, 32 devices: a whole 2x2x4 slice. The times are simulated.
32 devices in a mesh: ctx: 8 (over z, x), fsdp: 4 (over y, core).
Axes of the slice: x: 2, y: 2, z: 4, core: 2. Of those that a mesh axis runs over, the one named last changes fastest.
Arguments:
- streams: bfloat16 [4, 1024, 8192], P('fsdp', 'ctx'), may hold values from -6 to 6
- cotangent: bfloat16 [4, 1024, 8192], P('fsdp', 'ctx'), may hold values from -6 to 6
- w_qkv: bfloat16 [2048, 6144], P(('ctx', 'fsdp')), may hold values from -0.125 to 0.125
- w_out: bfloat16 [2048, 2048], P(('ctx', 'fsdp')), may hold values from -0.5 to 0.5
- w_gate_up: bfloat16 [2048, 16384], P(('ctx', 'fsdp')), may hold values from -0.125 to 0.125
- w_down: bfloat16 [8192, 2048], P(('ctx', 'fsdp')), may hold values from -0.0625 to 0.0625
- hc_weight: float32 [2, 2048, 6], replicated, may hold values from -0.125 to 0.125
- hc_static: float32 [2, 4, 6], replicated, may hold values from 0.2 to 0.8
- seq_lengths: int32 [4, 4], replicated, may hold values from 1 to 960, 1024 in all within a row
- pair_perm: int32 [4, 8], replicated, may hold values from 0 to 7, each once within a row
Outputs:
- out_streams: bfloat16 [4, 1024, 8192], P('fsdp', 'ctx')
- grad_streams: bfloat16 [4, 1024, 8192], P('fsdp', 'ctx')
- grad_qkv: float32 [2048, 6144], P(('ctx', 'fsdp'))
- grad_out: float32 [2048, 2048], P(('ctx', 'fsdp'))
- grad_gate_up: float32 [2048, 16384], P(('ctx', 'fsdp'))
- grad_down: float32 [8192, 2048], P(('ctx', 'fsdp'))
- grad_hc_weight: float32 [2, 2048, 6], replicated
- grad_hc_static: float32 [2, 4, 6], replicated
Inputs may be any that keep to these rules, and one draw needn't show every extreme that they name: `seq_lengths`: the lengths of a group sum to 1024; the longest is 960. `pair_perm`: each row is a permutation.
All inputs are finite; a program needn't handle non-finite values.
Results may differ from a plain program's by a relative error of at most 0.039.
Values may be sent and summed in bfloat16 or wider, within the bound.
No kernel may reach another device: no remote copies, remote signals or barrier semaphores. Data moves between devices by JAX's collectives and lax.ppermute only.
A program may use at most 512 MiB of HBM per device.

v0:
```python
import jax
import jax.numpy as jnp
from jax import lax
from jax.sharding import PartitionSpec as P

D = 2048
HEADS = 16
HEAD_DIM = 128
FF = 8192
STREAMS = 4


eps = 1e-05


def places(pair_row, length_row, rows):
    count = pair_row.shape[0]
    half = rows // 2
    index = jnp.arange(count * rows, dtype=jnp.int32)
    owner = index // rows
    slot = index % rows // half
    offset = index % half
    pair = jnp.sum(
        jnp.where(
            owner[:, None] == jnp.arange(count, dtype=jnp.int32)[None, :], pair_row[None, :], 0
        ),
        axis=1,
    )
    block = jnp.where(slot == 0, pair, 2 * count - 1 - pair)
    position = block * half + offset
    ends = jnp.cumsum(length_row)
    starts = ends - length_row
    doc = jnp.sum((position[:, None] >= ends[None, :]).astype(jnp.int32), axis=1)
    seq_ids = jnp.arange(length_row.shape[0], dtype=jnp.int32)
    inside = position - jnp.sum(
        jnp.where(doc[:, None] == seq_ids[None, :], starts[None, :], 0), axis=1
    )
    return (position, doc, inside)


def norm_rows(v):
    mean = jnp.mean(v, axis=-1, keepdims=True)
    cent = v - mean
    return cent * lax.rsqrt(jnp.mean(cent * cent, axis=-1, keepdims=True) + eps)


def mix_in(state, weight, static):
    normed = norm_rows(state)
    coef = static[None] + jnp.tanh(
        jnp.einsum("tnd,dk->tnk", normed, weight, precision=lax.Precision.HIGHEST)
    )
    layer_in = jnp.sum(coef[:, :, 0:1] * state, axis=1)
    return (norm_rows(layer_in), coef[:, :, 1:5], coef[:, :, 5])


def mix_out(state, mixing, beta, branch):
    return (
        jnp.einsum("tij,tid->tjd", mixing, state, precision=lax.Precision.HIGHEST)
        + beta[:, :, None] * branch[:, None, :]
    )


def rotate(v, inside, sign):
    half = v.shape[-1] // 2
    freq = 10000.0 ** (-jnp.arange(half, dtype=jnp.float32) / half)
    angle = inside.astype(jnp.float32)[:, None] * freq[None, :]
    cosine = jnp.cos(angle)[:, None, :]
    sine = sign * jnp.sin(angle)[:, None, :]
    first, second = (v[..., :half], v[..., half:])
    return jnp.concatenate(
        [first * cosine - second * sine, second * cosine + first * sine], axis=-1
    )


def swiglu(gate_up):
    return jax.nn.silu(gate_up[:, :FF]) * gate_up[:, FF:]


def scores_of(query, keys_head, keep):
    scores = jnp.einsum(
        "qhe,hke->hqk", query, keys_head, preferred_element_type=jnp.float32
    ) * HEAD_DIM ** (-0.5)
    return jnp.where(keep[None], scores, -1e30)


def weight_share(term, shard_rows):
    group_rows = shard_rows * lax.axis_size("fsdp")
    partial_rows = lax.psum_scatter(
        term(jnp.int32(0), group_rows * lax.axis_size("ctx")).astype(jnp.bfloat16),
        "ctx",
        scatter_dimension=0,
        tiled=True,
    )
    summed = lax.psum(partial_rows, "fsdp").astype(jnp.float32)
    first = lax.axis_index("fsdp") * shard_rows
    return lax.dynamic_slice_in_dim(summed, first, shard_rows, 0)


def on_device(
    streams,
    cotangent,
    w_qkv,
    w_out,
    w_gate_up,
    w_down,
    hc_weight,
    hc_static,
    seq_lengths,
    pair_perm,
):
    group = lax.axis_index("fsdp")
    place = lax.axis_index("ctx")
    rows = streams.shape[1]
    pair_row = lax.dynamic_index_in_dim(pair_perm, group, 0, keepdims=False)
    length_row = lax.dynamic_index_in_dim(seq_lengths, group, 0, keepdims=False)
    kpos, kdoc, kinside = places(pair_row, length_row, rows)
    start_row = place * rows
    qpos = lax.dynamic_slice_in_dim(kpos, start_row, rows)
    qdoc = lax.dynamic_slice_in_dim(kdoc, start_row, rows)
    qinside = lax.dynamic_slice_in_dim(kinside, start_row, rows)
    keep = (kpos[None, :] <= qpos[:, None]) & (kdoc[None, :] == qdoc[:, None])
    scale = HEAD_DIM ** (-0.5)
    state = streams[0].astype(jnp.float32).reshape(rows, STREAMS, D)
    qkv_full, out_full = (
        lax.all_gather(w_qkv, ("ctx", "fsdp"), axis=0, tiled=True),
        lax.all_gather(w_out, ("ctx", "fsdp"), axis=0, tiled=True),
    )
    (normed, mixing, beta), pull_in = jax.vjp(mix_in, state, hc_weight[0], hc_static[0])
    u_b = normed.astype(jnp.bfloat16)
    qkv = jnp.dot(u_b, qkv_full, preferred_element_type=jnp.float32)
    query = rotate(qkv[:, :D].reshape(rows, HEADS, HEAD_DIM), qinside, 1.0).astype(jnp.bfloat16)
    key_local = rotate(qkv[:, D : 2 * D].reshape(rows, HEADS, HEAD_DIM), qinside, 1.0).astype(
        jnp.bfloat16
    )
    value_local = qkv[:, 2 * D :].reshape(rows, HEADS, HEAD_DIM).astype(jnp.bfloat16)
    keys_head, values_head = (
        lax.all_gather(key_local.transpose(1, 0, 2), "ctx", axis=1, tiled=True),
        lax.all_gather(value_local.transpose(1, 0, 2), "ctx", axis=1, tiled=True),
    )
    scores = scores_of(query, keys_head, keep)
    top = jnp.max(scores, axis=-1, keepdims=True)
    total = jnp.sum(jnp.exp(scores - top), axis=-1, keepdims=True)
    lse = top + jnp.log(total)
    probs_b = jnp.exp(scores - lse).astype(jnp.bfloat16)
    attended = jnp.einsum("hqk,hke->qhe", probs_b, values_head, preferred_element_type=jnp.float32)
    attn_b = attended.reshape(rows, D).astype(jnp.bfloat16)
    branch = jnp.dot(attn_b, out_full, preferred_element_type=jnp.float32)
    mid, pull_out = jax.vjp(mix_out, state, mixing, beta, branch)
    gate_up_full, down_full = (
        lax.all_gather(w_gate_up, ("ctx", "fsdp"), axis=0, tiled=True),
        lax.all_gather(w_down, ("ctx", "fsdp"), axis=0, tiled=True),
    )
    (normed2, mixing2, beta2), pull_in2 = jax.vjp(mix_in, mid, hc_weight[1], hc_static[1])
    u2_b = normed2.astype(jnp.bfloat16)
    gate_up = jnp.dot(u2_b, gate_up_full, preferred_element_type=jnp.float32)
    hidden, pull_act = jax.vjp(swiglu, gate_up)
    hidden_b = hidden.astype(jnp.bfloat16)
    branch2 = jnp.dot(hidden_b, down_full, preferred_element_type=jnp.float32)
    final, pull_out2 = jax.vjp(mix_out, mid, mixing2, beta2, branch2)
    out_streams = final.reshape(1, rows, STREAMS * D).astype(jnp.bfloat16)
    grad_final = cotangent[0].astype(jnp.float32).reshape(rows, STREAMS, D)
    d_mid_direct, d_mixing2, d_beta2, d_branch2 = pull_out2(grad_final)
    dy2_b = d_branch2.astype(jnp.bfloat16)
    d_hidden = jnp.einsum("td,fd->tf", dy2_b, down_full, preferred_element_type=jnp.float32)

    def down_term(start, count):
        return jnp.einsum("tf,td->fd", hidden_b, dy2_b, preferred_element_type=jnp.float32)

    grad_down = weight_share(down_term, w_down.shape[0])
    d_hidden_low = lax.optimization_barrier(d_hidden.astype(jnp.bfloat16)).astype(jnp.float32)
    (d_gate_up,) = pull_act(d_hidden_low)
    dgu_b = d_gate_up.astype(jnp.bfloat16)
    d_normed2 = jnp.einsum("tg,dg->td", dgu_b, gate_up_full, preferred_element_type=jnp.float32)

    def gate_up_term(start, count):
        return jnp.einsum("td,tg->dg", u2_b, dgu_b, preferred_element_type=jnp.float32)

    grad_gate_up = weight_share(gate_up_term, w_gate_up.shape[0])
    d_mid_norm, d_weight1, d_static1 = pull_in2((d_normed2, d_mixing2, d_beta2))
    d_mid = d_mid_direct + d_mid_norm
    d_state_direct, d_mixing, d_beta, d_branch = pull_out(d_mid)
    dy_b = d_branch.astype(jnp.bfloat16)
    qkv_back, out_back = (
        lax.all_gather(w_qkv, ("ctx", "fsdp"), axis=0, tiled=True),
        lax.all_gather(w_out, ("ctx", "fsdp"), axis=0, tiled=True),
    )
    d_attended = jnp.einsum("td,ed->te", dy_b, out_back, preferred_element_type=jnp.float32)
    do_b = d_attended.astype(jnp.bfloat16).reshape(rows, HEADS, HEAD_DIM)

    def out_term(start, count):
        return jnp.einsum("td,te->de", attn_b, dy_b, preferred_element_type=jnp.float32)

    grad_out = weight_share(out_term, w_out.shape[0])
    again = jnp.exp(scores_of(query, keys_head, keep) - lse)
    d_probs = jnp.einsum("qhe,hke->hqk", do_b, values_head, preferred_element_type=jnp.float32)
    delta = jnp.sum(again * d_probs, axis=-1, keepdims=True)
    ds_b = (again * (d_probs - delta)).astype(jnp.bfloat16)
    d_query = (
        jnp.einsum("hqk,hke->qhe", ds_b, keys_head, preferred_element_type=jnp.float32) * scale
    )
    d_keys_all = jnp.einsum("hqk,qhe->hke", ds_b, query, preferred_element_type=jnp.float32) * scale
    d_values_all = jnp.einsum(
        "hqk,qhe->hke", again.astype(jnp.bfloat16), do_b, preferred_element_type=jnp.float32
    )
    d_keys_head, d_values_head = (
        lax.psum_scatter(
            d_keys_all.astype(jnp.bfloat16), "ctx", scatter_dimension=1, tiled=True
        ).astype(jnp.float32),
        lax.psum_scatter(
            d_values_all.astype(jnp.bfloat16), "ctx", scatter_dimension=1, tiled=True
        ).astype(jnp.float32),
    )
    d_keys = d_keys_head.transpose(1, 0, 2)
    d_values = d_values_head.transpose(1, 0, 2)
    d_query_raw = rotate(d_query, qinside, -1.0).reshape(rows, D)
    d_keys_raw = rotate(d_keys, qinside, -1.0).reshape(rows, D)
    d_qkv_b = jnp.concatenate([d_query_raw, d_keys_raw, d_values.reshape(rows, D)], axis=1).astype(
        jnp.bfloat16
    )
    d_normed = jnp.einsum("tc,dc->td", d_qkv_b, qkv_back, preferred_element_type=jnp.float32)

    def qkv_term(start, count):
        return jnp.einsum("td,tc->dc", u_b, d_qkv_b, preferred_element_type=jnp.float32)

    grad_qkv = weight_share(qkv_term, w_qkv.shape[0])
    d_state_norm, d_weight0, d_static0 = pull_in((d_normed, d_mixing, d_beta))
    d_state = d_state_direct + d_state_norm
    grad_streams = d_state.reshape(1, rows, STREAMS * D).astype(jnp.bfloat16)
    weight_terms = jnp.stack([d_weight0, d_weight1], axis=0)
    static_terms = jnp.stack([d_static0, d_static1], axis=0)
    grad_hc_weight, grad_hc_static = lax.psum((weight_terms, static_terms), ("ctx", "fsdp"))
    return (
        out_streams,
        grad_streams,
        grad_qkv,
        grad_out,
        grad_gate_up,
        grad_down,
        grad_hc_weight,
        grad_hc_static,
    )


def solution(mesh):
    return jax.shard_map(
        on_device,
        mesh=mesh,
        in_specs=(
            P("fsdp", "ctx", None),
            P("fsdp", "ctx", None),
            P(("ctx", "fsdp"), None),
            P(("ctx", "fsdp"), None),
            P(("ctx", "fsdp"), None),
            P(("ctx", "fsdp"), None),
            P(),
            P(),
            P(),
            P(),
        ),
        out_specs=(
            P("fsdp", "ctx", None),
            P("fsdp", "ctx", None),
            P(("ctx", "fsdp"), None),
            P(("ctx", "fsdp"), None),
            P(("ctx", "fsdp"), None),
            P(("ctx", "fsdp"), None),
            P(),
            P(),
        ),
        check_vma=False,
    )
```

profile of v0, /device:TPU:0, one launch (start us, length us, event | category | flops | bytes accessed | tf_op | source)
XLA Modules:
  0.0 3874.3 jit_solution(7618139894890489400)
XLA Ops:
  8.0 3.3 squeeze.14
  16.6 6.1 mul.514
  25.3 6.1 sub.123
  31.4 6.8 fusion.6
  38.3 6.1 mul.516
  45.1 8.7 broadcast_add_fusion.2
  56.5 6.3 mul.522
  63.5 3.4 fusion.7
  66.9 3.5 fusion.14
  71.5 96.7 %all-gather.7.cloned.1.call-done = bf16[2048,6144]{1,0:T(8,128)(2,1)} async-done(((bf16[64,6144]{1,0:T(8,128)(2,1)}), bf16[2048,6144]{1,0:T(8,128)(2,1)}) %all-gather.7.cloned.1.call-update) | async-done | bytes 25165840 | tf_op jit(solution)/shard_map/all_gather | solution.py:125
  168.3 10.1 fusion.97
  190.5 4.9 reshape.482
  195.5 59.5 %all-gather.11.cloned.1.call-done = bf16[16,1024,128]{2,1,0:T(8,128)(2,1)} async-done(((bf16[16,128,128]{2,1,0:T(8,128)(2,1)}), bf16[16,1024,128]{2,1,0:T(8,128)(2,1)}) %all-gather.11.cloned.1.call-update) | async-done | bytes 4194320 | tf_op jit(solution)/shard_map/all_gather | solution.py:137
  255.0 4.3 fusion
  262.6 68.3 %all-gather.9.cloned.1.call-done = bf16[16,1024,128]{1,2,0:T(8,128)(2,1)} async-done(((bf16[16,128,128]{1,2,0:T(8,128)(2,1)}), bf16[16,1024,128]{1,2,0:T(8,128)(2,1)}) %all-gather.9.cloned.1.call-update) | async-done | bytes 4194320 | tf_op jit(solution)/shard_map/all_gather | solution.py:138
  331.0 7.2 convolution_convert_fusion.7
  338.1 71.4 %all-gather.13.cloned.1.call-done = bf16[2048,2048]{1,0:T(8,128)(2,1)} async-done(((bf16[64,2048]{1,0:T(8,128)(2,1)}), bf16[2048,2048]{1,0:T(8,128)(2,1)}) %all-gather.13.cloned.1.call-update) | async-done | bytes 8388624 | tf_op jit(solution)/shard_map/all_gather | solution.py:126
  409.5 4.7 fusion.108
  414.2 6.0 fusion.107
  424.3 3.1 subtract_multiply_fusion.1
  429.5 6.0 broadcast_add_fusion.3
  437.0 10.9 fusion.110
  448.3 5.4 multiply_reduce_fusion.6
  453.9 313.2 %all-gather.15.cloned.1.call-done = bf16[2048,16384]{1,0:T(8,128)(2,1)} async-done(((bf16[64,16384]{1,0:T(8,128)(2,1)}), bf16[2048,16384]{1,0:T(8,128)(2,1)}) %all-gather.15.cloned.1.call-update) | async-done | bytes 67108880 | tf_op jit(solution)/shard_map/all_gather | solution.py:150
  767.1 27.4 fusion.98
  794.5 6.0 multiply_convert_fusion.2
  800.4 162.4 %all-gather.17.cloned.1.call-done = bf16[8192,2048]{1,0:T(8,128)(2,1)} async-done(((bf16[256,2048]{1,0:T(8,128)(2,1)}), bf16[8192,2048]{1,0:T(8,128)(2,1)}) %all-gather.17.cloned.1.call-update) | async-done | bytes 33554448 | tf_op jit(solution)/shard_map/all_gather | solution.py:151
  962.8 13.6 fusion.109
  977.4 5.1 fusion.9
  982.6 15.9 convolution_convert_fusion.3
  998.5 6.5 convert_multiply_fusion.3
  1004.9 31.4 multiply_reduce_fusion.9
  1040.1 3.5 fusion.52
  1049.4 7.1 fusion.99
  1057.1 15.5 multiply_reduce_fusion.1
  1072.6 6.6 fusion.32
  1079.2 3.4 multiply_reduce_fusion
  1087.5 4.0 multiply_convert_fusion
  1092.5 8.1 convolution_convert_fusion.5
  1101.7 5.7 convolution_convert_fusion.4
  1107.5 4.8 fusion.31
  1112.3 66.0 %reduce-scatter.7.cloned.1.call-done = bf16[16,128,128]{2,1,0:T(8,128)(2,1)} async-done(((bf16[16,1024,128]{2,1,0:T(8,128)(2,1)}), bf16[16,128,128]{2,1,0:T(8,128)(2,1)}) %reduce-scatter.7.cloned.1.call-update) | async-done | bytes 524304 | tf_op jit(solution)/shard_map/reduce_scatter | solution.py:206
  1188.1 82.5 %reduce-scatter.9.cloned.1.call-done = bf16[16,128,128]{2,1,0:T(8,128)(2,1)} async-done(((bf16[16,1024,128]{2,1,0:T(8,128)(2,1)}), bf16[16,128,128]{2,1,0:T(8,128)(2,1)}) %reduce-scatter.9.cloned.1.call-update) | async-done | bytes 524304 | tf_op jit(solution)/shard_map/reduce_scatter | solution.py:209
  1272.6 13.7 convolution_convert_fusion.2
  1287.3 15.6 convolution_convert_fusion.1
  1303.0 29.4 convolution_convert_fusion
  1334.0 11.3 fusion.111
  1347.7 7.3 fusion.25
  1355.0 14.6 multiply_reduce_fusion.8
  1373.7 3.5 fusion.53
  1382.3 7.6 fusion.1
  1389.9 4.6 fusion.28
  1395.2 27.8 reduce-scatter.13.cloned.1.call-done
  1423.0 407.0 %reduce-scatter.11.cloned.1.call-done = bf16[256,6144]{1,0:T(8,128)(2,1)} async-done(((bf16[2048,6144]{1,0:T(8,128)(2,1)}), bf16[256,6144]{1,0:T(8,128)(2,1)}) %reduce-scatter.11.cloned.1.call-update) | async-done | bytes 3145744 | tf_op jit(solution)/shard_map/reduce_scatter | solution.py:88
  1830.0 546.6 %reduce-scatter.17.cloned.1.call-done = bf16[1024,2048]{1,0:T(8,128)(2,1)} async-done(((bf16[8192,2048]{1,0:T(8,128)(2,1)}), bf16[1024,2048]{1,0:T(8,128)(2,1)}) %reduce-scatter.17.cloned.1.call-update) | async-done | bytes 4194320 | tf_op jit(solution)/shard_map/reduce_scatter | solution.py:88
  2376.7 1059.4 %reduce-scatter.15.cloned.1.call-done = bf16[256,16384]{1,0:T(8,128)(2,1)} async-done(((bf16[2048,16384]{1,0:T(8,128)(2,1)}), bf16[256,16384]{1,0:T(8,128)(2,1)}) %reduce-scatter.15.cloned.1.call-update) | async-done | bytes 8388624 | tf_op jit(solution)/shard_map/reduce_scatter | solution.py:88
  3437.4 12.8 add_convert_fusion.2
  3450.2 4.6 convert_element_type.174
  3454.9 15.2 add_convert_fusion.1
  3470.2 4.5 convert_element_type.186
  3474.7 39.4 %psum.47 = f32[2,4,6]{2,1,0:T(4,128)} all-reduce(f32[2,4,6]{2,1,0:T(4,128)S(1)} %pad_maximum_fusion.9), channel_id=1, replica_groups=mesh['ctx'=8,'fsdp'=4] {'ctx','fsdp'}, use_global_device_ids=true, to_apply=%region_44.45 | all-reduce | flops 48 | bytes 384 | tf_op jit(solution)/shard_map/psum | solution.py:231
  3514.2 50.7 %all-reduce.12.cloned.1.call-done = f32[2,2048,6]{1,2,0:T(8,128)} async-done(((f32[2,2048,6]{1,2,0:T(8,128)}), f32[2,2048,6]{1,2,0:T(8,128)}) %all-reduce.12.cloned.1.call-update) | async-done | bytes 98320 | tf_op jit(solution)/shard_map/psum | solution.py:231
  3566.5 290.2 %all-reduce.14.cloned.1.call-done = (bf16[256,6144]{1,0:T(8,128)(2,1)}, bf16[256,2048]{1,0:T(8,128)(2,1)}, bf16[256,16384]{1,0:T(8,128)(2,1)}, bf16[1024,2048]{1,0:T(8,128)(2,1)}) async-done(((bf16[256,6144]{1,0:T(8,128)(2,1)}, bf16[256,2048]{1,0:T(8,128)(2,1)}, bf16[256,16384]{1,0:T(8,128)(2,1)}, bf16[1024,2048]{1,0:T(8,128)(2,1)}), (bf16[256,6144]{1,0:T(8,128)(2,1)}, bf16[256,2048]{1,0:T(8,128)(2,1)}, ...) | async-done | bytes 16777232 | tf_op jit(solution)/shard_map/psum | solution.py:94
  3856.7 3.9 dynamic-slice_convert_fusion
  (303 shorter events, 92.2 us)
Async XLA Ops:
  7.2 55.9 %copy-start = (s32[4,8]{1,0:T(4,128)S(1)}, s32[4,8]{1,0:T(4,128)}, u32[]{:S(2)}) copy-start(s32[4,8]{1,0:T(4,128)} %param.19) | copy-start | bytes 388
  7.2 161.1 %all-gather.7.cloned.1.call-start = ((), (), s32[]{:S(2)}) async-start(), calls=%async_computation.6 | async-start | bytes 25952256 | tf_op jit(solution)/shard_map/all_gather | solution.py:125
  7.9 247.1 %all-gather.11.cloned.1.call-start = ((), (), s32[]{:S(2)}) async-start(), calls=%async_computation.8 | async-start | bytes 4718592 | tf_op jit(solution)/shard_map/all_gather | solution.py:137
  11.3 402.9 %copy-start.7 = (bf16[128,4,2048]{2,1,0:T(4,128)(2,1)}, bf16[128,4,2048]{2,1,0:T(4,128)(2,1)S(1)}, u32[]{:S(2)}) copy-start(bf16[128,4,2048]{2,1,0:T(4,128)(2,1)S(1)} %squeeze.14) | copy-start | bytes 6291460
  12.2 10.5 copy-start.35
  13.8 8.9 copy-start.77
  13.9 8.7 copy-start.44
  38.3 6.1 copy-start.81
  38.3 6.1 copy-start.62
  44.5 382.9 %copy-start.40 = (f32[1,2048,6]{1,0,2:T(1,128)}, f32[1,2048,6]{1,0,2:T(1,128)S(1)}, u32[]{:S(2)}) copy-start(f32[1,2048,6]{1,0,2:T(1,128)S(1)} %get-tuple-element.92) | copy-start | bytes 147460
  53.9 12.9 copy-start.47
  56.5 6.3 copy-start.84
  66.8 111.5 %copy-start.71 = (f32[128]{0:T(128)}, f32[128]{0:T(128)S(1)}, u32[]{:S(2)}) copy-start(f32[128]{0:T(128)S(1)} %broadcast_multiply_fusion.4) | copy-start | bytes 1540
  70.3 108.1 %copy-start.13 = (f32[128,2048]{1,0:T(8,128)}, f32[128,2048]{1,0:T(8,128)S(1)}, u32[]{:S(2)}) copy-start(f32[128,2048]{1,0:T(8,128)S(1)} %fusion.14) | copy-start | bytes 3145732
  70.6 107.8 %copy-start.82 = (f32[128]{0:T(128)}, f32[128]{0:T(128)S(1)}, u32[]{:S(2)}) copy-start(f32[128]{0:T(128)S(1)} %multiply_reduce_fusion.11) | copy-start | bytes 1540
  70.6 107.8 %copy-start.74 = (f32[128]{0:T(128)}, f32[128]{0:T(128)S(1)}, u32[]{:S(2)}) copy-start(f32[128]{0:T(128)S(1)} %fusion.76) | copy-start | bytes 1540
  71.5 109.2 %copy-start.42 = (f32[128,64]{1,0:T(8,128)}, f32[128,64]{1,0:T(8,128)S(1)}, u32[]{:S(2)}) copy-start(f32[128,64]{1,0:T(8,128)S(1)} %get-tuple-element.102) | copy-start | bytes 98308
  182.2 72.9 %copy-start.23 = (bf16[128,16,64]{2,0,1:T(8,128)(2,1)}, bf16[128,16,64]{2,0,1:T(8,128)(2,1)S(1)}, u32[]{:S(2)}) copy-start(bf16[128,16,64]{2,0,1:T(8,128)(2,1)S(1)} %get-tuple-element.76) | copy-start | bytes 786436
  182.2 72.9 %copy-start.25 = (bf16[128,16,64]{2,0,1:T(8,128)(2,1)}, bf16[128,16,64]{2,0,1:T(8,128)(2,1)S(1)}, u32[]{:S(2)}) copy-start(bf16[128,16,64]{2,0,1:T(8,128)(2,1)S(1)} %get-tuple-element.77) | copy-start | bytes 786436
  183.3 147.6 %all-gather.9.cloned.1.call-start = ((), (), s32[]{:S(2)}) async-start(), calls=%async_computation.7 | async-start | bytes 4718592 | tf_op jit(solution)/shard_map/all_gather | solution.py:138
  187.5 222.0 %all-gather.13.cloned.1.call-start = ((), (), s32[]{:S(2)}) async-start(), calls=%async_computation.9 | async-start | bytes 8650752 | tf_op jit(solution)/shard_map/all_gather | solution.py:126
  188.1 579.0 %all-gather.15.cloned.1.call-start = ((), (), s32[]{:S(2)}) async-start(), calls=%async_computation.10 | async-start | bytes 69206016 | tf_op jit(solution)/shard_map/all_gather | solution.py:150
  188.7 774.1 %all-gather.17.cloned.1.call-start = ((), (), s32[]{:S(2)}) async-start(), calls=%async_computation.11 | async-start | bytes 34603008 | tf_op jit(solution)/shard_map/all_gather | solution.py:151
  189.3 989.0 %reduce-scatter.7.cloned.1.call-start = ((), (), s32[]{:S(2)}) async-start(), calls=%async_computation.12 | async-start | bytes 4718592 | tf_op jit(solution)/shard_map/reduce_scatter | solution.py:206
  189.6 224.6 %copy-start.64 = (f32[128,4]{1,0:T(8,128)}, f32[128,4]{1,0:T(8,128)S(1)}, u32[]{:S(2)}) copy-start(f32[128,4]{1,0:T(8,128)S(1)} %copy.222) | copy-start | bytes 6148
  414.2 6.0 copy-start.37
  427.4 9.6 copy-start.19
  435.5 604.6 %copy-start.58 = (f32[128,4,6]{0,2,1:T(8,128)}, f32[128,4,6]{0,2,1:T(8,128)S(1)}, u32[]{:S(2)}) copy-start(f32[128,4,6]{0,2,1:T(8,128)S(1)} %get-tuple-element.110) | copy-start | bytes 36868
  800.4 177.0 %copy-start.49 = (f32[128,4]{1,0:T(8,128)S(1)}, f32[128,4]{1,0:T(8,128)}, u32[]{:S(2)}) copy-start(f32[128,4]{1,0:T(8,128)} %copy.236) | copy-start | bytes 6148
  962.8 14.6 copy-start.20
  982.6 15.9 copy-start.21
  1040.1 8.4 copy-start.65
  1040.1 5.5 copy-start.4
  1049.4 7.7 copy-start.5
  1049.4 29.8 slice-start
  1057.1 22.1 slice-start.1
  1072.6 6.6 copy-start.30
  1082.6 4.8 copy-start.24
  1082.6 4.8 copy-start.26
  1091.5 179.1 %reduce-scatter.9.cloned.1.call-start = ((), (), s32[]{:S(2)}) async-start(), calls=%async_computation.13 | async-start | bytes 4718592 | tf_op jit(solution)/shard_map/reduce_scatter | solution.py:209
  1100.7 322.3 %reduce-scatter.13.cloned.1.call-start = ((), (), s32[]{:S(2)}) async-start(), calls=%async_computation.15 | async-start | bytes 9437184 | tf_op jit(solution)/shard_map/reduce_scatter | solution.py:88
  1107.4 72.0 %copy-start.43 = (f32[128,64]{1,0:T(8,128)S(1)}, f32[128,64]{1,0:T(8,128)}, u32[]{:S(2)}) copy-start(f32[128,64]{1,0:T(8,128)} %copy-done.42) | copy-start | bytes 98308
  1107.4 72.0 %copy-start.50 = (f32[128,64]{1,0:T(8,128)S(1)}, f32[128,64]{1,0:T(8,128)}, u32[]{:S(2)}) copy-start(f32[128,64]{1,0:T(8,128)} %get-tuple-element.100) | copy-start | bytes 98308
  1107.4 722.6 %reduce-scatter.11.cloned.1.call-start = ((), (), s32[]{:S(2)}) async-start(), calls=%async_computation.14 | async-start | bytes 28311552 | tf_op jit(solution)/shard_map/reduce_scatter | solution.py:88
  1181.2 91.5 %copy-start.14 = (f32[128,2048]{1,0:T(8,128)S(1)}, f32[128,2048]{1,0:T(8,128)}, u32[]{:S(2)}) copy-start(f32[128,2048]{1,0:T(8,128)} %copy-done.13) | copy-start | bytes 3145732
  1181.2 91.5 %copy-start.72 = (f32[128]{0:T(128)S(1)}, f32[128]{0:T(128)}, u32[]{:S(2)}) copy-start(f32[128]{0:T(128)} %copy-done.71) | copy-start | bytes 1540
  1181.2 91.5 %copy-start.75 = (f32[128]{0:T(128)S(1)}, f32[128]{0:T(128)}, u32[]{:S(2)}) copy-start(f32[128]{0:T(128)} %copy-done.74) | copy-start | bytes 1540
  1183.6 102.7 %copy-start.31 = (bf16[128,16,128]{0,2,1:T(8,128)(2,1)}, bf16[128,16,128]{0,2,1:T(8,128)(2,1)S(1)}, u32[]{:S(2)}) copy-start(bf16[128,16,128]{0,2,1:T(8,128)(2,1)S(1)} %copy.253) | copy-start | bytes 1572868
  1286.3 1090.4 %reduce-scatter.17.cloned.1.call-start = ((), (), s32[]{:S(2)}) async-start(), calls=%async_computation.17 | async-start | bytes 37748736 | tf_op jit(solution)/shard_map/reduce_scatter | solution.py:88
  1303.0 2133.2 %reduce-scatter.15.cloned.1.call-start = ((), (), s32[]{:S(2)}) async-start(), calls=%async_computation.16 | async-start | bytes 75497472 | tf_op jit(solution)/shard_map/reduce_scatter | solution.py:88
  1332.5 14.6 copy-start.63
  1332.5 15.3 copy-start.59
  1332.5 15.3 copy-start.66
  1332.5 2232.4 %all-reduce.12.cloned.1.call-start = ((), (), s32[]{:S(2)}) async-start(), calls=%async_computation.18 | async-start | bytes 262144 | tf_op jit(solution)/shard_map/psum | solution.py:231
  1345.3 9.7 copy-start.15
  1355.0 14.6 copy-start.83
  1355.0 14.6 copy-start.73
  1355.0 14.6 copy-start.76
  1372.4 6.8 copy-start.36
  1373.7 16.2 copy-start.69
  1382.2 7.6 copy-start.51
  1382.2 7.6 copy-start.57
  1395.2 2461.5 %all-reduce.14.cloned.1.call-start = ((), (), s32[]{:S(2)}) async-start(), calls=%async_computation.19 | async-start | bytes 33554432 | tf_op jit(solution)/shard_map/psum | solution.py:94
  3856.7 10.8 copy-start.1
  (37 other events, 102.0 us)
Sparse Core Ops, SparseCore 0:
  10.9 157.3 all-gather.6
  183.4 71.5 all-gather.10
  257.6 73.2 all-gather.8
  333.7 75.7 all-gather.12
  412.2 354.8 all-gather.14
  769.8 192.9 all-gather.16
  1091.6 86.6 reduce-scatter.6
  1182.4 88.1 reduce-scatter.8
  1274.2 148.7 reduce-scatter.12
  1427.3 402.7 reduce-scatter.10
  1834.3 542.3 reduce-scatter.16
  2380.8 1055.2 reduce-scatter.14
  3443.2 121.6 all-reduce.11
  3567.8 288.8 all-reduce.13
where the time goes:
time: 3880 us; the launch traced here: 3870 us
  waiting for transfers between devices  3300 us (85%)
  matrix products  326 us (8%)
  other arithmetic  96.8 us (2%)
  local copies, waits for them, and re-layouts  92.2 us (2%)
  blocking collectives  39.4 us (1%)
    reduce_scatter x4, waiting for transfers between devices, weight_share(): lax.psum_scatter(term(jnp.int32(0), group_rows * lax.axis_size('ctx')).as...  2040 us
    all_gather x1, waiting for transfers between devices, on_device(): lax.all_gather(w_gate_up, ('ctx', 'fsdp'), axis=0, tiled=True)  313 us
    psum x1, waiting for transfers between devices, weight_share(): summed = lax.psum(partial_rows, 'fsdp').astype(jnp.float32)  290 us
    all_gather x1, waiting for transfers between devices, on_device(): lax.all_gather(w_down, ('ctx', 'fsdp'), axis=0, tiled=True)  162 us
    all_gather x1, waiting for transfers between devices, on_device(): lax.all_gather(w_qkv, ('ctx', 'fsdp'), axis=0, tiled=True)  96.7 us
    reduce_scatter x1, waiting for transfers between devices, on_device(): lax.psum_scatter(d_values_all.astype(jnp.bfloat16), 'ctx', scatter_dimens...  82.5 us
  transfers between devices with their start and end apart: 14, of which 14 were waited for; matrix products, arithmetic and copies ran while one was open for 9% of the time, Pallas kernels for 0%

commit v1 on v0

v1 whole, which is shorter than its diff:
```python
import functools

import jax
import jax.numpy as jnp
from jax import lax
from jax.experimental import pallas as pl
from jax.experimental.pallas import tpu as pltpu
from jax.sharding import PartitionSpec as P

D = 2048
HEADS = 16
HEAD_DIM = 128
FF = 8192
STREAMS = 4
SCALE = HEAD_DIM ** (-0.5)

eps = 1e-05
F32 = jnp.float32
BF16 = jnp.bfloat16
MIB = 1 << 20


def doc_of(position, length_row):
    ends = jnp.cumsum(length_row)
    starts = ends - length_row
    doc = jnp.sum((position[:, None] >= ends[None, :]).astype(jnp.int32), axis=1)
    seq_ids = jnp.arange(length_row.shape[0], dtype=jnp.int32)
    start = jnp.sum(jnp.where(doc[:, None] == seq_ids[None, :], starts[None, :], 0), axis=1)
    return (doc, start)


def places(pair_row, length_row, rows, owners):
    count = pair_row.shape[0]
    half = rows // 2
    ids = jnp.arange(count, dtype=jnp.int32)
    pair = jnp.sum(jnp.where(owners[:, None] == ids[None, :], pair_row[None, :], 0), axis=1)
    block = jnp.stack([pair, 2 * count - 1 - pair], axis=1)
    offset = jnp.arange(half, dtype=jnp.int32)
    position = (block[:, :, None] * half + offset[None, None, :]).reshape(-1)
    doc, start = doc_of(position, length_row)
    return (position, doc, start)


def ring_order(n):
    return list(range(0, n, 2)) + list(range(n - 1, 0, -2)) if n % 2 == 0 else list(range(n))


def ring_perms(n):
    order = ring_order(n)
    ahead = [(order[i], order[(i + 1) % n]) for i in range(n)]
    return (ahead, [(b, a) for a, b in ahead])


def ring_offsets(n):
    offsets = [0]
    for k in range(1, n // 2):
        offsets += [-k, k]
    return offsets + [-(n // 2)]


def ring_owners(n, place):
    order = jnp.array(ring_order(n), dtype=jnp.int32)
    ids = jnp.arange(n, dtype=jnp.int32)
    mine = jnp.sum(jnp.where(order == place, ids, 0))
    at = (mine + jnp.array(ring_offsets(n), dtype=jnp.int32)) % n
    return jnp.sum(jnp.where(at[:, None] == ids[None, :], order[None, :], 0), axis=1)


def ring_gather(block):
    n = lax.axis_size("ctx")
    ahead, back = ring_perms(n)
    one = other = block
    blocks = [block]
    for k in range(1, n // 2 + 1):
        if 2 * k == n:
            half = block.shape[0] // 2
            one = lax.ppermute(one[:half], "ctx", ahead)
            other = lax.ppermute(other[half:], "ctx", back)
        else:
            one = lax.ppermute(one, "ctx", ahead)
            other = lax.ppermute(other, "ctx", back)
        blocks += [one, other]
    return jnp.concatenate(blocks, axis=0)


def ring_scatter(partial, rows):
    n = lax.axis_size("ctx")
    ahead, back = ring_perms(n)
    offsets = ring_offsets(n)

    def part(offset):
        at = offsets.index(offset)
        return partial[at * rows : (at + 1) * rows]

    def add(moving, offset, first, last):
        own = part(offset)
        sent = [own[:first], own[first:last], own[last:]]
        sent[1] = (moving.astype(F32) + sent[1].astype(F32)).astype(BF16)
        return jnp.concatenate(sent, axis=0)

    half = n // 2
    mid = rows // 2
    one, other = part(-half)[:mid], part(-half)[mid:]
    span_one, span_other = (0, mid), (mid, rows)
    for k in range(half - 1, 0, -1):
        one = add(lax.ppermute(one, "ctx", ahead), k, *span_one)
        other = add(lax.ppermute(other, "ctx", back), -k, *span_other)
        span_one = span_other = (0, rows)
    one = lax.ppermute(one, "ctx", ahead).astype(F32)
    other = lax.ppermute(other, "ctx", back).astype(F32)
    if half == 1:
        return part(0).astype(F32) + jnp.concatenate([one, other], axis=0)
    return part(0).astype(F32) + one + other


def to_columns(weight, parts):
    n = lax.axis_size("ctx")
    place = lax.axis_index("ctx")
    rows = weight.shape[0]
    width = weight.shape[1] // parts // n
    if n <= 8:

        def piece(dest):
            return jnp.concatenate(
                [
                    lax.dynamic_slice_in_dim(weight, (p * n + dest) * width, width, 1)
                    for p in range(parts)
                ],
                axis=1,
            )

        held = jnp.zeros((n, rows, parts * width), weight.dtype)
        for k in range(n):
            got = piece((place + k) % n)
            if k:
                got = lax.ppermute(got, "ctx", [(i, (i + k) % n) for i in range(n)])
            held = lax.dynamic_update_slice_in_dim(held, got[None], (place - k) % n, 0)
    else:
        cut = weight.reshape(rows, parts, n, width).transpose(2, 0, 1, 3)
        held = lax.all_to_all(cut.reshape(n, rows, parts * width), "ctx", 0, 0, tiled=True)
    full = lax.all_gather(held.reshape(n * rows, parts * width), "fsdp", axis=0, tiled=True)
    return full


def to_rows(gradient, parts):
    n = lax.axis_size("ctx")
    place = lax.axis_index("ctx")
    mine = lax.psum_scatter(gradient.astype(BF16), "fsdp", scatter_dimension=0, tiled=True)
    rows = mine.shape[0] // n
    width = mine.shape[1] // parts
    if n <= 8:
        out = jnp.zeros((rows, parts * n * width), F32)
        for k in range(n):
            got = lax.dynamic_slice_in_dim(mine, (place + k) % n * rows, rows, 0)
            if k:
                got = lax.ppermute(got, "ctx", [(i, (i + k) % n) for i in range(n)])
            got = got.astype(F32)
            source = (place - k) % n
            for p in range(parts):
                out = lax.dynamic_update_slice_in_dim(
                    out, got[:, p * width : (p + 1) * width], (p * n + source) * width, 1
                )
        return out
    got = lax.all_to_all(mine.reshape(n, rows, parts * width), "ctx", 0, 0, tiled=True)
    got = got.reshape(n, rows, parts, width).transpose(1, 2, 0, 3)
    return got.reshape(rows, parts * n * width).astype(F32)


def share_rows(gradient):
    mine = lax.psum_scatter(gradient.astype(BF16), "fsdp", scatter_dimension=0, tiled=True)
    return mine.astype(F32)


def weight_share(gradient, shard_rows):
    partial_rows = lax.psum_scatter(
        gradient.astype(BF16), "ctx", scatter_dimension=0, tiled=True
    )
    return lax.psum_scatter(partial_rows, "fsdp", scatter_dimension=0, tiled=True).astype(F32)


def spread_columns(v):
    n, m = lax.axis_size("ctx"), lax.axis_size("fsdp")
    rows = v.shape[0]
    return v.reshape(rows, n, m, D // (n * m)).transpose(0, 2, 1, 3).reshape(rows, D)


def unspread_columns(v):
    n, m = lax.axis_size("ctx"), lax.axis_size("fsdp")
    rows = v.shape[0]
    return v.reshape(rows, m, n, D // (n * m)).transpose(0, 2, 1, 3).reshape(rows, D)


def sum_all(v):
    for axis in ("ctx", "fsdp"):
        n = lax.axis_size(axis)
        if n & (n - 1):
            v = lax.psum(v, axis)
            continue
        step = 1
        while step < n:
            v = v + lax.ppermute(v, axis, [(i, i ^ step) for i in range(n)])
            step *= 2
    return v


LANES = 128
HC_ROWS = 32


def lanes_of(rows):
    return lax.broadcasted_iota(jnp.int32, (rows, LANES), 1)


def put(held, lane, at, column):
    return jnp.where(lane == at, column, held)


def mean_of(v):
    return jnp.sum(v, axis=1, keepdims=True) * (1.0 / D)


def stream_parts(ref):
    return [ref[:, i * D : (i + 1) * D].astype(F32) for i in range(STREAMS)]


def mixed(parts, coef, branch):
    outs = []
    for j in range(STREAMS):
        total = coef[:, 8 * j + 5 : 8 * j + 6] * branch
        for i in range(STREAMS):
            total = total + coef[:, 8 * i + 1 + j : 8 * i + 2 + j] * parts[i]
        outs.append(total)
    return outs


def branch_grad(parts, coef):
    return sum(coef[:, 8 * j + 5 : 8 * j + 6] * parts[j] for j in range(STREAMS))


def layer_in(parts, coef):
    return sum(coef[:, 8 * i : 8 * i + 1] * parts[i] for i in range(STREAMS))


def enter(parts, wpack, static):
    rows = parts[0].shape[0]
    lane = lanes_of(rows)
    aux = jnp.zeros((rows, LANES), F32)
    pieces = ([], [], [])
    for i in range(STREAMS):
        mean = mean_of(parts[i])
        cent = parts[i] - mean
        rstd = lax.rsqrt(mean_of(cent * cent) + eps)
        left = cent * rstd
        for piece in pieces:
            piece.append(left.astype(BF16))
            left = left - piece[-1].astype(F32)
        aux = put(aux, lane, 8 * i + 6, mean)
        aux = put(aux, lane, 8 * i + 7, rstd)
    dims = (((1,), (1,)), ((), ()))
    proj = sum(
        lax.dot_general(jnp.concatenate(p, axis=0), wpack, dims, preferred_element_type=F32)
        for p in pieces[::-1]
    )
    proj = proj + pltpu.roll(proj, LANES - 32, 1) + pltpu.roll(proj, LANES - 64, 1)
    for i in range(STREAMS):
        own = jnp.where(lane < 6, proj[i * rows : (i + 1) * rows], 0.0)
        aux += own if i == 0 else pltpu.roll(own, 8 * i, 1)
    coef = static + jnp.tanh(aux)
    x = layer_in(parts, coef)
    mean = mean_of(x)
    cent = x - mean
    rstd = lax.rsqrt(mean_of(cent * cent) + eps)
    aux = put(aux, lane, 32, mean)
    aux = put(aux, lane, 33, rstd)
    return (aux, coef, cent * rstd)


def leave_grads(parts, grads, branch):
    rows = parts[0].shape[0]
    lane = lanes_of(rows)
    red = jnp.zeros((rows, LANES), F32)
    for j in range(STREAMS):
        red = put(red, lane, 8 * j + 5, jnp.sum(grads[j] * branch, axis=1, keepdims=True))
        for i in range(STREAMS):
            red = put(
                red, lane, 8 * i + 1 + j, jnp.sum(parts[i] * grads[j], axis=1, keepdims=True)
            )
    return red


def enter_back(parts, grads, aux, coef, red, du, wpack, normed_ref, dz_ref, stat_ref, step):
    rows = parts[0].shape[0]
    lane = lanes_of(rows)
    x = layer_in(parts, coef)
    rx = aux[:, 33:34]
    nx = (x - aux[:, 32:33]) * rx
    dx = rx * (du - mean_of(du) - nx * mean_of(du * nx))
    for i in range(STREAMS):
        red = put(red, lane, 8 * i, jnp.sum(parts[i] * dx, axis=1, keepdims=True))
    used = (lane < 8 * STREAMS) & (lane % 8 < 6)
    slope = jnp.tanh(aux)
    dz = jnp.where(used, red * (1.0 - slope * slope), 0.0)
    stat_ref[0:1, :] += jnp.sum(red, axis=0, keepdims=True)
    dz_ref[pl.ds(step * rows, rows), :] = dz
    both = dz * aux
    packed = []
    for i in range(STREAMS):
        own = dz if i == 0 else pltpu.roll(dz, LANES - 8 * i, 1)
        own = jnp.where(lane < 6, own, 0.0)
        top = own.astype(BF16).astype(F32)
        packed.append((top + pltpu.roll(top, 32, 1) + pltpu.roll(own - top, 96, 1)).astype(BF16))
    dn_all = lax.dot_general(
        jnp.concatenate(packed, axis=0), wpack, (((1,), (0,)), ((), ())), preferred_element_type=F32
    )
    outs = []
    total_rows = dz_ref.shape[0]
    for i in range(STREAMS):
        mean, rstd = aux[:, 8 * i + 6 : 8 * i + 7], aux[:, 8 * i + 7 : 8 * i + 8]
        normed = (parts[i] - mean) * rstd
        normed_ref[pl.ds(i * total_rows + step * rows, rows), :] = normed.astype(BF16)
        dn = dn_all[i * rows : (i + 1) * rows]
        own = (lane >= 8 * i) & (lane < 8 * i + 6)
        along = jnp.sum(jnp.where(own, both, 0.0), axis=1, keepdims=True) * (1.0 / D)
        total = coef[:, 8 * i : 8 * i + 1] * dx + rstd * (dn - mean_of(dn) - normed * along)
        for j in range(STREAMS):
            total = total + coef[:, 8 * i + 1 + j : 8 * i + 2 + j] * grads[j]
        outs.append(total)
    return outs


def finish_hc(normed_ref, dz_ref, stat_ref, hc_ref):
    across = dz_ref[...].T
    left = jnp.concatenate([across[8 * i : 8 * i + 8] for i in range(STREAMS)], axis=1)
    top = left.astype(BF16)
    low = (left - top.astype(F32)).astype(BF16)
    both = lax.dot_general(
        jnp.concatenate([top, low], axis=0),
        normed_ref[...],
        (((1,), (0,)), ((), ())),
        preferred_element_type=F32,
    )
    hc_ref[0:8, :] = both[0:8] + both[8:16]
    hc_ref[8:16, :] = jnp.zeros((8, D), F32)
    hc_ref[8:9, 0:LANES] = stat_ref[0:1, :]


def first_kernel(s_ref, w_ref, static_ref, u_ref, aux_ref):
    aux, _, u = enter(stream_parts(s_ref), w_ref[...], static_ref[0:1, :])
    u_ref[...] = u.astype(BF16)
    aux_ref[...] = aux


def middle_kernel(s_ref, c_ref, y_ref, aux0_ref, w_ref, static_ref, u_ref, dy_ref, aux_ref):
    coef0 = static_ref[0:1, :] + jnp.tanh(aux0_ref[...])
    mid = mixed(stream_parts(s_ref), coef0, y_ref[...])
    aux, coef, u = enter(mid, w_ref[...], static_ref[1:2, :])
    u_ref[...] = u.astype(BF16)
    aux_ref[...] = aux
    dy_ref[...] = branch_grad(stream_parts(c_ref), coef).astype(BF16)


def out_kernel(
    s_ref, c_ref, y_ref, y2_ref, aux0_ref, aux1_ref, static_ref, out_ref, red_ref
):
    coef0 = static_ref[0:1, :] + jnp.tanh(aux0_ref[...])
    coef1 = static_ref[1:2, :] + jnp.tanh(aux1_ref[...])
    mid = mixed(stream_parts(s_ref), coef0, y_ref[...])
    y2 = y2_ref[...]
    for j, total in enumerate(mixed(mid, coef1, y2)):
        out_ref[:, j * D : (j + 1) * D] = total.astype(BF16)
    red_ref[...] = leave_grads(mid, stream_parts(c_ref), y2)


def back_kernel(
    s_ref, c_ref, y_ref, du_ref, red_ref, aux0_ref, aux1_ref, w_ref, static_ref,
    dmid_ref, dy_ref, hc_ref, normed_ref, dz_ref, stat_ref,
):
    step = pl.program_id(0)

    @pl.when(step == 0)
    def _():
        stat_ref[...] = jnp.zeros_like(stat_ref)

    coef0 = static_ref[0:1, :] + jnp.tanh(aux0_ref[...])
    aux1 = aux1_ref[...]
    coef1 = static_ref[1:2, :] + jnp.tanh(aux1)
    mid = mixed(stream_parts(s_ref), coef0, y_ref[...])
    dmid = enter_back(
        mid, stream_parts(c_ref), aux1, coef1, red_ref[...], du_ref[...], w_ref[...],
        normed_ref, dz_ref, stat_ref, step,
    )
    for j in range(STREAMS):
        dmid_ref[:, j * D : (j + 1) * D] = dmid[j]
    dy_ref[...] = branch_grad(dmid, coef0).astype(BF16)

    @pl.when(step == pl.num_programs(0) - 1)
    def _():
        finish_hc(normed_ref, dz_ref, stat_ref, hc_ref)


def last_kernel(
    s_ref, dmid_ref, y_ref, du_ref, aux0_ref, w_ref, static_ref,
    ds_ref, hc_ref, normed_ref, dz_ref, stat_ref,
):
    step = pl.program_id(0)

    @pl.when(step == 0)
    def _():
        stat_ref[...] = jnp.zeros_like(stat_ref)

    aux0 = aux0_ref[...]
    coef0 = static_ref[0:1, :] + jnp.tanh(aux0)
    parts, grads = stream_parts(s_ref), stream_parts(dmid_ref)
    red = leave_grads(parts, grads, y_ref[...])
    ds = enter_back(
        parts, grads, aux0, coef0, red, du_ref[...], w_ref[...],
        normed_ref, dz_ref, stat_ref, step,
    )
    for j in range(STREAMS):
        ds_ref[:, j * D : (j + 1) * D] = ds[j].astype(BF16)

    @pl.when(step == pl.num_programs(0) - 1)
    def _():
        finish_hc(normed_ref, dz_ref, stat_ref, hc_ref)


def row_call(kernel, rows, ins, outs, hc=False):
    tile = HC_ROWS

    def cut(columns):
        return pl.BlockSpec((tile, columns), lambda i: (i, 0))

    def whole(shape):
        return pl.BlockSpec(shape, lambda i: (0, 0))

    in_specs = [cut(a.shape[1]) if by_rows else whole(a.shape) for a, by_rows in ins]
    out_specs = [cut(columns) for columns, _ in outs]
    out_shape = [jax.ShapeDtypeStruct((rows, columns), dtype) for columns, dtype in outs]
    scratch = []
    if hc:
        out_specs.append(whole((16, D)))
        out_shape.append(jax.ShapeDtypeStruct((16, D), F32))
        scratch = [
            pltpu.VMEM((STREAMS * rows, D), BF16),
            pltpu.VMEM((rows, LANES), F32),
            pltpu.VMEM((8, LANES), F32),
        ]
    return pl.pallas_call(
        kernel,
        grid=(rows // tile,),
        in_specs=in_specs,
        out_specs=out_specs,
        out_shape=out_shape,
        scratch_shapes=scratch,
        compiler_params=pltpu.CompilerParams(vmem_limit_bytes=40 * MIB),
    )(*[a for a, _ in ins])


def pack_weight(weight):
    across = jnp.pad(weight.T, ((0, 26), (0, 0)))
    top = lax.reduce_precision(across, 8, 7)
    mid = lax.reduce_precision(across - top, 8, 7)
    return jnp.concatenate([top, mid, across - top - mid, top], axis=0).astype(BF16)


Q_ROWS = 256


def turn(v, cosine, sine):
    return v * cosine + pltpu.roll(v, HEAD_DIM // 2, 1) * sine


def attend_kernel(
    q_ref, k_ref, v_ref, cos_ref, sin_ref, qpos_ref, qstart_ref, kpos_ref,
    o_ref, lse_ref, qr_ref, kr_ref, vb_ref,
):
    at = pl.program_id(1)

    @pl.when(at == 0)
    def _():
        kr_ref[...] = turn(k_ref[...], cos_ref[...], sin_ref[...]).astype(BF16)
        vb_ref[...] = v_ref[...].astype(BF16)

    here = pl.ds(at * Q_ROWS, Q_ROWS)
    query = turn(q_ref[...], cos_ref[here, :], sin_ref[here, :]).astype(BF16)
    qr_ref[...] = query
    scores = (
        lax.dot_general(query, kr_ref[...], (((1,), (1,)), ((), ())), preferred_element_type=F32)
        * SCALE
    )
    kpos = kpos_ref[0:1, :]
    keep = (kpos <= qpos_ref[...]) & (kpos >= qstart_ref[...])
    scores = jnp.where(keep, scores, -1e30)
    top = jnp.max(scores, axis=1, keepdims=True)
    grown = jnp.exp(scores - top)
    total = jnp.sum(grown, axis=1, keepdims=True)
    out = jnp.dot((grown / total).astype(BF16), vb_ref[...], preferred_element_type=F32)
    o_ref[...] = out.astype(BF16)
    lse_ref[...] = jnp.broadcast_to(top + jnp.log(total), lse_ref.shape)


def attend_back_kernel(
    q_ref, k_ref, v_ref, do_ref, lse_ref, cos_ref, sin_ref, qpos_ref, qstart_ref, kpos_ref,
    dq_ref, dk_ref, dv_ref, dk_sum, dv_sum,
):
    at = pl.program_id(1)

    @pl.when(at == 0)
    def _():
        dk_sum[...] = jnp.zeros_like(dk_sum)
        dv_sum[...] = jnp.zeros_like(dv_sum)

    here = pl.ds(at * Q_ROWS, Q_ROWS)
    query, keys, d_out = q_ref[...], k_ref[...], do_ref[...]
    nt = (((1,), (1,)), ((), ()))
    tn = (((0,), (0,)), ((), ()))
    scores = lax.dot_general(query, keys, nt, preferred_element_type=F32) * SCALE
    kpos = kpos_ref[0:1, :]
    keep = (kpos <= qpos_ref[...]) & (kpos >= qstart_ref[...])
    probs = jnp.where(keep, jnp.exp(scores - lse_ref[:, 0:1]), 0.0)
    d_probs = lax.dot_general(d_out, v_ref[...], nt, preferred_element_type=F32)
    delta = jnp.sum(probs * d_probs, axis=1, keepdims=True)
    ds = (probs * (d_probs - delta)).astype(BF16)
    dq = jnp.dot(ds, keys, preferred_element_type=F32) * SCALE
    dq_ref[...] = turn(dq, cos_ref[here, :], -sin_ref[here, :]).astype(BF16)
    dk_sum[...] += lax.dot_general(ds, query, tn, preferred_element_type=F32)
    dv_sum[...] += lax.dot_general(probs.astype(BF16), d_out, tn, preferred_element_type=F32)

    @pl.when(at == pl.num_programs(1) - 1)
    def _():
        dk_ref[...] = turn(dk_sum[...] * SCALE, cos_ref[...], -sin_ref[...]).astype(BF16)
        dv_ref[...] = dv_sum[...].astype(BF16)


def attention_specs(total):
    by_query = pl.BlockSpec((Q_ROWS, HEAD_DIM), lambda h, i: (i, h))
    by_head = pl.BlockSpec((total, HEAD_DIM), lambda h, i: (0, h))
    table = pl.BlockSpec((total, HEAD_DIM), lambda h, i: (0, 0))
    row = pl.BlockSpec((Q_ROWS, 1), lambda h, i: (i, 0))
    keys = pl.BlockSpec((8, total), lambda h, i: (0, 0))
    return (by_query, by_head, [table, table, row, row, keys])


def attend(qkv, heads, marks):
    total = qkv.shape[0]
    by_query, by_head, shared = attention_specs(total)

    def of(kind):
        return pl.BlockSpec((total, HEAD_DIM), lambda h, i: (0, kind * heads + h))

    low = jax.ShapeDtypeStruct((total, heads * HEAD_DIM), BF16)
    wide = jax.ShapeDtypeStruct((total, heads * HEAD_DIM), F32)
    return pl.pallas_call(
        attend_kernel,
        grid=(heads, total // Q_ROWS),
        in_specs=[by_query, of(1), of(2)] + shared,
        out_specs=[by_query, by_query, by_query, by_head, by_head],
        out_shape=[low, wide, low, low, low],
        compiler_params=pltpu.CompilerParams(vmem_limit_bytes=40 * MIB),
    )(qkv, qkv, qkv, *marks)


def attend_back(query, keys, values, d_out, lse, heads, marks):
    total = query.shape[0]
    by_query, by_head, shared = attention_specs(total)
    low = jax.ShapeDtypeStruct((total, heads * HEAD_DIM), BF16)
    return pl.pallas_call(
        attend_back_kernel,
        grid=(heads, total // Q_ROWS),
        in_specs=[by_query, by_head, by_head, by_query, by_query] + shared,
        out_specs=[by_query, by_head, by_head],
        out_shape=[low, low, low],
        scratch_shapes=[pltpu.VMEM((total, HEAD_DIM), F32)] * 2,
        compiler_params=pltpu.CompilerParams(vmem_limit_bytes=40 * MIB),
    )(query, keys, values, d_out, lse, *marks)


def angles(inside):
    half = HEAD_DIM // 2
    freq = 10000.0 ** (-jnp.arange(half, dtype=F32) / half)
    angle = inside.astype(F32)[:, None] * freq[None, :]
    cosine, sine = jnp.cos(angle), jnp.sin(angle)
    return (jnp.concatenate([cosine, cosine], axis=1), jnp.concatenate([-sine, sine], axis=1))


class HeadAttention:
    def __init__(self, rows, w_qkv, w_out, pair_row, length_row):
        n = lax.axis_size("ctx")
        self.place = lax.axis_index("ctx")
        self.rows, self.heads = rows, HEADS // n
        self.owners = ring_owners(n, self.place)
        position, _, start = places(pair_row, length_row, rows, self.owners)
        cosine, sine = angles(position - start)
        kpos = jnp.broadcast_to(position[None, :], (8, position.shape[0]))
        self.marks = (cosine, sine, position[:, None], start[:, None], kpos)
        self.qkv_cols = to_columns(w_qkv, 3)
        self.out_all = lax.all_gather(w_out, ("ctx", "fsdp"), axis=0, tiled=True)

    def to_tokens(self, heads_out):
        n = lax.axis_size("ctx")
        order, offsets = ring_order(n), ring_offsets(n)
        width = heads_out.shape[1]
        mine = jnp.zeros((self.rows, n * width), heads_out.dtype)
        for at, offset in enumerate(offsets):
            got = heads_out[at * self.rows : (at + 1) * self.rows]
            back = -offset if offset != -(n // 2) else offset
            if offset:
                pairs = [(order[i], order[(i + offset) % n]) for i in range(n)]
                got = lax.ppermute(got, "ctx", pairs)
            source = self.owners[offsets.index(back)]
            mine = lax.dynamic_update_slice_in_dim(mine, got, source * width, 1)
        return mine

    def forward(self, u):
        self.u_all = ring_gather(spread_columns(u))
        qkv = jnp.dot(self.u_all, self.qkv_cols, preferred_element_type=F32)
        self.o, self.lse, self.q, self.k, self.v = attend(qkv, self.heads, self.marks)
        return jnp.dot(self.to_tokens(self.o), self.out_all, preferred_element_type=F32)

    def backward(self, dy):
        dy_all = ring_gather(dy)
        width = self.heads * HEAD_DIM
        out_rows = lax.dynamic_slice_in_dim(self.out_all, self.place * width, width, 0)
        d_out = jnp.einsum("td,ed->te", dy_all, out_rows, preferred_element_type=F32).astype(BF16)
        grad_out = jnp.einsum("te,td->ed", self.o, dy_all, preferred_element_type=F32)
        dq, dk, dv = attend_back(self.q, self.k, self.v, d_out, self.lse, self.heads, self.marks)
        d_qkv = jnp.concatenate([dq, dk, dv], axis=1)
        partial = jnp.einsum(
            "tc,dc->td", d_qkv, self.qkv_cols, preferred_element_type=F32
        ).astype(BF16)
        grad_qkv = jnp.einsum("td,tc->dc", self.u_all, d_qkv, preferred_element_type=F32)
        du = unspread_columns(ring_scatter(partial, self.rows))
        return (du, to_rows(grad_qkv, 3), share_rows(grad_out))


def rotate(v, inside, sign):
    half = v.shape[-1] // 2
    freq = 10000.0 ** (-jnp.arange(half, dtype=F32) / half)
    angle = inside.astype(F32)[:, None] * freq[None, :]
    cosine = jnp.cos(angle)[:, None, :]
    sine = sign * jnp.sin(angle)[:, None, :]
    first, second = (v[..., :half], v[..., half:])
    return jnp.concatenate(
        [first * cosine - second * sine, second * cosine + first * sine], axis=-1
    )


class TokenAttention:
    def __init__(self, rows, w_qkv, w_out, pair_row, length_row):
        n = lax.axis_size("ctx")
        place = lax.axis_index("ctx")
        self.rows = rows
        owners = jnp.arange(n, dtype=jnp.int32)
        kpos, kdoc, kstart = places(pair_row, length_row, rows, owners)

        def own(v):
            return lax.dynamic_slice_in_dim(v, place * rows, rows)

        self.inside = own(kpos - kstart)
        self.keep = (kpos[None, :] <= own(kpos)[:, None]) & (kdoc[None, :] == own(kdoc)[:, None])
        self.w_qkv, self.w_out = w_qkv, w_out

    def gathered(self, weight):
        return lax.all_gather(weight, ("ctx", "fsdp"), axis=0, tiled=True)

    def scores(self):
        scores = jnp.einsum("qhe,hke->hqk", self.q, self.k, preferred_element_type=F32) * SCALE
        return jnp.where(self.keep[None], scores, -1e30)

    def forward(self, u):
        rows, shape = self.rows, (self.rows, HEADS, HEAD_DIM)
        self.u = u
        qkv = jnp.dot(u, self.gathered(self.w_qkv), preferred_element_type=F32)
        self.q = rotate(qkv[:, :D].reshape(shape), self.inside, 1.0).astype(BF16)
        key = rotate(qkv[:, D : 2 * D].reshape(shape), self.inside, 1.0).astype(BF16)
        value = qkv[:, 2 * D :].reshape(shape).astype(BF16)
        self.k = lax.all_gather(key.transpose(1, 0, 2), "ctx", axis=1, tiled=True)
        self.v = lax.all_gather(value.transpose(1, 0, 2), "ctx", axis=1, tiled=True)
        scores = self.scores()
        top = jnp.max(scores, axis=-1, keepdims=True)
        self.lse = top + jnp.log(jnp.sum(jnp.exp(scores - top), axis=-1, keepdims=True))
        probs = jnp.exp(scores - self.lse).astype(BF16)
        attended = jnp.einsum("hqk,hke->qhe", probs, self.v, preferred_element_type=F32)
        self.o = attended.reshape(rows, D).astype(BF16)
        return jnp.dot(self.o, self.gathered(self.w_out), preferred_element_type=F32)

    def backward(self, dy):
        rows = self.rows
        d_out = jnp.einsum(
            "td,ed->te", dy, self.gathered(self.w_out), preferred_element_type=F32
        )
        d_out = d_out.astype(BF16).reshape(rows, HEADS, HEAD_DIM)
        grad_out = jnp.einsum("te,td->ed", self.o, dy, preferred_element_type=F32)
        again = jnp.exp(self.scores() - self.lse)
        d_probs = jnp.einsum("qhe,hke->hqk", d_out, self.v, preferred_element_type=F32)
        delta = jnp.sum(again * d_probs, axis=-1, keepdims=True)
        ds = (again * (d_probs - delta)).astype(BF16)
        dq = jnp.einsum("hqk,hke->qhe", ds, self.k, preferred_element_type=F32) * SCALE
        dk_all = jnp.einsum("hqk,qhe->hke", ds, self.q, preferred_element_type=F32) * SCALE
        dv_all = jnp.einsum(
            "hqk,qhe->hke", again.astype(BF16), d_out, preferred_element_type=F32
        )

        def shared(v):
            mine = lax.psum_scatter(v.astype(BF16), "ctx", scatter_dimension=1, tiled=True)
            return mine.astype(F32).transpose(1, 0, 2)

        dk, dv = shared(dk_all), shared(dv_all)
        d_qkv = jnp.concatenate(
            [
                rotate(dq, self.inside, -1.0).reshape(rows, D),
                rotate(dk, self.inside, -1.0).reshape(rows, D),
                dv.reshape(rows, D),
            ],
            axis=1,
        ).astype(BF16)
        du = jnp.einsum("tc,dc->td", d_qkv, self.gathered(self.w_qkv), preferred_element_type=F32)
        grad_qkv = jnp.einsum("td,tc->dc", self.u, d_qkv, preferred_element_type=F32)
        return (
            du,
            weight_share(grad_qkv, self.w_qkv.shape[0]),
            weight_share(grad_out, self.w_out.shape[0]),
        )


def on_device(
    streams,
    cotangent,
    w_qkv,
    w_out,
    w_gate_up,
    w_down,
    hc_weight,
    hc_static,
    seq_lengths,
    pair_perm,
):
    n = lax.axis_size("ctx")
    group = lax.axis_index("fsdp")
    rows = streams.shape[1]
    pair_row = lax.dynamic_index_in_dim(pair_perm, group, 0, keepdims=False)
    length_row = lax.dynamic_index_in_dim(seq_lengths, group, 0, keepdims=False)
    state, cot = streams[0], cotangent[0]
    wpack0, wpack1 = pack_weight(hc_weight[0]), pack_weight(hc_weight[1])
    static = jnp.pad(hc_static, ((0, 0), (0, 0), (0, 2))).reshape(2, 8 * STREAMS)
    static = jnp.pad(static, ((0, 6), (0, LANES - 8 * STREAMS)))

    plan = HeadAttention if HEADS % n == 0 else TokenAttention
    attention = plan(rows, w_qkv, w_out, pair_row, length_row)
    u, aux0 = row_call(
        first_kernel,
        rows,
        [(state, True), (wpack0, False), (static, False)],
        [(D, BF16), (LANES, F32)],
    )
    gate_up_cols = to_columns(w_gate_up, 2)
    down_rows = lax.all_gather(w_down, "fsdp", axis=0, tiled=True)
    y = attention.forward(u)
    u2, dy2, aux1 = row_call(
        middle_kernel,
        rows,
        [(state, True), (cot, True), (y, True), (aux0, True), (wpack1, False), (static, False)],
        [(D, BF16), (D, BF16), (LANES, F32)],
    )
    u2_all = ring_gather(spread_columns(u2))
    dy2_all = ring_gather(dy2)
    width = FF // n
    gate_up = jnp.dot(u2_all, gate_up_cols, preferred_element_type=F32)
    gate, up = gate_up[:, :width], gate_up[:, width:]
    hidden = (jax.nn.silu(gate) * up).astype(BF16)
    y2_partial = jnp.dot(hidden, down_rows, preferred_element_type=F32).astype(BF16)
    y2 = ring_scatter(y2_partial, rows)
    d_hidden = jnp.einsum("td,fd->tf", dy2_all, down_rows, preferred_element_type=F32)
    d_hidden = lax.reduce_precision(d_hidden, 8, 7)
    grad_down = share_rows(
        jnp.einsum("tf,td->fd", hidden, dy2_all, preferred_element_type=F32)
    )
    open_gate = jax.nn.sigmoid(gate)
    d_up = d_hidden * gate * open_gate
    d_gate = d_hidden * up * open_gate * (1.0 + gate * (1.0 - open_gate))
    dgu = jnp.concatenate([d_gate, d_up], axis=1).astype(BF16)
    du2_partial = jnp.einsum("tg,dg->td", dgu, gate_up_cols, preferred_element_type=F32)
    du2 = unspread_columns(ring_scatter(du2_partial.astype(BF16), rows))
    grad_gate_up = to_rows(
        jnp.einsum("td,tg->dg", u2_all, dgu, preferred_element_type=F32), 2
    )
    out, red1 = row_call(
        out_kernel,
        rows,
        [
            (state, True), (cot, True), (y, True), (y2, True), (aux0, True), (aux1, True),
            (static, False),
        ],
        [(STREAMS * D, BF16), (LANES, F32)],
    )
    dmid, dy, hc1 = row_call(
        back_kernel,
        rows,
        [
            (state, True), (cot, True), (y, True), (du2, True), (red1, True), (aux0, True),
            (aux1, True), (wpack1, False), (static, False),
        ],
        [(STREAMS * D, F32), (D, BF16)],
        hc=True,
    )
    du, grad_qkv, grad_out = attention.backward(dy)
    grad_state, hc0 = row_call(
        last_kernel,
        rows,
        [
            (state, True), (dmid, True), (y, True), (du, True), (aux0, True), (wpack0, False),
            (static, False),
        ],
        [(STREAMS * D, BF16)],
        hc=True,
    )
    hc = jnp.stack([sum_all(hc0), sum_all(hc1)])
    grad_hc_weight = hc[:, 0:6].transpose(0, 2, 1)
    grad_hc_static = hc[:, 8, : 8 * STREAMS].reshape(2, STREAMS, 8)[:, :, 0:6]
    return (
        out[None],
        grad_state[None],
        grad_qkv,
        grad_out,
        grad_gate_up,
        grad_down,
        grad_hc_weight,
        grad_hc_static,
    )


def solution(mesh):
    return jax.shard_map(
        on_device,
        mesh=mesh,
        in_specs=(
            P("fsdp", "ctx", None),
            P("fsdp", "ctx", None),
            P(("ctx", "fsdp"), None),
            P(("ctx", "fsdp"), None),
            P(("ctx", "fsdp"), None),
            P(("ctx", "fsdp"), None),
            P(),
            P(),
            P(),
            P(),
        ),
        out_specs=(
            P("fsdp", "ctx", None),
            P("fsdp", "ctx", None),
            P(("ctx", "fsdp"), None),
            P(("ctx", "fsdp"), None),
            P(("ctx", "fsdp"), None),
            P(("ctx", "fsdp"), None),
            P(),
            P(),
        ),
        check_vma=False,
    )
```

time: 3880 us -> 802 us (0.21)
  the two profiles are of different devices: /device:TPU:0 before, /device:TPU:11 now
where the time goes in v1:
time: 802 us; the launch traced here: 794 us
  waiting for transfers between devices  376 us (47%)
  starting transfers between devices  130 us (16%)
  matrix products  100 us (12%)
  local copies, waits for them, and re-layouts  81 us (10%)
  Pallas kernels  58.5 us (7%)
  other arithmetic  26.6 us (3%)
  between operations  21.6 us (3%)
    ppermute x12, waiting for transfers between devices, ring_gather(): other = lax.ppermute(other, 'ctx', back)  76.4 us
    ppermute x14, waiting for transfers between devices, to_columns(): got = lax.ppermute(got, 'ctx', [(i, (i + k) % n) for i in range(n)])  57 us
    ppermute x14, waiting for transfers between devices, to_rows(): got = lax.ppermute(got, 'ctx', [(i, (i + k) % n) for i in range(n)])  56 us
    ppermute x12, waiting for transfers between devices, ring_gather(): one = lax.ppermute(one, 'ctx', ahead)  45.1 us
    pallas_call x5, Pallas kernels, row_call(): pl.pallas_call(kernel, grid=(rows // tile,), in_specs=in_specs, out_specs...  38.2 us
    ppermute x9, waiting for transfers between devices, ring_scatter(): one = add(lax.ppermute(one, 'ctx', ahead), k, *span_one)  32.9 us
    ppermute x9, waiting for transfers between devices, ring_scatter(): other = add(lax.ppermute(other, 'ctx', back), -k, *span_other)  31.4 us
    ppermute x10, starting transfers between devices, sum_all(): v = v + lax.ppermute(v, axis, [(i, i ^ step) for i in range(n)])  29.6 us
  transfers between devices with their start and end apart: 109, of which 69 were waited for; matrix products, arithmetic and copies ran while one was open for 19% of the time, Pallas kernels for 5%

profile of v1, /device:TPU:11, one launch (start us, length us, event | category | flops | bytes accessed | tf_op | source)
XLA Modules:
  0.0 793.6 jit_solution(2170712854279055035)
XLA Ops:
  17.6 10.9 %collective-permute-done.8 = bf16[64,768]{1,0:T(8,128)(2,1)} collective-permute-done((bf16[64,768]{1,0:T(8,128)(2,1)}, bf16[64,768]{1,0:T(8,128)(2,1)}, u32[]{:S(2)}, u32[]{:S(2)}) %collective-permute-start.8) | collective-permute-done | bytes 98336 | tf_op jit(solution)/shard_map/ppermute | solution.py:136
  32.3 4.0 collective-permute-done.14
  50.4 26.2 %collective-permute-done.32 = bf16[64,2048]{1,0:T(8,128)(2,1)S(1)} collective-permute-done((bf16[64,2048]{1,0:T(8,128)(2,1)S(1)}, bf16[64,2048]{1,0:T(8,128)(2,1)S(1)}, u32[]{:S(2)}, u32[]{:S(2)}) %collective-permute-start.32) | collective-permute-done | bytes 262176 | tf_op jit(solution)/shard_map/ppermute | solution.py:136
  77.3 7.0 collective-permute-done.33
  85.7 6.2 collective-permute-done.35
  94.7 5.3 shard_map.179
  104.7 17.3 %collective-permute-done.1 = bf16[128,2048]{0,1:T(8,128)(2,1)S(1)} collective-permute-done((bf16[128,2048]{0,1:T(8,128)(2,1)S(1)}, bf16[128,2048]{0,1:T(8,128)(2,1)S(1)}, u32[]{:S(2)}, u32[]{:S(2)}) %collective-permute-start.1) | collective-permute-done | bytes 524320 | tf_op jit(solution)/shard_map/ppermute | solution.py:81
  124.2 20.4 %collective-permute-done.3 = bf16[128,2048]{0,1:T(8,128)(2,1)} collective-permute-done((bf16[128,2048]{0,1:T(8,128)(2,1)S(1)}, bf16[128,2048]{0,1:T(8,128)(2,1)}, u32[]{:S(2)}, u32[]{:S(2)}) %collective-permute-start.3) | collective-permute-done | bytes 524320 | tf_op jit(solution)/shard_map/ppermute | solution.py:81
  144.6 3.4 collective-permute-start.5
  152.7 14.9 %collective-permute-done.5 = bf16[128,2048]{0,1:T(8,128)(2,1)S(1)} collective-permute-done((bf16[128,2048]{0,1:T(8,128)(2,1)}, bf16[128,2048]{0,1:T(8,128)(2,1)S(1)}, u32[]{:S(2)}, u32[]{:S(2)}) %collective-permute-start.5) | collective-permute-done | bytes 524320 | tf_op jit(solution)/shard_map/ppermute | solution.py:81
  177.1 4.5 collective-permute-done.7
  183.8 7.5 concatenate.104
  191.3 6.3 fusion.23.q_ref.k_ref.v_ref
  197.7 8.8 %shard_map.180 = (bf16[1024,256]{1,0:T(8,128)(2,1)S(1)}, f32[1024,256]{1,0:T(8,128)S(1)}, bf16[1024,256]{1,0:T(8,128)(2,1)S(1)}, bf16[1024,256]{1,0:T(8,128)(2,1)S(1)}, bf16[1024,256]{1,0:T(8,128)(2,1)S(1)}) custom-call(f32[1024,768]{1,0:T(8,128)S(1)} %fusion.23.q_ref.k_ref.v_ref, f32[1024,768]{1,0:T(8,128)S(1)} %fusion.23.q_ref.k_ref.v_ref, ...), custom_call_target="tpu_custom_call" | custom-call | tf_op jit(solution)/shard_map/pallas_call | solution.py:553
  229.3 5.0 fusion.24.y_ref
  234.4 7.7 shard_map.181
  249.6 5.2 collective-permute-done.45
  256.3 8.1 %collective-permute-done.23 = bf16[128,2048]{0,1:T(8,128)(2,1)S(1)} collective-permute-done((bf16[128,2048]{0,1:T(8,128)(2,1)S(1)}, bf16[128,2048]{0,1:T(8,128)(2,1)S(1)}, u32[]{:S(2)}, u32[]{:S(2)}) %collective-permute-start.23) | collective-permute-done | bytes 524320 | tf_op jit(solution)/shard_map/ppermute | solution.py:81
  266.1 3.8 collective-permute-start.24
  272.0 5.2 collective-permute-done.47
  278.7 8.1 %collective-permute-done.25 = bf16[128,2048]{0,1:T(8,128)(2,1)S(1)} collective-permute-done((bf16[128,2048]{0,1:T(8,128)(2,1)S(1)}, bf16[128,2048]{0,1:T(8,128)(2,1)S(1)}, u32[]{:S(2)}, u32[]{:S(2)}) %collective-permute-start.25) | collective-permute-done | bytes 524320 | tf_op jit(solution)/shard_map/ppermute | solution.py:81
  288.4 3.9 collective-permute-start.26
  293.5 6.1 collective-permute-done.49
  302.6 6.7 collective-permute-done.27
  311.1 4.5 collective-permute-start.28
  315.8 11.9 %collective-permute-done.29 = bf16[64,2048]{0,1:T(8,128)(2,1)S(1)} collective-permute-done((bf16[64,2048]{0,1:T(8,128)(2,1)S(1)}, bf16[64,2048]{0,1:T(8,128)(2,1)S(1)}, u32[]{:S(2)}, u32[]{:S(2)}) %collective-permute-start.29) | collective-permute-done | bytes 262176 | tf_op jit(solution)/shard_map/ppermute | solution.py:78
  328.5 7.3 concatenate.116
  339.1 14.7 %fusion.25 = f32[1024,2048]{1,0:T(8,128)} fusion(bf16[1024,2048]{0,1:T(8,128)(2,1)} %concatenate.116, bf16[2048,2048]{1,0:T(8,128)(2,1)} %all-gather.9.cloned.1.call-done), kind=kOutput, calls=%fused_computation.260 | convolution fusion | flops 8589934592 | bytes 20971520 | tf_op jit(solution)/shard_map/dot_general | solution.py:768
  353.8 13.3 %multiply_convert_fusion.1 = (bf16[1024,1024]{1,0:T(8,128)(2,1)S(1)}, bf16[1024,1024]{1,0:T(8,128)(2,1)S(1)}, bf16[1024,1024]{1,0:T(8,128)(2,1)}) fusion(f32[1024,2048]{1,0:T(8,128)} %fusion.25, bf16[1024,2048]{1,0:T(8,128)(2,1)} %constant_dynamic-update-slice_fusion, bf16[1024,2048]{1,0:T(8,128)(2,1)} %all-gather.11.cloned.1.call-done), kind=kOutput, calls=%fused_computation.3 | convolution fusion | flops 4312793088 | bytes 23068672 | tf_op jit(solution)/shard_map/td,fd->tf/dot_general | solution.py:773
  367.1 12.8 %convolution_convert_fusion.1 = bf16[1024,2048]{1,0:T(8,128)(2,1)S(1)} fusion(bf16[2048,2048]{1,0:T(8,128)(2,1)} %all-gather.9.cloned.1.call-done, bf16[1024,1024]{1,0:T(8,128)(2,1)S(1)} %get-tuple-element.73, bf16[1024,1024]{1,0:T(8,128)(2,1)S(1)} %get-tuple-element.72), kind=kOutput, calls=%fused_computation.6 | convolution fusion | flops 8600420352 | bytes 16777216 | tf_op jit(solution)/shard_map/tg,dg->td/dot_general | solution.py:782
  380.0 4.0 collective-permute-start.53
  384.0 7.3 convolution_convert_fusion.4
  400.7 8.1 %collective-permute-done.58 = bf16[128,2048]{1,0:T(8,128)(2,1)S(1)} collective-permute-done((bf16[128,2048]{1,0:T(8,128)(2,1)S(1)}, bf16[128,2048]{1,0:T(8,128)(2,1)S(1)}, u32[]{:S(2)}, u32[]{:S(2)}) %collective-permute-start.58) | collective-permute-done | bytes 524320 | tf_op jit(solution)/shard_map/ppermute | solution.py:107
  410.7 9.3 %collective-permute-done.42 = bf16[128,2048]{1,0:T(8,128)(2,1)S(1)} collective-permute-done((bf16[128,2048]{1,0:T(8,128)(2,1)S(1)}, bf16[128,2048]{1,0:T(8,128)(2,1)S(1)}, u32[]{:S(2)}, u32[]{:S(2)}) %collective-permute-start.42) | collective-permute-done | bytes 524320 | tf_op jit(solution)/shard_map/ppermute | solution.py:107
  421.9 7.5 collective-permute-done.55
  433.2 7.5 collective-permute-done.39
  445.4 6.5 collective-permute-done.56
  468.2 6.4 shard_map.182
  474.7 9.0 %shard_map.183 = (f32[128,8192]{1,0:T(8,128)S(1)}, bf16[128,2048]{1,0:T(8,128)(2,1)S(1)}, f32[16,2048]{1,0:T(8,128)S(1)}) custom-call(bf16[128,8192]{1,0:T(8,128)(2,1)S(1)} %bitcast.121, bf16[128,8192]{1,0:T(8,128)(2,1)S(1)} %bitcast.125, f32[128,2048]{1,0:T(8,128)S(1)} %fusion.24.y_ref, f32[128,2048]{1,0:T(8,128)S(1)} %copy-done.19, ...), custom_call_target="tpu_custom_call" | custom-call | tf_op jit(solution)/shard_map/pallas_call | solution.py:448
  485.2 6.5 collective-permute-done.61
  493.6 10.5 %collective-permute-done.63 = bf16[128,2048]{1,0:T(8,128)(2,1)S(1)} collective-permute-done((bf16[128,2048]{1,0:T(8,128)(2,1)S(1)}, bf16[128,2048]{1,0:T(8,128)(2,1)S(1)}, u32[]{:S(2)}, u32[]{:S(2)}) %collective-permute-start.63) | collective-permute-done | bytes 524320 | tf_op jit(solution)/shard_map/ppermute | solution.py:80
  506.0 11.3 %collective-permute-done.65 = bf16[128,2048]{1,0:T(8,128)(2,1)S(1)} collective-permute-done((bf16[128,2048]{1,0:T(8,128)(2,1)S(1)}, bf16[128,2048]{1,0:T(8,128)(2,1)S(1)}, u32[]{:S(2)}, u32[]{:S(2)}) %collective-permute-start.65) | collective-permute-done | bytes 524320 | tf_op jit(solution)/shard_map/ppermute | solution.py:80
  519.1 6.6 collective-permute-done.67
  530.9 9.4 %convolution_convert_fusion.3 = bf16[1024,2048]{1,0:T(8,128)(2,1)} fusion(bf16[1024,1024]{1,0:T(8,128)(2,1)} %get-tuple-element.74, bf16[1024,2048]{1,0:T(8,128)(2,1)} %constant_dynamic-update-slice_fusion), kind=kOutput, calls=%fused_computation.8 | convolution fusion | flops 4297064448 | bytes 10485760 | tf_op jit(solution)/shard_map/tf,td->fd/dot_general | solution.py:776
  540.4 3.9 convolution_convert_fusion.7.do_ref
  544.4 11.4 %shard_map.184 = (bf16[1024,256]{1,0:T(8,128)(2,1)S(1)}, bf16[1024,256]{1,0:T(8,128)(2,1)S(1)}, bf16[1024,256]{1,0:T(8,128)(2,1)S(1)}) custom-call(bf16[1024,256]{1,0:T(8,128)(2,1)S(1)} %copy-done.24, bf16[1024,256]{1,0:T(8,128)(2,1)S(1)} %copy-done.26, bf16[1024,256]{1,0:T(8,128)(2,1)S(1)} %copy-done.28, ...), custom_call_target="tpu_custom_call" | custom-call | tf_op jit(solution)/shard_map/pallas_call | solution.py:567
  557.2 4.8 convolution_convert_fusion.5
  562.0 14.0 %convolution_convert_fusion = bf16[2048,2048]{1,0:T(8,128)(2,1)} fusion(bf16[1024,2048]{0,1:T(8,128)(2,1)} %concatenate.116, bf16[1024,1024]{1,0:T(8,128)(2,1)} %copy-done.60, bf16[1024,1024]{1,0:T(8,128)(2,1)} %copy-done.59), kind=kOutput, calls=%fused_computation | convolution fusion | flops 8602517504 | bytes 16777216 | tf_op jit(solution)/shard_map/td,tg->dg/dot_general | solution.py:785
  576.0 6.4 convolution_convert_fusion.2
  584.1 3.8 collective-permute-done.69
  589.7 6.9 collective-permute-done.74
  596.6 3.1 collective-permute-done.70
  601.6 9.6 %collective-permute-done.71 = bf16[128,2048]{1,0:T(8,128)(2,1)S(1)} collective-permute-done((bf16[128,2048]{1,0:T(8,128)(2,1)S(1)}, bf16[128,2048]{1,0:T(8,128)(2,1)S(1)}, u32[]{:S(2)}, u32[]{:S(2)}) %collective-permute-start.71) | collective-permute-done | bytes 524320 | tf_op jit(solution)/shard_map/ppermute | solution.py:106
  616.3 9.2 %collective-permute-done.72 = bf16[128,2048]{1,0:T(8,128)(2,1)S(1)} collective-permute-done((bf16[128,2048]{1,0:T(8,128)(2,1)S(1)}, bf16[128,2048]{1,0:T(8,128)(2,1)S(1)}, u32[]{:S(2)}, u32[]{:S(2)}) %collective-permute-start.72) | collective-permute-done | bytes 524320 | tf_op jit(solution)/shard_map/ppermute | solution.py:109
  638.5 9.8 %shard_map.185 = (bf16[128,8192]{1,0:T(8,128)(2,1)}, f32[16,2048]{1,0:T(8,128)S(1)}) custom-call(bf16[128,8192]{1,0:T(8,128)(2,1)S(1)} %bitcast.122, f32[128,8192]{1,0:T(8,128)S(1)} %copy-done.18, f32[128,2048]{1,0:T(8,128)S(1)} %fusion.24.y_ref, f32[128,2048]{1,0:T(8,128)S(1)} %copy-done.20, f32[128,128]{1,0:T(8,128)S(1)} %get-tuple-element.30.aux0_ref, ...), custom_call_target="tpu_custom_call" | custom-call | tf_op jit(solution)/shard_map/pallas_call | solution.py:448
  662.7 14.5 %collective-permute-start.99 = (f32[16,2048]{1,0:T(8,128)S(1)}, f32[16,2048]{1,0:T(8,128)S(1)}, u32[]{:S(2)}, u32[]{:S(2)}) collective-permute-start(f32[16,2048]{1,0:T(8,128)S(1)} %add.922), channel_id=1, source_target_pairs={{0,1},{1,0},{2,3},{3,2},{4,5},{5,4},{6,7},{7,6},{8,9},{9,8},{10,11... | collective-permute-start | bytes 393224 | tf_op jit(solution)/shard_map/ppermute | solution.py:201
  682.5 5.7 collective-permute-done.100
  690.0 3.8 collective-permute-done.95
  709.1 7.1 collective-permute-done.79
  718.4 3.9 collective-permute-done.82
  723.2 9.8 %reduce-scatter.9.cloned.1.call-done = bf16[512,2048]{1,0:T(8,128)(2,1)} async-done(((bf16[2048,2048]{1,0:T(8,128)(2,1)}), bf16[512,2048]{1,0:T(8,128)(2,1)}) %reduce-scatter.9.cloned.1.call-update) | async-done | bytes 2097168 | tf_op jit(solution)/shard_map/reduce_scatter | solution.py:148
  742.4 5.2 collective-permute-done.85
  747.7 27.0 %collective-permute-done.86 = bf16[64,2048]{1,0:T(8,128)(2,1)S(1)} collective-permute-done((bf16[64,2048]{1,0:T(8,128)(2,1)S(1)}, bf16[64,2048]{1,0:T(8,128)(2,1)S(1)}, u32[]{:S(2)}, u32[]{:S(2)}) %collective-permute-start.86) | collective-permute-done | bytes 262176 | tf_op jit(solution)/shard_map/ppermute | solution.py:156
  774.8 5.5 collective-permute-done.87
  (513 shorter events, 229.5 us)
Async XLA Ops:
  7.2 184.1 %all-gather.5.cloned.1.call-start = ((), (), s32[]{:S(2)}) async-start(), calls=%async_computation.4 | async-start | bytes 3932160 | tf_op jit(solution)/shard_map/all_gather | solution.py:141
  8.8 20.7 %collective-permute-start.11 = (bf16[64,768]{1,0:T(8,128)(2,1)S(1)}, bf16[64,768]{1,0:T(8,128)(2,1)S(1)}, u32[]{:S(2)}, u32[]{:S(2)}) collective-permute-start(bf16[64,768]{1,0:T(8,128)(2,1)S(1)} %pad_maximum_fusion.23), channel_id=1, source_target_pairs={{0,16},{4,20},{8,24},{12,28},{16,0},{20,4},{24,8},{28,12},{1,17},{... | collective-permute-start | bytes 294920 | tf_op jit(solution)/shard_map/ppermute | solution.py:136
  11.2 18.3 %collective-permute-start.10 = (bf16[64,768]{1,0:T(8,128)(2,1)S(1)}, bf16[64,768]{1,0:T(8,128)(2,1)S(1)}, u32[]{:S(2)}, u32[]{:S(2)}) collective-permute-start(bf16[64,768]{1,0:T(8,128)(2,1)S(1)} %pad_maximum_fusion.22), channel_id=1, source_target_pairs={{0,12},{4,16},{8,20},{12,24},{16,28},{20,0},{24,4},{28,8},{1,13},{... | collective-permute-start | bytes 294920 | tf_op jit(solution)/shard_map/ppermute | solution.py:136
  11.9 17.5 %collective-permute-start.9 = (bf16[64,768]{1,0:T(8,128)(2,1)}, bf16[64,768]{1,0:T(8,128)(2,1)S(1)}, u32[]{:S(2)}, u32[]{:S(2)}) collective-permute-start(bf16[64,768]{1,0:T(8,128)(2,1)} %pad_maximum_fusion.21), channel_id=1, source_target_pairs={{0,8},{4,12},{8,16},{12,20},{16,24},{20,28},{24,0},{28,4},{1,9},{5... | collective-permute-start | bytes 294920 | tf_op jit(solution)/shard_map/ppermute | solution.py:136
  14.7 13.8 %collective-permute-start.8 = (bf16[64,768]{1,0:T(8,128)(2,1)}, bf16[64,768]{1,0:T(8,128)(2,1)}, u32[]{:S(2)}, u32[]{:S(2)}) collective-permute-start(bf16[64,768]{1,0:T(8,128)(2,1)} %pad_maximum_fusion.20), channel_id=1, source_target_pairs={{0,4},{4,8},{8,12},{12,16},{16,20},{20,24},{24,28},{28,0},{1,5},{5... | collective-permute-start | bytes 294920 | tf_op jit(solution)/shard_map/ppermute | solution.py:136
  37.3 192.0 %all-gather.7.cloned.1.call-start = ((), (), s32[]{:S(2)}) async-start(), calls=%async_computation.5 | async-start | bytes 8650752 | tf_op jit(solution)/shard_map/all_gather | solution.py:597
  38.1 301.1 %all-gather.9.cloned.1.call-start = ((), (), s32[]{:S(2)}) async-start(), calls=%async_computation.6 | async-start | bytes 10485760 | tf_op jit(solution)/shard_map/all_gather | solution.py:141
  40.0 36.5 %collective-permute-start.32 = (bf16[64,2048]{1,0:T(8,128)(2,1)S(1)}, bf16[64,2048]{1,0:T(8,128)(2,1)S(1)}, u32[]{:S(2)}, u32[]{:S(2)}) collective-permute-start(bf16[64,2048]{1,0:T(8,128)(2,1)S(1)} %pad_maximum_fusion.15), channel_id=1, source_target_pairs={{0,12},{4,16},{8,20},{12,24},{16,28},{20,0},{24,4},{28,8},{1,13},{... | collective-permute-start | bytes 786440 | tf_op jit(solution)/shard_map/ppermute | solution.py:136
  41.4 42.8 %collective-permute-start.33 = (bf16[64,2048]{1,0:T(8,128)(2,1)S(1)}, bf16[64,2048]{1,0:T(8,128)(2,1)S(1)}, u32[]{:S(2)}, u32[]{:S(2)}) collective-permute-start(bf16[64,2048]{1,0:T(8,128)(2,1)S(1)} %pad_maximum_fusion.16), channel_id=1, source_target_pairs={{0,16},{4,20},{8,24},{12,28},{16,0},{20,4},{24,8},{28,12},{1,17},{... | collective-permute-start | bytes 786440 | tf_op jit(solution)/shard_map/ppermute | solution.py:136
  43.5 41.4 %collective-permute-start.34 = (bf16[64,2048]{1,0:T(8,128)(2,1)S(1)}, bf16[64,2048]{1,0:T(8,128)(2,1)S(1)}, u32[]{:S(2)}, u32[]{:S(2)}) collective-permute-start(bf16[64,2048]{1,0:T(8,128)(2,1)S(1)} %pad_maximum_fusion.17), channel_id=1, source_target_pairs={{0,20},{4,24},{8,28},{12,0},{16,4},{20,8},{24,12},{28,16},{1,21},{... | collective-permute-start | bytes 786440 | tf_op jit(solution)/shard_map/ppermute | solution.py:136
  46.0 45.9 %collective-permute-start.35 = (bf16[64,2048]{1,0:T(8,128)(2,1)S(1)}, bf16[64,2048]{1,0:T(8,128)(2,1)S(1)}, u32[]{:S(2)}, u32[]{:S(2)}) collective-permute-start(bf16[64,2048]{1,0:T(8,128)(2,1)S(1)} %pad_maximum_fusion.18), channel_id=1, source_target_pairs={{0,24},{4,28},{8,0},{12,4},{16,8},{20,12},{24,16},{28,20},{1,25},{... | collective-permute-start | bytes 786440 | tf_op jit(solution)/shard_map/ppermute | solution.py:136
  49.1 43.7 %collective-permute-start.36 = (bf16[64,2048]{1,0:T(8,128)(2,1)S(1)}, bf16[64,2048]{1,0:T(8,128)(2,1)S(1)}, u32[]{:S(2)}, u32[]{:S(2)}) collective-permute-start(bf16[64,2048]{1,0:T(8,128)(2,1)S(1)} %pad_maximum_fusion.19), channel_id=1, source_target_pairs={{0,28},{4,0},{8,4},{12,8},{16,12},{20,16},{24,20},{28,24},{1,29},{... | collective-permute-start | bytes 786440 | tf_op jit(solution)/shard_map/ppermute | solution.py:136
  93.6 260.2 %all-gather.11.cloned.1.call-start = ((), (), s32[]{:S(2)}) async-start(), calls=%async_computation.7 | async-start | bytes 5242880 | tf_op jit(solution)/shard_map/all_gather | solution.py:757
  101.1 20.8 %collective-permute-start.1 = (bf16[128,2048]{0,1:T(8,128)(2,1)S(1)}, bf16[128,2048]{0,1:T(8,128)(2,1)S(1)}, u32[]{:S(2)}, u32[]{:S(2)}) collective-permute-start(bf16[128,2048]{0,1:T(8,128)(2,1)S(1)} %bitcast.131), channel_id=1, source_target_pairs={{8,0},{16,8},{24,16},{28,24},{20,28},{12,20},{4,12},{0,4},{9,1},{1... | collective-permute-start | bytes 1572872 | tf_op jit(solution)/shard_map/ppermute | solution.py:81
  101.2 21.9 %collective-permute-start = (bf16[128,2048]{0,1:T(8,128)(2,1)S(1)}, bf16[128,2048]{0,1:T(8,128)(2,1)}, u32[]{:S(2)}, u32[]{:S(2)}) collective-permute-start(bf16[128,2048]{0,1:T(8,128)(2,1)S(1)} %bitcast.132), channel_id=1, source_target_pairs={{0,8},{8,16},{16,24},{24,28},{28,20},{20,12},{12,4},{4,0},{1,9},{9... | collective-permute-start | bytes 1572872 | tf_op jit(solution)/shard_map/ppermute | solution.py:80
  102.7 585.6 %reduce-scatter.7.cloned.1.call-start = ((), (), s32[]{:S(2)}) async-start(), calls=%async_computation.9 | async-start | bytes 1310720 | tf_op jit(solution)/shard_map/reduce_scatter | solution.py:170
  122.0 22.6 %collective-permute-start.3 = (bf16[128,2048]{0,1:T(8,128)(2,1)S(1)}, bf16[128,2048]{0,1:T(8,128)(2,1)}, u32[]{:S(2)}, u32[]{:S(2)}) collective-permute-start(bf16[128,2048]{0,1:T(8,128)(2,1)S(1)} %collective-permute-done.1), channel_id=1, source_target_pairs={{8,0},{16,8},{24,16},{28,24},{20,28},{12,20},{4,12},{0,4},{9,1},{1... | collective-permute-start | bytes 1572872 | tf_op jit(solution)/shard_map/ppermute | solution.py:81
  123.1 24.9 %collective-permute-start.2 = (bf16[128,2048]{0,1:T(8,128)(2,1)}, bf16[128,2048]{0,1:T(8,128)(2,1)}, u32[]{:S(2)}, u32[]{:S(2)}) collective-permute-start(bf16[128,2048]{0,1:T(8,128)(2,1)} %collective-permute-done), channel_id=1, source_target_pairs={{0,8},{8,16},{16,24},{24,28},{28,20},{20,12},{12,4},{4,0},{1,9},{9... | collective-permute-start | bytes 1572872 | tf_op jit(solution)/shard_map/ppermute | solution.py:80
  144.6 23.0 %collective-permute-start.5 = (bf16[128,2048]{0,1:T(8,128)(2,1)}, bf16[128,2048]{0,1:T(8,128)(2,1)S(1)}, u32[]{:S(2)}, u32[]{:S(2)}) collective-permute-start(bf16[128,2048]{0,1:T(8,128)(2,1)} %collective-permute-done.3), channel_id=1, source_target_pairs={{8,0},{16,8},{24,16},{28,24},{20,28},{12,20},{4,12},{0,4},{9,1},{1... | collective-permute-start | bytes 1572872 | tf_op jit(solution)/shard_map/ppermute | solution.py:81
  148.0 23.6 %collective-permute-start.4 = (bf16[128,2048]{0,1:T(8,128)(2,1)}, bf16[128,2048]{0,1:T(8,128)(2,1)}, u32[]{:S(2)}, u32[]{:S(2)}) collective-permute-start(bf16[128,2048]{0,1:T(8,128)(2,1)} %collective-permute-done.2), channel_id=1, source_target_pairs={{0,8},{8,16},{16,24},{24,28},{28,20},{20,12},{12,4},{4,0},{1,9},{9... | collective-permute-start | bytes 1572872 | tf_op jit(solution)/shard_map/ppermute | solution.py:80
  248.1 16.3 %collective-permute-start.23 = (bf16[128,2048]{0,1:T(8,128)(2,1)S(1)}, bf16[128,2048]{0,1:T(8,128)(2,1)S(1)}, u32[]{:S(2)}, u32[]{:S(2)}) collective-permute-start(bf16[128,2048]{0,1:T(8,128)(2,1)S(1)} %bitcast.134), channel_id=1, source_target_pairs={{8,0},{16,8},{24,16},{28,24},{20,28},{12,20},{4,12},{0,4},{9,1},{1... | collective-permute-start | bytes 1572872 | tf_op jit(solution)/shard_map/ppermute | solution.py:81
  249.6 16.5 %collective-permute-start.22 = (bf16[128,2048]{0,1:T(8,128)(2,1)S(1)}, bf16[128,2048]{0,1:T(8,128)(2,1)S(1)}, u32[]{:S(2)}, u32[]{:S(2)}) collective-permute-start(bf16[128,2048]{0,1:T(8,128)(2,1)S(1)} %bitcast.135), channel_id=1, source_target_pairs={{0,8},{8,16},{16,24},{24,28},{28,20},{20,12},{12,4},{4,0},{1,9},{9... | collective-permute-start | bytes 1572872 | tf_op jit(solution)/shard_map/ppermute | solution.py:80
  254.8 22.4 %collective-permute-start.47 = (bf16[128,2048]{1,0:T(8,128)(2,1)}, bf16[128,2048]{1,0:T(8,128)(2,1)S(1)}, u32[]{:S(2)}, u32[]{:S(2)}) collective-permute-start(bf16[128,2048]{1,0:T(8,128)(2,1)} %collective-permute-done.45), channel_id=1, source_target_pairs={{0,8},{8,16},{16,24},{24,28},{28,20},{20,12},{12,4},{4,0},{1,9},{9... | collective-permute-start | bytes 1572872 | tf_op jit(solution)/shard_map/ppermute | solution.py:80
  254.8 22.4 %collective-permute-start.48 = (bf16[128,2048]{1,0:T(8,128)(2,1)}, bf16[128,2048]{1,0:T(8,128)(2,1)S(1)}, u32[]{:S(2)}, u32[]{:S(2)}) collective-permute-start(bf16[128,2048]{1,0:T(8,128)(2,1)} %collective-permute-done.46), channel_id=1, source_target_pairs={{8,0},{16,8},{24,16},{28,24},{20,28},{12,20},{4,12},{0,4},{9,1},{1... | collective-permute-start | bytes 1572872 | tf_op jit(solution)/shard_map/ppermute | solution.py:81
  264.4 22.4 %collective-permute-start.25 = (bf16[128,2048]{0,1:T(8,128)(2,1)S(1)}, bf16[128,2048]{0,1:T(8,128)(2,1)S(1)}, u32[]{:S(2)}, u32[]{:S(2)}) collective-permute-start(bf16[128,2048]{0,1:T(8,128)(2,1)S(1)} %collective-permute-done.23), channel_id=1, source_target_pairs={{8,0},{16,8},{24,16},{28,24},{20,28},{12,20},{4,12},{0,4},{9,1},{1... | collective-permute-start | bytes 1572872 | tf_op jit(solution)/shard_map/ppermute | solution.py:81
  266.1 22.4 %collective-permute-start.24 = (bf16[128,2048]{0,1:T(8,128)(2,1)S(1)}, bf16[128,2048]{0,1:T(8,128)(2,1)S(1)}, u32[]{:S(2)}, u32[]{:S(2)}) collective-permute-start(bf16[128,2048]{0,1:T(8,128)(2,1)S(1)} %collective-permute-done.22), channel_id=1, source_target_pairs={{0,8},{8,16},{16,24},{24,28},{28,20},{20,12},{12,4},{4,0},{1,9},{9... | collective-permute-start | bytes 1572872 | tf_op jit(solution)/shard_map/ppermute | solution.py:80
  277.2 22.5 %collective-permute-start.49 = (bf16[128,2048]{1,0:T(8,128)(2,1)S(1)}, bf16[128,2048]{1,0:T(8,128)(2,1)S(1)}, u32[]{:S(2)}, u32[]{:S(2)}) collective-permute-start(bf16[128,2048]{1,0:T(8,128)(2,1)S(1)} %collective-permute-done.47), channel_id=1, source_target_pairs={{0,8},{8,16},{16,24},{24,28},{28,20},{20,12},{12,4},{4,0},{1,9},{9... | collective-permute-start | bytes 1572872 | tf_op jit(solution)/shard_map/ppermute | solution.py:80
  277.2 23.2 %collective-permute-start.50 = (bf16[128,2048]{1,0:T(8,128)(2,1)S(1)}, bf16[128,2048]{1,0:T(8,128)(2,1)S(1)}, u32[]{:S(2)}, u32[]{:S(2)}) collective-permute-start(bf16[128,2048]{1,0:T(8,128)(2,1)S(1)} %collective-permute-done.48), channel_id=1, source_target_pairs={{8,0},{16,8},{24,16},{28,24},{20,28},{12,20},{4,12},{0,4},{9,1},{1... | collective-permute-start | bytes 1572872 | tf_op jit(solution)/shard_map/ppermute | solution.py:81
  286.8 22.5 %collective-permute-start.27 = (bf16[128,2048]{0,1:T(8,128)(2,1)S(1)}, bf16[128,2048]{0,1:T(8,128)(2,1)S(1)}, u32[]{:S(2)}, u32[]{:S(2)}) collective-permute-start(bf16[128,2048]{0,1:T(8,128)(2,1)S(1)} %collective-permute-done.25), channel_id=1, source_target_pairs={{8,0},{16,8},{24,16},{28,24},{20,28},{12,20},{4,12},{0,4},{9,1},{1... | collective-permute-start | bytes 1572872 | tf_op jit(solution)/shard_map/ppermute | solution.py:81
  288.4 22.7 %collective-permute-start.26 = (bf16[128,2048]{0,1:T(8,128)(2,1)S(1)}, bf16[128,2048]{0,1:T(8,128)(2,1)S(1)}, u32[]{:S(2)}, u32[]{:S(2)}) collective-permute-start(bf16[128,2048]{0,1:T(8,128)(2,1)S(1)} %collective-permute-done.24), channel_id=1, source_target_pairs={{0,8},{8,16},{16,24},{24,28},{28,20},{20,12},{12,4},{4,0},{1,9},{9... | collective-permute-start | bytes 1572872 | tf_op jit(solution)/shard_map/ppermute | solution.py:80
  300.4 35.4 %collective-permute-start.51 = (bf16[64,2048]{1,0:T(8,128)(2,1)}, bf16[64,2048]{1,0:T(8,128)(2,1)}, u32[]{:S(2)}, u32[]{:S(2)}) collective-permute-start(bf16[64,2048]{1,0:T(8,128)(2,1)} %slice.463), channel_id=1, source_target_pairs={{0,8},{8,16},{16,24},{24,28},{28,20},{20,12},{12,4},{4,0},{1,9},{9... | collective-permute-start | bytes 786440 | tf_op jit(solution)/shard_map/ppermute | solution.py:77
  301.1 36.3 %collective-permute-start.52 = (bf16[64,2048]{1,0:T(8,128)(2,1)}, bf16[64,2048]{1,0:T(8,128)(2,1)}, u32[]{:S(2)}, u32[]{:S(2)}) collective-permute-start(bf16[64,2048]{1,0:T(8,128)(2,1)} %slice.464), channel_id=1, source_target_pairs={{8,0},{16,8},{24,16},{28,24},{20,28},{12,20},{4,12},{0,4},{9,1},{1... | collective-permute-start | bytes 786440 | tf_op jit(solution)/shard_map/ppermute | solution.py:78
  309.5 18.2 %collective-permute-start.29 = (bf16[64,2048]{0,1:T(8,128)(2,1)S(1)}, bf16[64,2048]{0,1:T(8,128)(2,1)S(1)}, u32[]{:S(2)}, u32[]{:S(2)}) collective-permute-start(bf16[64,2048]{0,1:T(8,128)(2,1)S(1)} %slice.449), channel_id=1, source_target_pairs={{8,0},{16,8},{24,16},{28,24},{20,28},{12,20},{4,12},{0,4},{9,1},{1... | collective-permute-start | bytes 786440 | tf_op jit(solution)/shard_map/ppermute | solution.py:78
  311.1 17.4 %collective-permute-start.28 = (bf16[64,2048]{0,1:T(8,128)(2,1)S(1)}, bf16[64,2048]{0,1:T(8,128)(2,1)}, u32[]{:S(2)}, u32[]{:S(2)}) collective-permute-start(bf16[64,2048]{0,1:T(8,128)(2,1)S(1)} %bitcast.139), channel_id=1, source_target_pairs={{0,8},{8,16},{16,24},{24,28},{28,20},{20,12},{12,4},{4,0},{1,9},{9... | collective-permute-start | bytes 786440 | tf_op jit(solution)/shard_map/ppermute | solution.py:77
  380.0 13.4 %collective-permute-start.53 = (bf16[64,2048]{1,0:T(8,128)(2,1)S(1)}, bf16[64,2048]{1,0:T(8,128)(2,1)S(1)}, u32[]{:S(2)}, u32[]{:S(2)}) collective-permute-start(bf16[64,2048]{1,0:T(8,128)(2,1)S(1)} %get-tuple-element.91), channel_id=1, source_target_pairs={{0,8},{8,16},{16,24},{24,28},{28,20},{20,12},{12,4},{4,0},{1,9},{9... | collective-permute-start | bytes 786440 | tf_op jit(solution)/shard_map/ppermute | solution.py:106
  393.6 15.2 %collective-permute-start.58 = (bf16[128,2048]{1,0:T(8,128)(2,1)S(1)}, bf16[128,2048]{1,0:T(8,128)(2,1)S(1)}, u32[]{:S(2)}, u32[]{:S(2)}) collective-permute-start(bf16[128,2048]{1,0:T(8,128)(2,1)S(1)} %pad_maximum_fusion.10), channel_id=1, source_target_pairs={{8,0},{16,8},{24,16},{28,24},{20,28},{12,20},{4,12},{0,4},{9,1},{1... | collective-permute-start | bytes 1572872 | tf_op jit(solution)/shard_map/ppermute | solution.py:107
  393.7 15.1 %collective-permute-start.54 = (bf16[128,2048]{1,0:T(8,128)(2,1)S(1)}, bf16[128,2048]{1,0:T(8,128)(2,1)S(1)}, u32[]{:S(2)}, u32[]{:S(2)}) collective-permute-start(bf16[128,2048]{1,0:T(8,128)(2,1)S(1)} %pad_maximum_fusion.9), channel_id=1, source_target_pairs={{0,8},{8,16},{16,24},{24,28},{28,20},{20,12},{12,4},{4,0},{1,9},{9... | collective-permute-start | bytes 1572872 | tf_op jit(solution)/shard_map/ppermute | solution.py:106
  399.1 20.9 %collective-permute-start.42 = (bf16[128,2048]{1,0:T(8,128)(2,1)S(1)}, bf16[128,2048]{1,0:T(8,128)(2,1)S(1)}, u32[]{:S(2)}, u32[]{:S(2)}) collective-permute-start(bf16[128,2048]{1,0:T(8,128)(2,1)S(1)} %pad_maximum_fusion.8), channel_id=1, source_target_pairs={{8,0},{16,8},{24,16},{28,24},{20,28},{12,20},{4,12},{0,4},{9,1},{1... | collective-permute-start | bytes 1572872 | tf_op jit(solution)/shard_map/ppermute | solution.py:107
  399.2 20.8 %collective-permute-start.38 = (bf16[128,2048]{1,0:T(8,128)(2,1)S(1)}, bf16[128,2048]{1,0:T(8,128)(2,1)S(1)}, u32[]{:S(2)}, u32[]{:S(2)}) collective-permute-start(bf16[128,2048]{1,0:T(8,128)(2,1)S(1)} %pad_maximum_fusion.7), channel_id=1, source_target_pairs={{0,8},{8,16},{16,24},{24,28},{28,20},{20,12},{12,4},{4,0},{1,9},{9... | collective-permute-start | bytes 1572872 | tf_op jit(solution)/shard_map/ppermute | solution.py:106
  409.2 20.3 %collective-permute-start.55 = (bf16[128,2048]{1,0:T(8,128)(2,1)S(1)}, bf16[128,2048]{1,0:T(8,128)(2,1)S(1)}, u32[]{:S(2)}, u32[]{:S(2)}) collective-permute-start(bf16[128,2048]{1,0:T(8,128)(2,1)S(1)} %get-tuple-element.87), channel_id=1, source_target_pairs={{0,8},{8,16},{16,24},{24,28},{28,20},{20,12},{12,4},{4,0},{1,9},{9... | collective-permute-start | bytes 1572872 | tf_op jit(solution)/shard_map/ppermute | solution.py:106
  410.7 20.5 %collective-permute-start.59 = (bf16[128,2048]{1,0:T(8,128)(2,1)S(1)}, bf16[128,2048]{1,0:T(8,128)(2,1)S(1)}, u32[]{:S(2)}, u32[]{:S(2)}) collective-permute-start(bf16[128,2048]{1,0:T(8,128)(2,1)S(1)} %get-tuple-element.88), channel_id=1, source_target_pairs={{8,0},{16,8},{24,16},{28,24},{20,28},{12,20},{4,12},{0,4},{9,1},{1... | collective-permute-start | bytes 1572872 | tf_op jit(solution)/shard_map/ppermute | solution.py:107
  420.4 20.3 %collective-permute-start.39 = (bf16[128,2048]{1,0:T(8,128)(2,1)S(1)}, bf16[128,2048]{1,0:T(8,128)(2,1)S(1)}, u32[]{:S(2)}, u32[]{:S(2)}) collective-permute-start(bf16[128,2048]{1,0:T(8,128)(2,1)S(1)} %get-tuple-element.97), channel_id=1, source_target_pairs={{0,8},{8,16},{16,24},{24,28},{28,20},{20,12},{12,4},{4,0},{1,9},{9... | collective-permute-start | bytes 1572872 | tf_op jit(solution)/shard_map/ppermute | solution.py:106
  421.9 20.6 %collective-permute-start.43 = (bf16[128,2048]{1,0:T(8,128)(2,1)S(1)}, bf16[128,2048]{1,0:T(8,128)(2,1)S(1)}, u32[]{:S(2)}, u32[]{:S(2)}) collective-permute-start(bf16[128,2048]{1,0:T(8,128)(2,1)S(1)} %get-tuple-element.98), channel_id=1, source_target_pairs={{8,0},{16,8},{24,16},{28,24},{20,28},{12,20},{4,12},{0,4},{9,1},{1... | collective-permute-start | bytes 1572872 | tf_op jit(solution)/shard_map/ppermute | solution.py:107
  431.6 20.3 %collective-permute-start.56 = (bf16[128,2048]{1,0:T(8,128)(2,1)S(1)}, bf16[128,2048]{1,0:T(8,128)(2,1)S(1)}, u32[]{:S(2)}, u32[]{:S(2)}) collective-permute-start(bf16[128,2048]{1,0:T(8,128)(2,1)S(1)} %get-tuple-element.85), channel_id=1, source_target_pairs={{0,8},{8,16},{16,24},{24,28},{28,20},{20,12},{12,4},{4,0},{1,9},{9... | collective-permute-start | bytes 1572872 | tf_op jit(solution)/shard_map/ppermute | solution.py:109
  433.2 20.6 %collective-permute-start.60 = (bf16[128,2048]{1,0:T(8,128)(2,1)S(1)}, bf16[128,2048]{1,0:T(8,128)(2,1)S(1)}, u32[]{:S(2)}, u32[]{:S(2)}) collective-permute-start(bf16[128,2048]{1,0:T(8,128)(2,1)S(1)} %get-tuple-element.86), channel_id=1, source_target_pairs={{8,0},{16,8},{24,16},{28,24},{20,28},{12,20},{4,12},{0,4},{9,1},{1... | collective-permute-start | bytes 1572872 | tf_op jit(solution)/shard_map/ppermute | solution.py:110
  443.9 19.4 %collective-permute-start.40 = (bf16[128,2048]{1,0:T(8,128)(2,1)}, bf16[128,2048]{1,0:T(8,128)(2,1)}, u32[]{:S(2)}, u32[]{:S(2)}) collective-permute-start(bf16[128,2048]{1,0:T(8,128)(2,1)} %get-tuple-element.95), channel_id=1, source_target_pairs={{0,8},{8,16},{16,24},{24,28},{28,20},{20,12},{12,4},{4,0},{1,9},{9... | collective-permute-start | bytes 1572872 | tf_op jit(solution)/shard_map/ppermute | solution.py:109
  445.4 19.7 %collective-permute-start.44 = (bf16[128,2048]{1,0:T(8,128)(2,1)}, bf16[128,2048]{1,0:T(8,128)(2,1)}, u32[]{:S(2)}, u32[]{:S(2)}) collective-permute-start(bf16[128,2048]{1,0:T(8,128)(2,1)} %get-tuple-element.96), channel_id=1, source_target_pairs={{8,0},{16,8},{24,16},{28,24},{20,28},{12,20},{4,12},{0,4},{9,1},{1... | collective-permute-start | bytes 1572872 | tf_op jit(solution)/shard_map/ppermute | solution.py:110
  504.1 13.2 %collective-permute-start.65 = (bf16[128,2048]{1,0:T(8,128)(2,1)S(1)}, bf16[128,2048]{1,0:T(8,128)(2,1)S(1)}, u32[]{:S(2)}, u32[]{:S(2)}) collective-permute-start(bf16[128,2048]{1,0:T(8,128)(2,1)S(1)} %collective-permute-done.63), channel_id=1, source_target_pairs={{0,8},{8,16},{16,24},{24,28},{28,20},{20,12},{12,4},{4,0},{1,9},{9... | collective-permute-start | bytes 1572872 | tf_op jit(solution)/shard_map/ppermute | solution.py:80
  530.8 164.4 %reduce-scatter.11.cloned.1.call-start = ((), (), s32[]{:S(2)}) async-start(), calls=%async_computation.11 | async-start | bytes 5242880 | tf_op jit(solution)/shard_map/reduce_scatter | solution.py:170
  540.3 157.8 %reduce-scatter.5.cloned.1.call-start = ((), (), s32[]{:S(2)}) async-start(), calls=%async_computation.8 | async-start | bytes 3932160 | tf_op jit(solution)/shard_map/reduce_scatter | solution.py:148
  561.9 171.1 %reduce-scatter.9.cloned.1.call-start = ((), (), s32[]{:S(2)}) async-start(), calls=%async_computation.10 | async-start | bytes 10485760 | tf_op jit(solution)/shard_map/reduce_scatter | solution.py:148
  615.1 36.2 %collective-permute-start.96 = (f32[16,2048]{1,0:T(8,128)S(1)}, f32[16,2048]{1,0:T(8,128)}, u32[]{:S(2)}, u32[]{:S(2)}) collective-permute-start(f32[16,2048]{1,0:T(8,128)S(1)} %get-tuple-element.47), channel_id=1, source_target_pairs={{0,4},{4,0},{8,12},{12,8},{16,20},{20,16},{24,28},{28,24},{1,5},{5... | collective-permute-start | bytes 393224 | tf_op jit(solution)/shard_map/ppermute | solution.py:201
  658.0 19.2 %collective-permute-start.93 = (f32[16,2048]{1,0:T(8,128)S(1)}, f32[16,2048]{1,0:T(8,128)S(1)}, u32[]{:S(2)}, u32[]{:S(2)}) collective-permute-start(f32[16,2048]{1,0:T(8,128)S(1)} %add.916), channel_id=1, source_target_pairs={{0,16},{4,20},{8,24},{12,28},{16,0},{20,4},{24,8},{28,12},{1,17},{... | collective-permute-start | bytes 393224 | tf_op jit(solution)/shard_map/ppermute | solution.py:201
  662.7 16.9 %collective-permute-start.99 = (f32[16,2048]{1,0:T(8,128)S(1)}, f32[16,2048]{1,0:T(8,128)S(1)}, u32[]{:S(2)}, u32[]{:S(2)}) collective-permute-start(f32[16,2048]{1,0:T(8,128)S(1)} %add.922), channel_id=1, source_target_pairs={{0,1},{1,0},{2,3},{3,2},{4,5},{5,4},{6,7},{7,6},{8,9},{9,8},{10,11... | collective-permute-start | bytes 393224 | tf_op jit(solution)/shard_map/ppermute | solution.py:201
  702.2 14.0 %collective-permute-start.79 = (bf16[64,768]{1,0:T(8,128)(2,1)S(1)}, bf16[64,768]{1,0:T(8,128)(2,1)S(1)}, u32[]{:S(2)}, u32[]{:S(2)}) collective-permute-start(bf16[64,768]{1,0:T(8,128)(2,1)S(1)} %get-tuple-element.133), channel_id=1, source_target_pairs={{0,12},{4,16},{8,20},{12,24},{16,28},{20,0},{24,4},{28,8},{1,13},{... | collective-permute-start | bytes 294920 | tf_op jit(solution)/shard_map/ppermute | solution.py:156
  705.1 13.3 %collective-permute-start.80 = (bf16[64,768]{1,0:T(8,128)(2,1)S(1)}, bf16[64,768]{1,0:T(8,128)(2,1)S(1)}, u32[]{:S(2)}, u32[]{:S(2)}) collective-permute-start(bf16[64,768]{1,0:T(8,128)(2,1)S(1)} %get-tuple-element.132), channel_id=1, source_target_pairs={{0,16},{4,20},{8,24},{12,28},{16,0},{20,4},{24,8},{28,12},{1,17},{... | collective-permute-start | bytes 294920 | tf_op jit(solution)/shard_map/ppermute | solution.py:156
  705.1 13.3 %collective-permute-start.81 = (bf16[64,768]{1,0:T(8,128)(2,1)S(1)}, bf16[64,768]{1,0:T(8,128)(2,1)S(1)}, u32[]{:S(2)}, u32[]{:S(2)}) collective-permute-start(bf16[64,768]{1,0:T(8,128)(2,1)S(1)} %get-tuple-element.131), channel_id=1, source_target_pairs={{0,20},{4,24},{8,28},{12,0},{16,4},{20,8},{24,12},{28,16},{1,21},{... | collective-permute-start | bytes 294920 | tf_op jit(solution)/shard_map/ppermute | solution.py:156
  706.7 15.6 %collective-permute-start.82 = (bf16[64,768]{1,0:T(8,128)(2,1)S(1)}, bf16[64,768]{1,0:T(8,128)(2,1)S(1)}, u32[]{:S(2)}, u32[]{:S(2)}) collective-permute-start(bf16[64,768]{1,0:T(8,128)(2,1)S(1)} %get-tuple-element.130), channel_id=1, source_target_pairs={{0,24},{4,28},{8,0},{12,4},{16,8},{20,12},{24,16},{28,20},{1,25},{... | collective-permute-start | bytes 294920 | tf_op jit(solution)/shard_map/ppermute | solution.py:156
  709.0 13.7 %collective-permute-start.83 = (bf16[64,768]{1,0:T(8,128)(2,1)S(1)}, bf16[64,768]{1,0:T(8,128)(2,1)S(1)}, u32[]{:S(2)}, u32[]{:S(2)}) collective-permute-start(bf16[64,768]{1,0:T(8,128)(2,1)S(1)} %get-tuple-element.129), channel_id=1, source_target_pairs={{0,28},{4,0},{8,4},{12,8},{16,12},{20,16},{24,20},{28,24},{1,29},{... | collective-permute-start | bytes 294920 | tf_op jit(solution)/shard_map/ppermute | solution.py:156
  737.2 37.5 %collective-permute-start.86 = (bf16[64,2048]{1,0:T(8,128)(2,1)S(1)}, bf16[64,2048]{1,0:T(8,128)(2,1)S(1)}, u32[]{:S(2)}, u32[]{:S(2)}) collective-permute-start(bf16[64,2048]{1,0:T(8,128)(2,1)S(1)} %get-tuple-element.109), channel_id=1, source_target_pairs={{0,12},{4,16},{8,20},{12,24},{16,28},{20,0},{24,4},{28,8},{1,13},{... | collective-permute-start | bytes 786440 | tf_op jit(solution)/shard_map/ppermute | solution.py:156
  738.3 42.0 %collective-permute-start.87 = (bf16[64,2048]{1,0:T(8,128)(2,1)S(1)}, bf16[64,2048]{1,0:T(8,128)(2,1)S(1)}, u32[]{:S(2)}, u32[]{:S(2)}) collective-permute-start(bf16[64,2048]{1,0:T(8,128)(2,1)S(1)} %get-tuple-element.108), channel_id=1, source_target_pairs={{0,16},{4,20},{8,24},{12,28},{16,0},{20,4},{24,8},{28,12},{1,17},{... | collective-permute-start | bytes 786440 | tf_op jit(solution)/shard_map/ppermute | solution.py:156
  739.6 40.8 %collective-permute-start.88 = (bf16[64,2048]{1,0:T(8,128)(2,1)S(1)}, bf16[64,2048]{1,0:T(8,128)(2,1)S(1)}, u32[]{:S(2)}, u32[]{:S(2)}) collective-permute-start(bf16[64,2048]{1,0:T(8,128)(2,1)S(1)} %get-tuple-element.107), channel_id=1, source_target_pairs={{0,20},{4,24},{8,28},{12,0},{16,4},{20,8},{24,12},{28,16},{1,21},{... | collective-permute-start | bytes 786440 | tf_op jit(solution)/shard_map/ppermute | solution.py:156
  742.0 41.4 %collective-permute-start.89 = (bf16[64,2048]{1,0:T(8,128)(2,1)S(1)}, bf16[64,2048]{1,0:T(8,128)(2,1)S(1)}, u32[]{:S(2)}, u32[]{:S(2)}) collective-permute-start(bf16[64,2048]{1,0:T(8,128)(2,1)S(1)} %get-tuple-element.106), channel_id=1, source_target_pairs={{0,24},{4,28},{8,0},{12,4},{16,8},{20,12},{24,16},{28,20},{1,25},{... | collective-permute-start | bytes 786440 | tf_op jit(solution)/shard_map/ppermute | solution.py:156
  747.6 36.9 %collective-permute-start.90 = (bf16[64,2048]{1,0:T(8,128)(2,1)S(1)}, bf16[64,2048]{1,0:T(8,128)(2,1)S(1)}, u32[]{:S(2)}, u32[]{:S(2)}) collective-permute-start(bf16[64,2048]{1,0:T(8,128)(2,1)S(1)} %get-tuple-element.105), channel_id=1, source_target_pairs={{0,28},{4,0},{8,4},{12,8},{16,12},{20,16},{24,20},{28,24},{1,29},{... | collective-permute-start | bytes 786440 | tf_op jit(solution)/shard_map/ppermute | solution.py:156
  (106 other events, 1421.6 us)
Sparse Core Ops, SparseCore 0:
  37.4 30.3 all-gather.4
  70.7 100.0 all-gather.6
  172.9 58.7 all-gather.8
  233.2 34.4 all-gather.10
  531.0 33.7 reduce-scatter.6
  567.2 44.5 reduce-scatter.10
  614.9 37.9 reduce-scatter.4
  655.6 77.3 reduce-scatter.8

commit v2 on v1

--- a/solution.py
+++ b/solution.py
@@ -66,109 +66,395 @@
     return jnp.sum(jnp.where(at[:, None] == ids[None, :], order[None, :], 0), axis=1)
 
 
-def ring_gather(block):
+def ring_gather(block, early=None):
     n = lax.axis_size("ctx")
     ahead, back = ring_perms(n)
-    one = other = block
+    moving = [block, block]
     blocks = [block]
-    for k in range(1, n // 2 + 1):
-        if 2 * k == n:
+    for step in range(n // 2):
+        if 2 * (step + 1) == n:
             half = block.shape[0] // 2
-            one = lax.ppermute(one[:half], "ctx", ahead)
-            other = lax.ppermute(other[half:], "ctx", back)
-        else:
-            one = lax.ppermute(one, "ctx", ahead)
-            other = lax.ppermute(other, "ctx", back)
-        blocks += [one, other]
-    return jnp.concatenate(blocks, axis=0)
-
-
-def ring_scatter(partial, rows):
+            moving = [moving[0][:half], moving[1][half:]]
+        moving = [lax.ppermute(moving[0], "ctx", ahead), lax.ppermute(moving[1], "ctx", back)]
+        if early:
+            moving = early(step, moving)
+        blocks += moving
+    return blocks
+
+
+def add_pair(moving, partial, rows, slots, spans):
+    def kernel(one_ref, other_ref, one_own, other_own, one_out, other_out):
+        for ref, own, out, (first, last) in (
+            (one_ref, one_own, one_out, spans[0]),
+            (other_ref, other_own, other_out, spans[1]),
+        ):
+            if last - first < rows:
+                out[...] = own[...]
+            here = slice(first, last)
+            out[here, :] = (ref[...].astype(F32) + own[here, :].astype(F32)).astype(BF16)
+
+    def whole(shape, at):
+        return pl.BlockSpec(shape, lambda i: (at, 0))
+
+    shape = (rows, partial.shape[1])
+    return pl.pallas_call(
+        kernel,
+        grid=(1,),
+        in_specs=[whole(v.shape, 0) for v in moving] + [whole(shape, at) for at in slots],
+        out_specs=[whole(shape, 0)] * 2,
+        out_shape=[jax.ShapeDtypeStruct(shape, BF16)] * 2,
+        cost_estimate=cost(moving, [jax.ShapeDtypeStruct(shape, BF16)] * 4),
+        compiler_params=room(12 * rows * partial.shape[1] * 2),
+    )(*moving, partial, partial)
+
+
+def ring_scatter(partial, rows, early=None):
     n = lax.axis_size("ctx")
     ahead, back = ring_perms(n)
     offsets = ring_offsets(n)
-
-    def part(offset):
-        at = offsets.index(offset)
-        return partial[at * rows : (at + 1) * rows]
-
-    def add(moving, offset, first, last):
-        own = part(offset)
-        sent = [own[:first], own[first:last], own[last:]]
-        sent[1] = (moving.astype(F32) + sent[1].astype(F32)).astype(BF16)
-        return jnp.concatenate(sent, axis=0)
-
     half = n // 2
     mid = rows // 2
-    one, other = part(-half)[:mid], part(-half)[mid:]
-    span_one, span_other = (0, mid), (mid, rows)
-    for k in range(half - 1, 0, -1):
-        one = add(lax.ppermute(one, "ctx", ahead), k, *span_one)
-        other = add(lax.ppermute(other, "ctx", back), -k, *span_other)
-        span_one = span_other = (0, rows)
-    one = lax.ppermute(one, "ctx", ahead).astype(F32)
-    other = lax.ppermute(other, "ctx", back).astype(F32)
+    last = offsets.index(-half) * rows
+    moving = [partial[last : last + mid], partial[last + mid : last + rows]]
+    spans = [(0, mid), (mid, rows)]
+    for step in range(half):
+        moving = [lax.ppermute(moving[0], "ctx", ahead), lax.ppermute(moving[1], "ctx", back)]
+        if early:
+            moving = early(step, moving)
+        k = half - 1 - step
+        if k:
+            slots = [offsets.index(k), offsets.index(-k)]
+            moving = add_pair(moving, partial, rows, slots, spans)
+            spans = [(0, rows), (0, rows)]
     if half == 1:
-        return part(0).astype(F32) + jnp.concatenate([one, other], axis=0)
-    return part(0).astype(F32) + one + other
-
-
-def to_columns(weight, parts):
+        moving = [jnp.concatenate(moving, axis=0), jnp.zeros((rows, partial.shape[1]), BF16)]
+    return (partial, *moving)
+
+
+def joined_dot(blocks, weight, nt=False, tile=256, dtype=F32):
+    total, depth = sum(v.shape[0] for v in blocks), blocks[0].shape[1]
+    columns = weight.shape[0] if nt else weight.shape[1]
+    tile = min(tile, columns)
+    count = len(blocks)
+
+    def kernel(*refs):
+        w_ref, joined, out = refs[count:]
+
+        @pl.when(pl.program_id(0) == 0)
+        def _():
+            at = 0
+            for ref in refs[:count]:
+                joined[at : at + ref.shape[0], :] = ref[...]
+                at += ref.shape[0]
+
+        dims = (((1,), (1 if nt else 0,)), ((), ()))
+        out[...] = lax.dot_general(
+            joined[...], w_ref[...], dims, preferred_element_type=F32
+        ).astype(dtype)
+
+    once = pl.Buffered(1)
+    outs = [
+        jax.ShapeDtypeStruct((total, depth), BF16),
+        jax.ShapeDtypeStruct((total, columns), dtype),
+    ]
+    w_spec = (
+        pl.BlockSpec((tile, depth), lambda j: (j, 0))
+        if nt
+        else pl.BlockSpec((depth, tile), lambda j: (0, j))
+    )
+    return pl.pallas_call(
+        kernel,
+        grid=(columns // tile,),
+        in_specs=[
+            pl.BlockSpec(v.shape, lambda j: (0, 0), pipeline_mode=once) for v in blocks
+        ]
+        + [w_spec],
+        out_specs=[
+            pl.BlockSpec((total, depth), lambda j: (0, 0), pipeline_mode=once),
+            pl.BlockSpec((total, tile), lambda j: (0, j)),
+        ],
+        out_shape=outs,
+        cost_estimate=cost((*blocks, weight), outs, 2 * total * depth * columns),
+        compiler_params=room(4 * total * depth, 4 * tile * depth, 12 * total * tile),
+    )(*blocks, weight)
+
+
+def ffn_specs(blocks, width):
+    total, depth = sum(v.shape[0] for v in blocks), blocks[0].shape[1]
+    tile = min(256 if total <= 1024 else 128, width)
+    once = pl.Buffered(1)
+    whole = [pl.BlockSpec(v.shape, lambda j: (0, 0), pipeline_mode=once) for v in blocks]
+    joined = pl.BlockSpec((total, depth), lambda j: (0, 0), pipeline_mode=once)
+    return (total, depth, tile, whole, joined, pl.BlockSpec((total, tile), lambda j: (0, j)))
+
+
+def join_once(refs, joined):
+    @pl.when(pl.program_id(0) == 0)
+    def _():
+        at = 0
+        for ref in refs:
+            joined[at : at + ref.shape[0], :] = ref[...]
+            at += ref.shape[0]
+
+
+def ffn_enter(blocks, weight):
+    width = weight.shape[1] // 2
+    total, depth, tile, whole, joined_spec, cut = ffn_specs(blocks, width)
+    count, steps = len(blocks), width // tile
+
+    def kernel(*refs):
+        wg_ref, wu_ref, joined, gate_ref, up_ref, hidden_ref = refs[count:]
+        join_once(refs[:count], joined)
+        gate = jnp.dot(joined[...], wg_ref[...], preferred_element_type=F32)
+        up = jnp.dot(joined[...], wu_ref[...], preferred_element_type=F32)
+        gate_ref[...] = gate
+        up_ref[...] = up
+        hidden_ref[...] = (gate * jax.nn.sigmoid(gate) * up).astype(BF16)
+
+    outs = [
+        jax.ShapeDtypeStruct((total, depth), BF16),
+        jax.ShapeDtypeStruct((total, width), F32),
+        jax.ShapeDtypeStruct((total, width), F32),
+        jax.ShapeDtypeStruct((total, width), BF16),
+    ]
+    w_specs = [
+        pl.BlockSpec((depth, tile), lambda j: (0, j)),
+        pl.BlockSpec((depth, tile), lambda j: (0, steps + j)),
+    ]
+    return pl.pallas_call(
+        kernel,
+        grid=(steps,),
+        in_specs=whole + w_specs,
+        out_specs=[joined_spec, cut, cut, cut],
+        out_shape=outs,
+        cost_estimate=cost((*blocks, weight), outs, 4 * total * depth * width),
+        compiler_params=room(4 * total * depth, 8 * tile * depth, 36 * total * tile),
+    )(*blocks, weight, weight)
+
+
+def ffn_back(blocks, weight, gate, up):
+    width = weight.shape[0]
+    total, depth, tile, whole, joined_spec, cut = ffn_specs(blocks, width)
+    count = len(blocks)
+
+    def kernel(*refs):
+        w_ref, gate_ref, up_ref, joined, d_gate_ref, d_up_ref = refs[count:]
+        join_once(refs[:count], joined)
+        d_hidden = lax.dot_general(
+            joined[...], w_ref[...], (((1,), (1,)), ((), ())), preferred_element_type=F32
+        )
+        d_hidden = d_hidden.astype(BF16).astype(F32)
+        gate = gate_ref[...]
+        open_gate = jax.nn.sigmoid(gate)
+        part = d_hidden * open_gate
+        d_up_ref[...] = (part * gate).astype(BF16)
+        d_gate_ref[...] = (part * up_ref[...] * (1.0 + gate * (1.0 - open_gate))).astype(BF16)
+
+    outs = [jax.ShapeDtypeStruct((total, depth), BF16)]
+    outs += [jax.ShapeDtypeStruct((total, width), BF16)] * 2
+    return pl.pallas_call(
+        kernel,
+        grid=(width // tile,),
+        in_specs=whole + [pl.BlockSpec((tile, depth), lambda j: (j, 0)), cut, cut],
+        out_specs=[joined_spec, cut, cut],
+        out_shape=outs,
+        cost_estimate=cost((*blocks, weight, gate, up), outs, 2 * total * depth * width),
+        compiler_params=room(4 * total * depth, 4 * tile * depth, 40 * total * tile),
+    )(*blocks, weight, gate, up)
+
+
+def ffn_leave(d_gate, d_up, weight):
+    total, width = d_gate.shape
+    depth, tile = weight.shape[0], 256
+
+    def kernel(g_ref, u_ref, w_ref, out_ref):
+        nt = (((1,), (1,)), ((), ()))
+        out = lax.dot_general(g_ref[...], w_ref[:, :width], nt, preferred_element_type=F32)
+        out += lax.dot_general(u_ref[...], w_ref[:, width:], nt, preferred_element_type=F32)
+        out_ref[...] = out.astype(BF16)
+
+    out = jax.ShapeDtypeStruct((total, depth), BF16)
+    resident = pl.BlockSpec((total, width), lambda j: (0, 0), pipeline_mode=pl.Buffered(1))
+    return pl.pallas_call(
+        kernel,
+        grid=(depth // tile,),
+        in_specs=[resident, resident, pl.BlockSpec((tile, 2 * width), lambda j: (j, 0))],
+        out_specs=pl.BlockSpec((total, tile), lambda j: (0, j)),
+        out_shape=out,
+        cost_estimate=cost((d_gate, d_up, weight), [out], 4 * total * depth * width),
+        compiler_params=room(4 * total * width, 8 * tile * width, 12 * total * tile),
+    )(d_gate, d_up, weight)
+
+
+def after(value, *others):
+    return lax.optimization_barrier((value, *others))[0]
+
+
+def cost(ins, outs, flops=0, exps=0):
+    moved = sum(v.size * v.dtype.itemsize for v in (*ins, *outs))
+    return pl.CostEstimate(flops=flops, bytes_accessed=moved, transcendentals=exps)
+
+
+def room(*sizes):
+    return pltpu.CompilerParams(vmem_limit_bytes=60 * MIB)
+
+
+def bytes_of(*arrays):
+    return sum(v.size * v.dtype.itemsize for v in arrays)
+
+
+def place_call(kernel, place, ins, outs, scratch=()):
+    vmem = pl.BlockSpec(memory_space=pltpu.VMEM)
+    return pl.pallas_call(
+        kernel,
+        in_specs=[pl.BlockSpec(memory_space=pltpu.SMEM)] + [vmem] * len(ins),
+        out_specs=[vmem] * len(outs),
+        out_shape=outs,
+        scratch_shapes=scratch,
+        cost_estimate=cost(ins, outs),
+        compiler_params=room(bytes_of(*ins, *outs) * 3 // 2),
+    )(place.reshape(1), *ins)
+
+
+def shifted(place_ref, k, n):
+    return lax.rem(place_ref[0] + (k + n), n)
+
+
+def lanes_at(index, width):
+    return pl.ds(pl.multiple_of(index * width, width), width)
+
+
+def cut_columns(weight, parts, place, n):
+    rows = weight.shape[0]
+    width = weight.shape[1] // parts // n
+
+    def kernel(place_ref, w_ref, *outs):
+        for k in range(n):
+            dest = shifted(place_ref, k, n)
+            for p in range(parts):
+                outs[k][:, p * width : (p + 1) * width] = w_ref[:, lanes_at(p * n + dest, width)]
+
+    piece = jax.ShapeDtypeStruct((rows, parts * width), weight.dtype)
+    return place_call(kernel, place, [weight], [piece] * n)
+
+
+def cut_rows(v, place, n):
+    rows = v.shape[0] // n
+
+    def kernel(place_ref, v_ref, *outs):
+        for k in range(n):
+            outs[k][...] = v_ref[lanes_at(shifted(place_ref, k, n), rows), :]
+
+    piece = jax.ShapeDtypeStruct((rows, v.shape[1]), v.dtype)
+    return place_call(kernel, place, [v], [piece] * n)
+
+
+def join_rows(pieces, place, n):
+    rows, width = pieces[0].shape
+
+    def kernel(place_ref, *refs):
+        for k in range(n):
+            refs[n][lanes_at(shifted(place_ref, -k, n), rows), :] = refs[k][...]
+
+    whole = jax.ShapeDtypeStruct((n * rows, width), pieces[0].dtype)
+    return place_call(kernel, place, pieces, [whole])[0]
+
+
+def join_columns(lists, parts, place, dtype):
+    n = len(lists[0])
+    rows, width = lists[0][0].shape[0], lists[0][0].shape[1] // parts
+
+    def kernel(place_ref, *refs):
+        for i in range(len(lists)):
+            for k in range(n):
+                source = shifted(place_ref, -k, n)
+                for p in range(parts):
+                    cut = refs[i * n + k][:, p * width : (p + 1) * width]
+                    here = lanes_at((i * parts + p) * n + source, width)
+                    refs[-1][:, here] = cut.astype(dtype)
+
+    whole = jax.ShapeDtypeStruct((rows, len(lists) * parts * n * width), dtype)
+    return place_call(kernel, place, [v for one in lists for v in one], [whole])[0]
+
+
+def send_one(pieces, k, *ties):
+    n = len(pieces)
+    return lax.ppermute(after(pieces[k], *ties), "ctx", [(i, (i + k) % n) for i in range(n)])
+
+
+def send_on(pieces):
+    got = [pieces[0]]
+    for k in range(1, len(pieces)):
+        got.append(send_one(pieces, k, *got[max(k - 4, 0) : max(k - 3, 0)]))
+    return got
+
+
+def send_columns(weight, parts):
     n = lax.axis_size("ctx")
-    place = lax.axis_index("ctx")
     rows = weight.shape[0]
     width = weight.shape[1] // parts // n
     if n <= 8:
-
-        def piece(dest):
-            return jnp.concatenate(
-                [
-                    lax.dynamic_slice_in_dim(weight, (p * n + dest) * width, width, 1)
-                    for p in range(parts)
-                ],
-                axis=1,
-            )
-
-        held = jnp.zeros((n, rows, parts * width), weight.dtype)
-        for k in range(n):
-            got = piece((place + k) % n)
-            if k:
-                got = lax.ppermute(got, "ctx", [(i, (i + k) % n) for i in range(n)])
-            held = lax.dynamic_update_slice_in_dim(held, got[None], (place - k) % n, 0)
-    else:
-        cut = weight.reshape(rows, parts, n, width).transpose(2, 0, 1, 3)
-        held = lax.all_to_all(cut.reshape(n, rows, parts * width), "ctx", 0, 0, tiled=True)
-    full = lax.all_gather(held.reshape(n * rows, parts * width), "fsdp", axis=0, tiled=True)
-    return full
-
-
-def to_rows(gradient, parts):
+        return send_on(cut_columns(weight, parts, lax.axis_index("ctx"), n))
+    cut = weight.reshape(rows, parts, n, width).transpose(2, 0, 1, 3)
+    return [lax.all_to_all(cut.reshape(n, rows, parts * width), "ctx", 0, 0, tiled=True)]
+
+
+def take_columns(sent):
+    if len(sent) == 1:
+        return sent[0].reshape(-1, sent[0].shape[-1])
+    return join_rows(sent, lax.axis_index("ctx"), len(sent))
+
+
+def send_rows(mine):
     n = lax.axis_size("ctx")
-    place = lax.axis_index("ctx")
-    mine = lax.psum_scatter(gradient.astype(BF16), "fsdp", scatter_dimension=0, tiled=True)
-    rows = mine.shape[0] // n
-    width = mine.shape[1] // parts
     if n <= 8:
-        out = jnp.zeros((rows, parts * n * width), F32)
-        for k in range(n):
-            got = lax.dynamic_slice_in_dim(mine, (place + k) % n * rows, rows, 0)
-            if k:
-                got = lax.ppermute(got, "ctx", [(i, (i + k) % n) for i in range(n)])
-            got = got.astype(F32)
-            source = (place - k) % n
-            for p in range(parts):
-                out = lax.dynamic_update_slice_in_dim(
-                    out, got[:, p * width : (p + 1) * width], (p * n + source) * width, 1
-                )
-        return out
-    got = lax.all_to_all(mine.reshape(n, rows, parts * width), "ctx", 0, 0, tiled=True)
-    got = got.reshape(n, rows, parts, width).transpose(1, 2, 0, 3)
-    return got.reshape(rows, parts * n * width).astype(F32)
-
-
-def share_rows(gradient):
-    mine = lax.psum_scatter(gradient.astype(BF16), "fsdp", scatter_dimension=0, tiled=True)
-    return mine.astype(F32)
+        return send_on(cut_rows(mine, lax.axis_index("ctx"), n))
+    return [lax.all_to_all(mine.reshape(n, -1, mine.shape[1]), "ctx", 0, 0, tiled=True)]
+
+
+def take_rows(lists, parts):
+    if len(lists[0]) > 1:
+        return join_columns(lists, parts, lax.axis_index("ctx"), F32)
+    wholes = []
+    for (sent,) in lists:
+        n, rows = sent.shape[:2]
+        got = sent.reshape(n, rows, parts, -1).transpose(1, 2, 0, 3)
+        wholes.append(got.reshape(rows, -1).astype(F32))
+    return jnp.concatenate(wholes, axis=1)
+
+
+def gather_groups(v):
+    return lax.all_gather(v, "fsdp", axis=0, tiled=True)
+
+
+def scatter_groups(v):
+    return lax.psum_scatter(v, "fsdp", scatter_dimension=0, tiled=True)
+
+
+def far(v):
+    return lax.ppermute(v, "fsdp", [(i, i ^ 2) for i in range(4)])
+
+
+def near(v):
+    return lax.ppermute(v, "fsdp", [(i, i ^ 1) for i in range(4)])
+
+
+def in_order(held):
+    me = lax.axis_index("fsdp")
+    out = jnp.zeros((4,) + held[0].shape, held[0].dtype)
+    for k, h in enumerate(held):
+        out = lax.dynamic_update_slice_in_dim(out, h[None], me ^ k, 0)
+    return out.reshape(4 * held[0].shape[0], held[0].shape[1])
+
+
+def cut_groups(v):
+    me = lax.axis_index("fsdp")
+    rows = v.shape[0] // 4
+    return [lax.dynamic_slice_in_dim(v, (me ^ k) * rows, rows, 0) for k in range(4)]
+
+
+def add_low(got, own):
+    return (got.astype(F32) + own.astype(F32)).astype(BF16)
 
 
 def weight_share(gradient, shard_rows):
@@ -178,16 +464,14 @@
     return lax.psum_scatter(partial_rows, "fsdp", scatter_dimension=0, tiled=True).astype(F32)
 
 
-def spread_columns(v):
-    n, m = lax.axis_size("ctx"), lax.axis_size("fsdp")
-    rows = v.shape[0]
-    return v.reshape(rows, n, m, D // (n * m)).transpose(0, 2, 1, 3).reshape(rows, D)
-
-
-def unspread_columns(v):
-    n, m = lax.axis_size("ctx"), lax.axis_size("fsdp")
-    rows = v.shape[0]
-    return v.reshape(rows, m, n, D // (n * m)).transpose(0, 2, 1, 3).reshape(rows, D)
+def spread_lanes(v, n, m):
+    w = D // (n * m)
+    cuts = [v[:, (c * m + f) * w : (c * m + f + 1) * w] for f in range(m) for c in range(n)]
+    return jnp.concatenate(cuts, axis=1)
+
+
+def unspread_lanes(v, n, m):
+    return spread_lanes(v, m, n)
 
 
 def sum_all(v):
@@ -339,41 +623,46 @@
         (((1,), (0,)), ((), ())),
         preferred_element_type=F32,
     )
-    hc_ref[0:8, :] = both[0:8] + both[8:16]
-    hc_ref[8:16, :] = jnp.zeros((8, D), F32)
-    hc_ref[8:9, 0:LANES] = stat_ref[0:1, :]
-
-
-def first_kernel(s_ref, w_ref, static_ref, u_ref, aux_ref):
+    hc_ref[...] = both[0:8] + both[8:16]
+    hc_ref[6:7, 0:LANES] = stat_ref[0:1, :]
+
+
+def sum_of(refs):
+    return sum(ref[...].astype(F32) for ref in refs)
+
+
+def first_kernel(order, s_ref, w_ref, static_ref, u_ref, aux_ref):
     aux, _, u = enter(stream_parts(s_ref), w_ref[...], static_ref[0:1, :])
-    u_ref[...] = u.astype(BF16)
+    u = u.astype(BF16)
+    u_ref[...] = spread_lanes(u, *order) if order else u
     aux_ref[...] = aux
 
 
-def middle_kernel(s_ref, c_ref, y_ref, aux0_ref, w_ref, static_ref, u_ref, dy_ref, aux_ref):
+def middle_kernel(order, s_ref, c_ref, y_ref, aux0_ref, w_ref, static_ref, u_ref, dy_ref, aux_ref):
     coef0 = static_ref[0:1, :] + jnp.tanh(aux0_ref[...])
     mid = mixed(stream_parts(s_ref), coef0, y_ref[...])
     aux, coef, u = enter(mid, w_ref[...], static_ref[1:2, :])
-    u_ref[...] = u.astype(BF16)
+    u_ref[...] = spread_lanes(u.astype(BF16), *order)
     aux_ref[...] = aux
     dy_ref[...] = branch_grad(stream_parts(c_ref), coef).astype(BF16)
 
 
 def out_kernel(
-    s_ref, c_ref, y_ref, y2_ref, aux0_ref, aux1_ref, static_ref, out_ref, red_ref
+    s_ref, c_ref, y_ref, y2a_ref, y2b_ref, y2c_ref, aux0_ref, aux1_ref, static_ref,
+    out_ref, red_ref,
 ):
     coef0 = static_ref[0:1, :] + jnp.tanh(aux0_ref[...])
     coef1 = static_ref[1:2, :] + jnp.tanh(aux1_ref[...])
     mid = mixed(stream_parts(s_ref), coef0, y_ref[...])
-    y2 = y2_ref[...]
+    y2 = sum_of((y2a_ref, y2b_ref, y2c_ref))
     for j, total in enumerate(mixed(mid, coef1, y2)):
         out_ref[:, j * D : (j + 1) * D] = total.astype(BF16)
     red_ref[...] = leave_grads(mid, stream_parts(c_ref), y2)
 
 
 def back_kernel(
-    s_ref, c_ref, y_ref, du_ref, red_ref, aux0_ref, aux1_ref, w_ref, static_ref,
-    dmid_ref, dy_ref, hc_ref, normed_ref, dz_ref, stat_ref,
+    order, s_ref, c_ref, y_ref, dua_ref, dub_ref, duc_ref, red_ref, aux0_ref, aux1_ref, w_ref,
+    static_ref, dmid_ref, dy_ref, hc_ref, normed_ref, dz_ref, stat_ref,
 ):
     step = pl.program_id(0)
 
@@ -385,8 +674,9 @@
     aux1 = aux1_ref[...]
     coef1 = static_ref[1:2, :] + jnp.tanh(aux1)
     mid = mixed(stream_parts(s_ref), coef0, y_ref[...])
+    du = unspread_lanes(sum_of((dua_ref, dub_ref, duc_ref)), *order)
     dmid = enter_back(
-        mid, stream_parts(c_ref), aux1, coef1, red_ref[...], du_ref[...], w_ref[...],
+        mid, stream_parts(c_ref), aux1, coef1, red_ref[...], du, w_ref[...],
         normed_ref, dz_ref, stat_ref, step,
     )
     for j in range(STREAMS):
@@ -398,10 +688,15 @@
         finish_hc(normed_ref, dz_ref, stat_ref, hc_ref)
 
 
+def red_kernel(s_ref, dmid_ref, y_ref, red_ref):
+    red_ref[...] = leave_grads(stream_parts(s_ref), stream_parts(dmid_ref), y_ref[...])
+
+
 def last_kernel(
-    s_ref, dmid_ref, y_ref, du_ref, aux0_ref, w_ref, static_ref,
-    ds_ref, hc_ref, normed_ref, dz_ref, stat_ref,
+    order, s_ref, dmid_ref, *refs
 ):
+    du_refs = refs[:-9]
+    red_ref, aux0_ref, w_ref, static_ref, ds_ref, hc_ref, normed_ref, dz_ref, stat_ref = refs[-9:]
     step = pl.program_id(0)
 
     @pl.when(step == 0)
@@ -411,9 +706,11 @@
     aux0 = aux0_ref[...]
     coef0 = static_ref[0:1, :] + jnp.tanh(aux0)
     parts, grads = stream_parts(s_ref), stream_parts(dmid_ref)
-    red = leave_grads(parts, grads, y_ref[...])
+    du = sum_of(du_refs)
+    if order:
+        du = unspread_lanes(du, *order)
     ds = enter_back(
-        parts, grads, aux0, coef0, red, du_ref[...], w_ref[...],
+        parts, grads, aux0, coef0, red_ref[...], du, w_ref[...],
         normed_ref, dz_ref, stat_ref, step,
     )
     for j in range(STREAMS):
@@ -438,8 +735,8 @@
     out_shape = [jax.ShapeDtypeStruct((rows, columns), dtype) for columns, dtype in outs]
     scratch = []
     if hc:
-        out_specs.append(whole((16, D)))
-        out_shape.append(jax.ShapeDtypeStruct((16, D), F32))
+        out_specs.append(whole((8, D)))
+        out_shape.append(jax.ShapeDtypeStruct((8, D), F32))
         scratch = [
             pltpu.VMEM((STREAMS * rows, D), BF16),
             pltpu.VMEM((rows, LANES), F32),
@@ -452,7 +749,8 @@
         out_specs=out_specs,
         out_shape=out_shape,
         scratch_shapes=scratch,
-        compiler_params=pltpu.CompilerParams(vmem_limit_bytes=40 * MIB),
+        cost_estimate=cost([a for a, _ in ins], out_shape, 100 * rows * STREAMS * D),
+        compiler_params=pltpu.CompilerParams(vmem_limit_bytes=60 * MIB),
     )(*[a for a, _ in ins])
 
 
@@ -556,7 +854,8 @@
         in_specs=[by_query, of(1), of(2)] + shared,
         out_specs=[by_query, by_query, by_query, by_head, by_head],
         out_shape=[low, wide, low, low, low],
-        compiler_params=pltpu.CompilerParams(vmem_limit_bytes=40 * MIB),
+        cost_estimate=cost([qkv], [low] * 4, 4 * heads * total**2 * HEAD_DIM, heads * total**2),
+        compiler_params=room(20 * Q_ROWS * total, 40 * total * HEAD_DIM),
     )(qkv, qkv, qkv, *marks)
 
 
@@ -571,7 +870,8 @@
         out_specs=[by_query, by_head, by_head],
         out_shape=[low, low, low],
         scratch_shapes=[pltpu.VMEM((total, HEAD_DIM), F32)] * 2,
-        compiler_params=pltpu.CompilerParams(vmem_limit_bytes=40 * MIB),
+        cost_estimate=cost([lse], [low] * 7, 10 * heads * total**2 * HEAD_DIM, heads * total**2),
+        compiler_params=room(32 * Q_ROWS * total, 48 * total * HEAD_DIM),
     )(query, keys, values, d_out, lse, *marks)
 
 
@@ -586,51 +886,127 @@
 class HeadAttention:
     def __init__(self, rows, w_qkv, w_out, pair_row, length_row):
         n = lax.axis_size("ctx")
-        self.place = lax.axis_index("ctx")
+        self.group = lax.axis_index("fsdp")
         self.rows, self.heads = rows, HEADS // n
-        self.owners = ring_owners(n, self.place)
-        position, _, start = places(pair_row, length_row, rows, self.owners)
+        owners = ring_owners(n, lax.axis_index("ctx"))
+        position, _, start = places(pair_row, length_row, rows, owners)
         cosine, sine = angles(position - start)
         kpos = jnp.broadcast_to(position[None, :], (8, position.shape[0]))
         self.marks = (cosine, sine, position[:, None], start[:, None], kpos)
-        self.qkv_cols = to_columns(w_qkv, 3)
-        self.out_all = lax.all_gather(w_out, ("ctx", "fsdp"), axis=0, tiled=True)
+        self.sent_qkv = send_columns(w_qkv, 3)
+        self.w_out = w_out
 
     def to_tokens(self, heads_out):
         n = lax.axis_size("ctx")
         order, offsets = ring_order(n), ring_offsets(n)
-        width = heads_out.shape[1]
-        mine = jnp.zeros((self.rows, n * width), heads_out.dtype)
-        for at, offset in enumerate(offsets):
-            got = heads_out[at * self.rows : (at + 1) * self.rows]
-            back = -offset if offset != -(n // 2) else offset
-            if offset:
-                pairs = [(order[i], order[(i + offset) % n]) for i in range(n)]
-                got = lax.ppermute(got, "ctx", pairs)
-            source = self.owners[offsets.index(back)]
-            mine = lax.dynamic_update_slice_in_dim(mine, got, source * width, 1)
-        return mine
-
-    def forward(self, u):
-        self.u_all = ring_gather(spread_columns(u))
-        qkv = jnp.dot(self.u_all, self.qkv_cols, preferred_element_type=F32)
+        got = []
+        for offset in offsets:
+            at = offsets.index(-offset if 2 * offset != -n else offset)
+            own = heads_out[at * self.rows : (at + 1) * self.rows]
+            pairs = [(order[i], order[(i - offset) % n]) for i in range(n)]
+            got.append(lax.ppermute(own, "ctx", pairs) if offset else own)
+        return got
+
+    def join_tokens(self, got):
+        n, m = lax.axis_size("ctx"), lax.axis_size("fsdp")
+        offsets, width = ring_offsets(n), got[0].shape[1]
+
+        def kernel(place_ref, *refs):
+            place = place_ref[0]
+            mine = jnp.where(place % 2 == 0, place // 2, n - 1 - place // 2)
+            held = refs[-1]
+            for k, offset in enumerate(offsets):
+                at = lax.rem(mine + offset + n, n)
+                owner = jnp.where(at < n // 2, 2 * at, 2 * (n - 1 - at) + 1)
+                held[:, lanes_at(owner, width)] = refs[k][...]
+            refs[n][...] = spread_lanes(held[...], n, m)
+
+        whole = jax.ShapeDtypeStruct((self.rows, n * width), got[0].dtype)
+        scratch = [pltpu.VMEM(whole.shape, whole.dtype)]
+        return place_call(kernel, lax.axis_index("ctx"), got, [whole], scratch)[0]
+
+    def forward(self, u, w_gate_up, w_down):
+        n, m = lax.axis_size("ctx"), lax.axis_size("fsdp")
+        got = {}
+
+        out_ctx = lax.all_gather(self.w_out, "ctx", axis=0, tiled=True)
+        u, sent_qkv = lax.optimization_barrier((u, self.sent_qkv))
+
+        def early(step, arrived):
+            if step == 0:
+                got["own"] = take_columns(sent_qkv)
+                got["far"] = far(got["own"])
+            if step == 1:
+                arrived, got["far"] = lax.optimization_barrier((arrived, got["far"]))
+                got["near"] = [near(got["own"]), near(got["far"])]
+            if step == 2:
+                arrived, got["near"], got["out"] = lax.optimization_barrier(
+                    (arrived, got["near"], out_ctx)
+                )
+                held = [got["own"], got["near"][0], got["far"], got["near"][1]]
+                got["cols"] = in_order(held)
+            if step == 3:
+                arrived, got["cols"] = lax.optimization_barrier((arrived, got["cols"]))
+            return arrived
+
+        blocks = ring_gather(u, early)
+        self.qkv_cols = got["cols"]
+        out_all = lax.all_gather(got["out"], "fsdp", axis=0, tiled=True)
+        down_rows = gather_groups(after(w_down, *blocks))
+        cut = cut_columns(after(w_gate_up, *blocks), 2, lax.axis_index("ctx"), n)
+        self.u_all, qkv = joined_dot(blocks, self.qkv_cols)
+        sent = [cut[0]] + [send_one(cut, k) for k in range(1, 4)]
         self.o, self.lse, self.q, self.k, self.v = attend(qkv, self.heads, self.marks)
-        return jnp.dot(self.to_tokens(self.o), self.out_all, preferred_element_type=F32)
-
-    def backward(self, dy):
-        dy_all = ring_gather(dy)
-        width = self.heads * HEAD_DIM
-        out_rows = lax.dynamic_slice_in_dim(self.out_all, self.place * width, width, 0)
-        d_out = jnp.einsum("td,ed->te", dy_all, out_rows, preferred_element_type=F32).astype(BF16)
-        grad_out = jnp.einsum("te,td->ed", self.o, dy_all, preferred_element_type=F32)
+        o, *sent = lax.optimization_barrier((self.o, *sent))
+        sent_o = self.to_tokens(o)
+        sent += [send_one(cut, k, o) for k in range(4, n)]
+        held = out_all.reshape(m, n, -1, D)
+        held = lax.dynamic_slice_in_dim(held, lax.axis_index("ctx"), 1, 1)
+        self.out_rows = held.reshape(-1, D)
+        y = jnp.dot(self.join_tokens(sent_o), out_all, preferred_element_type=F32)
+        y, *sent[:6] = lax.optimization_barrier((y, *sent[:6]))
+        return (y, sent, down_rows)
+
+    def backward(self, dy, grad_gate, grad_up):
+        got = {}
+
+        def early_dy(step, arrived):
+            if step == 2:
+                arrived, got["gate"] = lax.optimization_barrier((arrived, grad_gate))
+            return arrived
+
+        blocks = ring_gather(dy, early_dy)
+        dy_all, d_out = joined_dot(blocks, self.out_rows, nt=True, dtype=BF16)
+        sent_gate = send_rows(after(got["gate"], dy_all))
+        d_out, grad_up = lax.optimization_barrier((d_out, grad_up))
         dq, dk, dv = attend_back(self.q, self.k, self.v, d_out, self.lse, self.heads, self.marks)
         d_qkv = jnp.concatenate([dq, dk, dv], axis=1)
         partial = jnp.einsum(
             "tc,dc->td", d_qkv, self.qkv_cols, preferred_element_type=F32
         ).astype(BF16)
-        grad_qkv = jnp.einsum("td,tc->dc", self.u_all, d_qkv, preferred_element_type=F32)
-        du = unspread_columns(ring_scatter(partial, self.rows))
-        return (du, to_rows(grad_qkv, 3), share_rows(grad_out))
+
+
+        def early(step, arrived):
+            if step == 0:
+                u_all = after(self.u_all, partial)
+                g = jnp.einsum("td,tc->dc", u_all, d_qkv, preferred_element_type=F32)
+                got["qkv"] = scatter_groups(g.astype(BF16))
+            if step == 1:
+                o, dy_now = after([self.o, dy_all], arrived)
+                g = jnp.einsum("te,td->ed", o, dy_now, preferred_element_type=F32)
+                got["out"] = scatter_groups(g.astype(BF16)).astype(F32)
+            return arrived
+
+        du = ring_scatter(partial, self.rows, early)
+        du, sent_gate = lax.optimization_barrier((du, sent_gate))
+        sent_up = send_rows(after(grad_up, du[1]))
+        sent_qkv = send_rows(after(got["qkv"], du[1]))
+        return (
+            du,
+            lambda tie: take_rows([after(sent_qkv, tie)], 3),
+            got["out"],
+            take_rows([sent_gate, sent_up], 1),
+        )
 
 
 def rotate(v, inside, sign):
@@ -667,7 +1043,7 @@
         scores = jnp.einsum("qhe,hke->hqk", self.q, self.k, preferred_element_type=F32) * SCALE
         return jnp.where(self.keep[None], scores, -1e30)
 
-    def forward(self, u):
+    def forward(self, u, w_gate_up, w_down):
         rows, shape = self.rows, (self.rows, HEADS, HEAD_DIM)
         self.u = u
         qkv = jnp.dot(u, self.gathered(self.w_qkv), preferred_element_type=F32)
@@ -682,9 +1058,10 @@
         probs = jnp.exp(scores - self.lse).astype(BF16)
         attended = jnp.einsum("hqk,hke->qhe", probs, self.v, preferred_element_type=F32)
         self.o = attended.reshape(rows, D).astype(BF16)
-        return jnp.dot(self.o, self.gathered(self.w_out), preferred_element_type=F32)
-
-    def backward(self, dy):
+        y = jnp.dot(self.o, self.gathered(self.w_out), preferred_element_type=F32)
+        return (y, send_columns(w_gate_up, 2), gather_groups(w_down))
+
+    def backward(self, dy, grad_gate, grad_up):
         rows = self.rows
         d_out = jnp.einsum(
             "td,ed->te", dy, self.gathered(self.w_out), preferred_element_type=F32
@@ -716,10 +1093,12 @@
         ).astype(BF16)
         du = jnp.einsum("tc,dc->td", d_qkv, self.gathered(self.w_qkv), preferred_element_type=F32)
         grad_qkv = jnp.einsum("td,tc->dc", self.u, d_qkv, preferred_element_type=F32)
+        grad_qkv = weight_share(grad_qkv, self.w_qkv.shape[0])
         return (
-            du,
-            weight_share(grad_qkv, self.w_qkv.shape[0]),
+            (du,),
+            lambda tie: grad_qkv,
             weight_share(grad_out, self.w_out.shape[0]),
+            take_rows([send_rows(g) for g in (grad_gate, grad_up)], 1),
         )
 
 
@@ -745,78 +1124,125 @@
     static = jnp.pad(hc_static, ((0, 0), (0, 0), (0, 2))).reshape(2, 8 * STREAMS)
     static = jnp.pad(static, ((0, 6), (0, LANES - 8 * STREAMS)))
 
-    plan = HeadAttention if HEADS % n == 0 else TokenAttention
+    by_heads = HEADS % n == 0 and n % 2 == 0 and n > 2 and lax.axis_size("fsdp") == 4
+    plan = HeadAttention if by_heads else TokenAttention
     attention = plan(rows, w_qkv, w_out, pair_row, length_row)
+    order = (n, lax.axis_size("fsdp"))
+    own_order = order if by_heads else None
     u, aux0 = row_call(
-        first_kernel,
+        functools.partial(first_kernel, own_order),
         rows,
         [(state, True), (wpack0, False), (static, False)],
         [(D, BF16), (LANES, F32)],
     )
-    gate_up_cols = to_columns(w_gate_up, 2)
-    down_rows = lax.all_gather(w_down, "fsdp", axis=0, tiled=True)
-    y = attention.forward(u)
+    y, sent_gate_up, down_rows = attention.forward(u, w_gate_up, w_down)
     u2, dy2, aux1 = row_call(
-        middle_kernel,
+        functools.partial(middle_kernel, order),
         rows,
         [(state, True), (cot, True), (y, True), (aux0, True), (wpack1, False), (static, False)],
         [(D, BF16), (D, BF16), (LANES, F32)],
     )
-    u2_all = ring_gather(spread_columns(u2))
-    dy2_all = ring_gather(dy2)
+    got = {}
+
+    def early_u2(step, arrived):
+        if step == 0:
+            got["own"] = take_columns(sent_gate_up)
+            arrived, got["own"], got["down"] = lax.optimization_barrier(
+                (arrived, got["own"], down_rows)
+            )
+        return arrived
+
+    u2_blocks = ring_gather(u2, early_u2)
+    gate_up_cols, down_rows = gather_groups(got["own"]), got["down"]
     width = FF // n
-    gate_up = jnp.dot(u2_all, gate_up_cols, preferred_element_type=F32)
-    gate, up = gate_up[:, :width], gate_up[:, width:]
-    hidden = (jax.nn.silu(gate) * up).astype(BF16)
+    u2_all, gate, up, hidden = ffn_enter(u2_blocks, gate_up_cols)
+
+    def early_dy2(step, arrived):
+        return after(arrived, gate) if step == 2 else arrived
+
+    dy2_blocks = ring_gather(after(dy2, *u2_blocks[-2:]), early_dy2)
     y2_partial = jnp.dot(hidden, down_rows, preferred_element_type=F32).astype(BF16)
-    y2 = ring_scatter(y2_partial, rows)
-    d_hidden = jnp.einsum("td,fd->tf", dy2_all, down_rows, preferred_element_type=F32)
-    d_hidden = lax.reduce_precision(d_hidden, 8, 7)
-    grad_down = share_rows(
-        jnp.einsum("tf,td->fd", hidden, dy2_all, preferred_element_type=F32)
-    )
-    open_gate = jax.nn.sigmoid(gate)
-    d_up = d_hidden * gate * open_gate
-    d_gate = d_hidden * up * open_gate * (1.0 + gate * (1.0 - open_gate))
-    dgu = jnp.concatenate([d_gate, d_up], axis=1).astype(BF16)
-    du2_partial = jnp.einsum("tg,dg->td", dgu, gate_up_cols, preferred_element_type=F32)
-    du2 = unspread_columns(ring_scatter(du2_partial.astype(BF16), rows))
-    grad_gate_up = to_rows(
-        jnp.einsum("td,tg->dg", u2_all, dgu, preferred_element_type=F32), 2
-    )
-    out, red1 = row_call(
-        out_kernel,
+    y2_partial, dy2_blocks = lax.optimization_barrier((y2_partial, dy2_blocks))
+
+    def early_y2(step, arrived):
+        if step == 0:
+            got["dy2_all"], got["d_gate"], got["d_up"] = ffn_back(
+                after(dy2_blocks, arrived), down_rows, gate, up
+            )
+        if step == 1:
+            d_gate, d_up = after([got["d_gate"], got["d_up"]], arrived)
+            got["du2"] = ffn_leave(d_gate, d_up, gate_up_cols)
+        return arrived
+
+    y2 = ring_scatter(y2_partial, rows, early_y2)
+    for name in ("gate", "up", "down"):
+        if name == "down":
+            left, right = hidden, got["dy2_all"]
+        else:
+            left, right = u2_all, got["d_" + name]
+        left = after(left, got["du2"], *[v for k, v in got.items() if k.startswith("grad_")])
+        g = jnp.einsum("td,tg->dg", left, right, preferred_element_type=F32)
+        got["grad_" + name] = g.astype(BF16)
+
+    def leave(terms):
+        return row_call(
+            out_kernel,
+            rows,
+            [
+                (state, True), (cot, True), (y, True), *[(v, True) for v in terms],
+                (aux0, True), (aux1, True), (static, False),
+            ],
+            [(STREAMS * D, BF16), (LANES, F32)],
+        )
+
+    def early_du2(step, arrived):
+        if step == 1:
+            arrived, y2_all = lax.optimization_barrier((arrived, tuple(y2)))
+            got["y2"] = y2_all
+        if step == 2:
+            arrived, got["grad_gate"], got["grad_up"] = lax.optimization_barrier(
+                (arrived, got["grad_gate"], got["grad_up"])
+            )
+            got["out"] = leave(got["y2"])
+        if step == 3:
+            arrived, got["out"], got["grad_down"] = lax.optimization_barrier(
+                (arrived, got["out"], got["grad_down"])
+            )
+        return arrived
+
+    du2 = ring_scatter(got["du2"], rows, early_du2)
+    if "out" not in got:
+        got["out"] = leave(y2)
+    out, red1 = got["out"]
+    grad_gate, grad_up = [scatter_groups(got[k]) for k in ("grad_gate", "grad_up")]
+    grad_down = scatter_groups(got["grad_down"]).astype(F32)
+    dmid, dy, hc1 = row_call(
+        functools.partial(back_kernel, order),
         rows,
         [
-            (state, True), (cot, True), (y, True), (y2, True), (aux0, True), (aux1, True),
-            (static, False),
-        ],
-        [(STREAMS * D, BF16), (LANES, F32)],
-    )
-    dmid, dy, hc1 = row_call(
-        back_kernel,
-        rows,
-        [
-            (state, True), (cot, True), (y, True), (du2, True), (red1, True), (aux0, True),
-            (aux1, True), (wpack1, False), (static, False),
+            (state, True), (cot, True), (y, True), *[(v, True) for v in du2], (red1, True),
+            (aux0, True), (aux1, True), (wpack1, False), (static, False),
         ],
         [(STREAMS * D, F32), (D, BF16)],
         hc=True,
     )
-    du, grad_qkv, grad_out = attention.backward(dy)
+    red0 = row_call(red_kernel, rows, [(state, True), (dmid, True), (y, True)], [(LANES, F32)])[0]
+    du, take_grad_qkv, grad_out, grad_gate_up = attention.backward(dy, grad_gate, grad_up)
+    du, grad_down = lax.optimization_barrier((du, grad_down))
     grad_state, hc0 = row_call(
-        last_kernel,
+        functools.partial(last_kernel, own_order),
         rows,
         [
-            (state, True), (dmid, True), (y, True), (du, True), (aux0, True), (wpack0, False),
-            (static, False),
+            (state, True), (dmid, True), *[(v, True) for v in du], (red0, True), (aux0, True),
+            (wpack0, False), (static, False),
         ],
         [(STREAMS * D, BF16)],
         hc=True,
     )
-    hc = jnp.stack([sum_all(hc0), sum_all(hc1)])
+    grad_qkv = take_grad_qkv(hc0)
+    hc = sum_all(jnp.concatenate([hc0, hc1], axis=0)).reshape(2, 8, D)
     grad_hc_weight = hc[:, 0:6].transpose(0, 2, 1)
-    grad_hc_static = hc[:, 8, : 8 * STREAMS].reshape(2, STREAMS, 8)[:, :, 0:6]
+    grad_hc_static = hc[:, 6, : 8 * STREAMS].reshape(2, STREAMS, 8)[:, :, 0:6]
     return (
         out[None],
         grad_state[None],

time: 802 us -> 714 us (0.89)
  the two profiles are of different devices: /device:TPU:11 before, /device:TPU:0 now
where the time goes in v2:
time: 714 us; the launch traced here: 704 us
  waiting for transfers between devices  253 us (35%)
  Pallas kernels  180 us (25%)
  starting transfers between devices  143 us (20%)
  matrix products  58.2 us (8%)
  local copies, waits for them, and re-layouts  41.8 us (6%)
  between operations  15.6 us (2%)
  other arithmetic  11.8 us (2%)
    ppermute x16, waiting for transfers between devices, ring_gather(): lax.ppermute(moving[1], 'ctx', back)  91.9 us
    ppermute x35, starting transfers between devices, send_one(): lax.ppermute(after(pieces[k], *ties), 'ctx', [(i, (i + k) % n) for i in r...  66.9 us
    ppermute x35, waiting for transfers between devices, send_one(): lax.ppermute(after(pieces[k], *ties), 'ctx', [(i, (i + k) % n) for i in r...  64.2 us
    pallas_call x6, Pallas kernels, row_call(): pl.pallas_call(kernel, grid=(rows // tile,), in_specs=in_specs, out_specs...  53 us
    ppermute x16, waiting for transfers between devices, ring_gather(): lax.ppermute(moving[0], 'ctx', ahead)  42.2 us
    dot_general x3, matrix products, on_device(): g = jnp.einsum('td,tg->dg', left, right, preferred_element_type=F32)  28 us
    ppermute x16, starting transfers between devices, ring_gather(): lax.ppermute(moving[1], 'ctx', back)  25.9 us
    pallas_call x10, Pallas kernels, place_call(): pl.pallas_call(kernel, in_specs=[pl.BlockSpec(memory_space=pltpu.SMEM)] +...  25.4 us
  transfers between devices with their start and end apart: 115, of which 54 were waited for; matrix products, arithmetic and copies ran while one was open for 13% of the time, Pallas kernels for 24%

profile of v2, /device:TPU:0, one launch (start us, length us, event | category | flops | bytes accessed | tf_op | source)
XLA Modules:
  0.0 704.1 jit_solution(16256348409496102845)
XLA Ops:
  10.1 4.0 collective-permute-start.3
  21.7 3.1 collective-permute-done.refs_1_
  26.0 8.3 %collective-permute-done.2.refs_3_ = bf16[64,768]{1,0:T(8,128)(2,1)S(1)} collective-permute-done((bf16[64,768]{1,0:T(8,128)(2,1)}, bf16[64,768]{1,0:T(8,128)(2,1)S(1)}, u32[]{:S(2)}, u32[]{:S(2)}) %collective-permute-start.2) | collective-permute-done | bytes 98336 | tf_op jit(solution)/shard_map/ppermute | solution.py:382
  34.4 6.8 collective-permute-start.6
  43.3 7.6 %shard_map.179 = (bf16[128,2048]{1,0:T(8,128)(2,1)}, f32[128,128]{1,0:T(8,128)}) custom-call(bf16[128,8192]{1,0:T(8,128)(2,1)} %bitcast.66, bf16[128,2048]{1,0:T(8,128)(2,1)} %pad_maximum_fusion.w_ref.refs_5_, f32[8,128]{1,0:T(8,128)} %pad.17.static_ref.refs_6_), custom_call_target="tpu_custom_call" | custom-call | flops 104857600 | bytes 3215360 | tf_op jit(solution)/shard_map/pallas_call | solution.py:745
  56.8 21.2 %collective-permute-done.8.refs_2_ = bf16[128,2048]{1,0:T(8,128)(2,1)S(1)} collective-permute-done((bf16[128,2048]{1,0:T(8,128)(2,1)}, bf16[128,2048]{1,0:T(8,128)(2,1)S(1)}, u32[]{:S(2)}, u32[]{:S(2)}) %collective-permute-start.8) | collective-permute-done | bytes 524320 | tf_op jit(solution)/shard_map/ppermute | solution.py:78
  80.0 11.5 %collective-permute-done.10.refs_4_ = bf16[128,2048]{1,0:T(8,128)(2,1)S(1)} collective-permute-done((bf16[128,2048]{1,0:T(8,128)(2,1)S(1)}, bf16[128,2048]{1,0:T(8,128)(2,1)S(1)}, u32[]{:S(2)}, u32[]{:S(2)}) %collective-permute-start.10) | collective-permute-done | bytes 524320 | tf_op jit(solution)/shard_map/ppermute | solution.py:78
  93.8 12.2 %collective-permute-done.12.refs_5_ = bf16[128,2048]{1,0:T(8,128)(2,1)S(1)} collective-permute-done((bf16[128,2048]{1,0:T(8,128)(2,1)S(1)}, bf16[128,2048]{1,0:T(8,128)(2,1)S(1)}, u32[]{:S(2)}, u32[]{:S(2)}) %collective-permute-start.12) | collective-permute-done | bytes 524320 | tf_op jit(solution)/shard_map/ppermute | solution.py:78
  128.1 3.0 shard_map.184
  135.1 8.0 %shard_map.182 = (bf16[1024,2048]{1,0:T(8,128)(2,1)}, f32[1024,768]{1,0:T(8,128)}) custom-call(bf16[128,2048]{1,0:T(8,128)(2,1)} %get-tuple-element.243.refs_0_, bf16[128,2048]{1,0:T(8,128)(2,1)} %copy-done.96, bf16[128,2048]{1,0:T(8,128)(2,1)} %copy-done.95, bf16[128,2048]{1,0:T(8,128)(2,1)} %copy-done.98, bf16[128,2048]{1,0:T(8,128)(2,1)} %copy-done.97, ...), custom_call_target="tpu_custom_call" | custom-call | flops 3221225472 | bytes 14680064 | tf_op jit(solution)/shard_map/pallas_call | solution.py:165
  143.8 11.1 %shard_map.183 = (bf16[1024,256]{1,0:T(8,128)(2,1)}, f32[1024,256]{1,0:T(8,128)}, bf16[1024,256]{1,0:T(8,128)(2,1)}, bf16[1024,256]{1,0:T(8,128)(2,1)}, bf16[1024,256]{1,0:T(8,128)(2,1)}) custom-call(f32[1024,768]{1,0:T(8,128)} %get-tuple-element.262.q_ref.k_ref.v_ref, f32[1024,768]{1,0:T(8,128)} %get-tuple-element.262.q_ref.k_ref.v_ref, ...), custom_call_target="tpu_custom_call" | custom-call | flops 1073741824 | bytes 5242880 | tf_op jit(solution)/shard_map/pallas_call | solution.py:851
  163.8 2.9 collective-permute-start.23
  176.9 6.0 fusion.13.y_ref
  183.0 6.4 collective-permute-done.28.refs_4_
  189.4 10.1 %shard_map.186 = (bf16[128,2048]{1,0:T(8,128)(2,1)}, bf16[128,2048]{1,0:T(8,128)(2,1)}, f32[128,128]{1,0:T(8,128)}) custom-call(bf16[128,8192]{1,0:T(8,128)(2,1)} %bitcast.67, bf16[128,8192]{1,0:T(8,128)(2,1)} %bitcast.73, f32[128,2048]{1,0:T(8,128)} %fusion.13.y_ref, f32[128,128]{1,0:T(8,128)} %get-tuple-element.280.aux0_ref.refs_4_, ...), custom_call_target="tpu_custom_call" | custom-call | flops 104857600 | bytes 6950912 | tf_op jit(solution)/shard_map/pallas_call | solution.py:745
  199.5 6.3 collective-permute-start.31
  205.7 3.0 collective-permute-start.32
  210.1 13.8 %collective-permute-done.32.refs_6_ = bf16[64,2048]{1,0:T(8,128)(2,1)S(1)} collective-permute-done((bf16[64,2048]{1,0:T(8,128)(2,1)S(1)}, bf16[64,2048]{1,0:T(8,128)(2,1)S(1)}, u32[]{:S(2)}, u32[]{:S(2)}) %collective-permute-start.32) | collective-permute-done | bytes 262176 | tf_op jit(solution)/shard_map/ppermute | solution.py:382
  224.0 3.9 collective-permute-done.33.refs_7_
  228.6 3.0 shard_map.187
  233.8 10.2 %collective-permute-done.34.refs_3_ = bf16[128,2048]{1,0:T(8,128)(2,1)S(1)} collective-permute-done((bf16[128,2048]{1,0:T(8,128)(2,1)S(1)}, bf16[128,2048]{1,0:T(8,128)(2,1)S(1)}, u32[]{:S(2)}, u32[]{:S(2)}) %collective-permute-start.34) | collective-permute-done | bytes 524320 | tf_op jit(solution)/shard_map/ppermute | solution.py:78
  246.0 9.8 %collective-permute-done.36.refs_5_ = bf16[128,2048]{1,0:T(8,128)(2,1)S(1)} collective-permute-done((bf16[128,2048]{1,0:T(8,128)(2,1)S(1)}, bf16[128,2048]{1,0:T(8,128)(2,1)S(1)}, u32[]{:S(2)}, u32[]{:S(2)}) %collective-permute-start.36) | collective-permute-done | bytes 524320 | tf_op jit(solution)/shard_map/ppermute | solution.py:78
  258.4 3.8 collective-permute-done.38.refs_7_
  266.3 9.9 %collective-permute-done.41.refs_2_ = bf16[128,2048]{1,0:T(8,128)(2,1)S(1)} collective-permute-done((bf16[128,2048]{1,0:T(8,128)(2,1)S(1)}, bf16[128,2048]{1,0:T(8,128)(2,1)S(1)}, u32[]{:S(2)}, u32[]{:S(2)}) %collective-permute-start.41) | collective-permute-done | bytes 524320 | tf_op jit(solution)/shard_map/ppermute | solution.py:78
  278.6 9.6 %collective-permute-done.43.refs_4_ = bf16[128,2048]{1,0:T(8,128)(2,1)S(1)} collective-permute-done((bf16[128,2048]{1,0:T(8,128)(2,1)S(1)}, bf16[128,2048]{1,0:T(8,128)(2,1)S(1)}, u32[]{:S(2)}, u32[]{:S(2)}) %collective-permute-start.43) | collective-permute-done | bytes 524320 | tf_op jit(solution)/shard_map/ppermute | solution.py:78
  291.7 14.1 %shard_map.188 = (bf16[1024,2048]{1,0:T(8,128)(2,1)}, f32[1024,1024]{1,0:T(8,128)}, f32[1024,1024]{1,0:T(8,128)}, bf16[1024,1024]{1,0:T(8,128)(2,1)}) custom-call(bf16[128,2048]{1,0:T(8,128)(2,1)} %get-tuple-element.281.refs_0_, bf16[128,2048]{1,0:T(8,128)(2,1)} %copy-done.100, bf16[128,2048]{1,0:T(8,128)(2,1)} %copy-done.99, bf16[128,2048]{1,0:T(8,128)(2,1)} %copy-done.101, ...), custom_call_target="tpu_custom_call" | custom-call | flops 8589934592 | bytes 27262976 | tf_op jit(solution)/shard_map/pallas_call | solution.py:224
  308.0 7.3 %convolution_convert_fusion.4.one_own.other_own.y2a_ref = bf16[1024,2048]{1,0:T(8,128)(2,1)S(1)} fusion(bf16[1024,1024]{1,0:T(8,128)(2,1)} %get-tuple-element.352, bf16[1024,2048]{1,0:T(8,128)(2,1)} %all-gather.9.cloned.1.call-done.refs_9_), kind=kOutput, calls=%fused_computation.4 | convolution fusion | flops 4297064448 | bytes 10485760 | tf_op jit(solution)/shard_map/dot_general | solution.py:1164
  319.4 5.9 collective-permute-done.49.other_ref
  332.1 11.5 %shard_map.189 = (bf16[1024,2048]{1,0:T(8,128)(2,1)}, bf16[1024,1024]{1,0:T(8,128)(2,1)}, bf16[1024,1024]{1,0:T(8,128)(2,1)}) custom-call(bf16[128,2048]{1,0:T(8,128)(2,1)} %get-tuple-element.313.refs_0_, bf16[128,2048]{1,0:T(8,128)(2,1)} %copy-done.10, bf16[128,2048]{1,0:T(8,128)(2,1)} %copy-done.9, bf16[128,2048]{1,0:T(8,128)(2,1)} %copy-done.14, ...), custom_call_target="tpu_custom_call" | custom-call | flops 4294967296 | bytes 25165824 | tf_op jit(solution)/shard_map/pallas_call | solution.py:255
  349.1 14.2 %shard_map.191.one_own.other_own.dua_ref = bf16[1024,2048]{1,0:T(8,128)(2,1)} custom-call(bf16[1024,1024]{1,0:T(8,128)(2,1)} %get-tuple-element.327.g_ref, bf16[1024,1024]{1,0:T(8,128)(2,1)} %get-tuple-element.328.u_ref, bf16[2048,2048]{1,0:T(8,128)(2,1)} %all-gather.11.cloned.1.call-done.refs_9_.refs_10_.w_ref), custom_call_target="tpu_custom_call" | custom-call | flops 8589934592 | bytes 16777216 | tf_op jit(solution)/shard_map/pallas_call | solution.py:278
  366.5 4.3 collective-permute-done.53.other_ref
  383.8 9.4 %convolution_convert_fusion.3 = bf16[2048,1024]{1,0:T(8,128)(2,1)} fusion(bf16[1024,2048]{1,0:T(8,128)(2,1)} %get-tuple-element.341, bf16[1024,1024]{1,0:T(8,128)(2,1)} %get-tuple-element.327.g_ref), kind=kOutput, calls=%fused_computation.3 | convolution fusion | flops 4297064448 | bytes 10485760 | tf_op jit(solution)/shard_map/td,tg->dg/dot_general | solution.py:1184
  393.2 3.7 collective-permute-done.58.y2b_ref
  397.0 3.0 shard_map.195
  402.1 9.4 %convolution_convert_fusion.2 = bf16[2048,1024]{1,0:T(8,128)(2,1)} fusion(bf16[1024,2048]{1,0:T(8,128)(2,1)} %get-tuple-element.341, bf16[1024,1024]{1,0:T(8,128)(2,1)} %get-tuple-element.328.u_ref), kind=kOutput, calls=%fused_computation.2 | convolution fusion | flops 4297064448 | bytes 10485760 | tf_op jit(solution)/shard_map/td,tg->dg/dot_general | solution.py:1184
  417.3 9.3 %convolution_convert_fusion.1 = bf16[1024,2048]{1,0:T(8,128)(2,1)} fusion(bf16[1024,1024]{1,0:T(8,128)(2,1)S(1)} %copy-done.118, bf16[1024,2048]{1,0:T(8,128)(2,1)} %get-tuple-element.353), kind=kOutput, calls=%fused_computation.1 | convolution fusion | flops 4297064448 | bytes 10485760 | tf_op jit(solution)/shard_map/td,tg->dg/dot_general | solution.py:1184
  426.5 7.9 %shard_map.197 = (bf16[128,8192]{1,0:T(8,128)(2,1)}, f32[128,128]{1,0:T(8,128)}) custom-call(bf16[128,8192]{1,0:T(8,128)(2,1)} %bitcast.68, bf16[128,8192]{1,0:T(8,128)(2,1)} %bitcast.74, f32[128,2048]{1,0:T(8,128)} %fusion.13.y_ref, bf16[1024,2048]{1,0:T(8,128)(2,1)} %copy-done.2, bf16[128,2048]{1,0:T(8,128)(2,1)} %copy-done.15, ...), custom_call_target="tpu_custom_call" | custom-call | flops 104857600 | bytes 12783616 | tf_op jit(solution)/shard_map/pallas_call | solution.py:745
  435.4 12.1 %shard_map.198 = (f32[128,8192]{1,0:T(8,128)}, bf16[128,2048]{1,0:T(8,128)(2,1)}, f32[8,2048]{1,0:T(8,128)}) custom-call(bf16[128,8192]{1,0:T(8,128)(2,1)} %bitcast.69, bf16[128,8192]{1,0:T(8,128)(2,1)} %bitcast.75, f32[128,2048]{1,0:T(8,128)} %fusion.13.y_ref, bf16[1024,2048]{1,0:T(8,128)(2,1)} %shard_map.191.one_own.other_own.dua_ref, ...), custom_call_target="tpu_custom_call" | custom-call | flops 104857600 | bytes 15994880 | tf_op jit(solution)/shard_map/pallas_call | solution.py:745
  449.6 11.6 %collective-permute-done.65.refs_2_ = bf16[128,2048]{1,0:T(8,128)(2,1)S(1)} collective-permute-done((bf16[128,2048]{1,0:T(8,128)(2,1)}, bf16[128,2048]{1,0:T(8,128)(2,1)S(1)}, u32[]{:S(2)}, u32[]{:S(2)}) %collective-permute-start.65) | collective-permute-done | bytes 524320 | tf_op jit(solution)/shard_map/ppermute | solution.py:78
  463.5 12.0 %collective-permute-done.67.refs_4_ = bf16[128,2048]{1,0:T(8,128)(2,1)S(1)} collective-permute-done((bf16[128,2048]{1,0:T(8,128)(2,1)S(1)}, bf16[128,2048]{1,0:T(8,128)(2,1)S(1)}, u32[]{:S(2)}, u32[]{:S(2)}) %collective-permute-start.67) | collective-permute-done | bytes 524320 | tf_op jit(solution)/shard_map/ppermute | solution.py:78
  478.3 9.0 %collective-permute-done.69.refs_6_ = bf16[128,2048]{1,0:T(8,128)(2,1)S(1)} collective-permute-done((bf16[128,2048]{1,0:T(8,128)(2,1)S(1)}, bf16[128,2048]{1,0:T(8,128)(2,1)S(1)}, u32[]{:S(2)}, u32[]{:S(2)}) %collective-permute-start.69) | collective-permute-done | bytes 524320 | tf_op jit(solution)/shard_map/ppermute | solution.py:78
  499.4 5.8 shard_map.199
  505.2 13.2 %shard_map.200 = (bf16[1024,256]{1,0:T(8,128)(2,1)}, bf16[1024,256]{1,0:T(8,128)(2,1)}, bf16[1024,256]{1,0:T(8,128)(2,1)}) custom-call(bf16[1024,256]{1,0:T(8,128)(2,1)} %get-tuple-element.359.q_ref, bf16[1024,256]{1,0:T(8,128)(2,1)} %get-tuple-element.360.k_ref, bf16[1024,256]{1,0:T(8,128)(2,1)} %get-tuple-element.361.v_ref, ...), custom_call_target="tpu_custom_call" | custom-call | flops 2684354560 | bytes 4718592 | tf_op jit(solution)/shard_map/pallas_call | solution.py:866
  521.6 7.4 %convolution_convert_fusion.one_own.other_own.refs_0_ = bf16[1024,2048]{1,0:T(8,128)(2,1)} fusion(bf16[1024,768]{1,0:T(8,128)(2,1)S(1)} %constant_dynamic-update-slice_fusion, bf16[2048,768]{1,0:T(8,128)(2,1)} %bitcast.9.refs_9_), kind=kOutput, calls=%fused_computation | convolution fusion | flops 3223322624 | bytes 8912896 | tf_op jit(solution)/shard_map/tc,dc->td/dot_general | solution.py:984
  529.1 5.0 convolution_convert_fusion.5
  537.3 4.3 collective-permute-done.73.other_ref
  547.5 8.1 %collective-permute-done.74.one_ref = bf16[128,2048]{1,0:T(8,128)(2,1)S(1)} collective-permute-done((bf16[128,2048]{1,0:T(8,128)(2,1)}, bf16[128,2048]{1,0:T(8,128)(2,1)S(1)}, u32[]{:S(2)}, u32[]{:S(2)}) %collective-permute-start.74) | collective-permute-done | bytes 524320 | tf_op jit(solution)/shard_map/ppermute | solution.py:121
  557.2 3.0 shard_map.202
  562.7 8.8 %collective-permute-done.76.one_ref = bf16[128,2048]{1,0:T(8,128)(2,1)S(1)} collective-permute-done((bf16[128,2048]{1,0:T(8,128)(2,1)}, bf16[128,2048]{1,0:T(8,128)(2,1)S(1)}, u32[]{:S(2)}, u32[]{:S(2)}) %collective-permute-start.76) | collective-permute-done | bytes 524320 | tf_op jit(solution)/shard_map/ppermute | solution.py:121
  579.7 4.4 convolution_convert_fusion.6
  588.8 3.2 collective-permute-start.82
  592.0 6.1 collective-permute-done.81.refs_2_
  599.8 5.3 collective-permute-done.82.refs_3_
  606.5 7.3 %collective-permute-start.86 = (bf16[64,1024]{1,0:T(8,128)(2,1)}, bf16[64,1024]{1,0:T(8,128)(2,1)S(1)}, u32[]{:S(2)}, u32[]{:S(2)}) collective-permute-start(bf16[64,1024]{1,0:T(8,128)(2,1)} %get-tuple-element.393), channel_id=1, source_target_pairs={{0,28},{4,0},{8,4},{12,8},{16,12},{20,16},{24,20},{28,24},{1,29},{... | collective-permute-start | bytes 393224 | tf_op jit(solution)/shard_map/ppermute | solution.py:382
  613.8 5.3 shard_map.205.refs_3_
  623.6 10.1 %shard_map.206 = (bf16[128,8192]{1,0:T(8,128)(2,1)}, f32[8,2048]{1,0:T(8,128)}) custom-call(bf16[128,8192]{1,0:T(8,128)(2,1)} %bitcast.71, f32[128,8192]{1,0:T(8,128)} %get-tuple-element.358.dmid_ref, bf16[1024,2048]{1,0:T(8,128)(2,1)} %convolution_convert_fusion.one_own.other_own.refs_0_, bf16[128,2048]{1,0:T(8,128)(2,1)} %copy-done.11, ...), custom_call_target="tpu_custom_call" | custom-call | flops 104857600 | bytes 14356480 | tf_op jit(solution)/shard_map/pallas_call | solution.py:745
  634.6 5.0 collective-permute-done.101
  639.7 5.6 collective-permute-done.102
  649.8 2.9 collective-permute-start.96
  658.7 5.7 collective-permute-done.96.refs_11_
  664.4 6.9 collective-permute-start.100
  674.9 3.1 collective-permute-start.89
  678.8 3.9 shard_map.210
  684.9 2.9 collective-permute-start.92
  (517 shorter events, 214.8 us)
Async XLA Ops:
  7.2 101.1 %all-gather.5.cloned.1.call-start = ((), (), s32[]{:S(2)}) async-start(), calls=%async_computation.5 | async-start | bytes 2359296 | tf_op jit(solution)/shard_map/all_gather | solution.py:932
  7.9 169.0 %all-gather.7.cloned.1.call-start = ((), (), s32[]{:S(2)}) async-start(), calls=%async_computation.6 | async-start | bytes 10485760 | tf_op jit(solution)/shard_map/all_gather | solution.py:954
  10.1 40.9 %collective-permute-start.3 = (bf16[64,768]{1,0:T(8,128)(2,1)}, bf16[64,768]{1,0:T(8,128)(2,1)S(1)}, u32[]{:S(2)}, u32[]{:S(2)}) collective-permute-start(bf16[64,768]{1,0:T(8,128)(2,1)} %get-tuple-element.236), channel_id=1, source_target_pairs={{0,16},{4,20},{8,24},{12,28},{16,0},{20,4},{24,8},{28,12},{1,17},{... | collective-permute-start | bytes 294920 | tf_op jit(solution)/shard_map/ppermute | solution.py:382
  17.2 17.2 %collective-permute-start.2 = (bf16[64,768]{1,0:T(8,128)(2,1)}, bf16[64,768]{1,0:T(8,128)(2,1)S(1)}, u32[]{:S(2)}, u32[]{:S(2)}) collective-permute-start(bf16[64,768]{1,0:T(8,128)(2,1)} %get-tuple-element.234), channel_id=1, source_target_pairs={{0,12},{4,16},{8,20},{12,24},{16,28},{20,0},{24,4},{28,8},{1,13},{... | collective-permute-start | bytes 294920 | tf_op jit(solution)/shard_map/ppermute | solution.py:382
  21.0 30.0 %collective-permute-start.5 = (bf16[64,768]{1,0:T(8,128)(2,1)}, bf16[64,768]{1,0:T(8,128)(2,1)S(1)}, u32[]{:S(2)}, u32[]{:S(2)}) collective-permute-start(bf16[64,768]{1,0:T(8,128)(2,1)} %get-tuple-element.240), channel_id=1, source_target_pairs={{0,24},{4,28},{8,0},{12,4},{16,8},{20,12},{24,16},{28,20},{1,25},{... | collective-permute-start | bytes 294920 | tf_op jit(solution)/shard_map/ppermute | solution.py:382
  24.8 26.2 %collective-permute-start.4 = (bf16[64,768]{1,0:T(8,128)(2,1)}, bf16[64,768]{1,0:T(8,128)(2,1)S(1)}, u32[]{:S(2)}, u32[]{:S(2)}) collective-permute-start(bf16[64,768]{1,0:T(8,128)(2,1)} %get-tuple-element.238), channel_id=1, source_target_pairs={{0,20},{4,24},{8,28},{12,0},{16,4},{20,8},{24,12},{28,16},{1,21},{... | collective-permute-start | bytes 294920 | tf_op jit(solution)/shard_map/ppermute | solution.py:382
  34.4 16.7 %collective-permute-start.6 = (bf16[64,768]{1,0:T(8,128)(2,1)}, bf16[64,768]{1,0:T(8,128)(2,1)S(1)}, u32[]{:S(2)}, u32[]{:S(2)}) collective-permute-start(bf16[64,768]{1,0:T(8,128)(2,1)} %get-tuple-element.242), channel_id=1, source_target_pairs={{0,28},{4,0},{8,4},{12,8},{16,12},{20,16},{24,20},{28,24},{1,29},{... | collective-permute-start | bytes 294920 | tf_op jit(solution)/shard_map/ppermute | solution.py:382
  51.0 27.0 %collective-permute-start.8 = (bf16[128,2048]{1,0:T(8,128)(2,1)}, bf16[128,2048]{1,0:T(8,128)(2,1)S(1)}, u32[]{:S(2)}, u32[]{:S(2)}) collective-permute-start(bf16[128,2048]{1,0:T(8,128)(2,1)} %get-tuple-element.243.refs_0_), channel_id=1, source_target_pairs={{8,0},{16,8},{24,16},{28,24},{20,28},{12,20},{4,12},{0,4},{9,1},{1... | collective-permute-start | bytes 1572872 | tf_op jit(solution)/shard_map/ppermute | solution.py:78
  51.1 26.9 %collective-permute-start.7 = (bf16[128,2048]{1,0:T(8,128)(2,1)}, bf16[128,2048]{1,0:T(8,128)(2,1)S(1)}, u32[]{:S(2)}, u32[]{:S(2)}) collective-permute-start(bf16[128,2048]{1,0:T(8,128)(2,1)} %get-tuple-element.243.refs_0_), channel_id=1, source_target_pairs={{0,8},{8,16},{16,24},{24,28},{28,20},{20,12},{12,4},{4,0},{1,9},{9... | collective-permute-start | bytes 1572872 | tf_op jit(solution)/shard_map/ppermute | solution.py:78
  55.3 24.7 %collective-permute-start.11 = (bf16[512,768]{1,0:T(8,128)(2,1)}, bf16[512,768]{1,0:T(8,128)(2,1)S(1)}, u32[]{:S(2)}, u32[]{:S(2)}) collective-permute-start(bf16[512,768]{1,0:T(8,128)(2,1)} %shard_map.181), channel_id=1, source_target_pairs={{0,2},{1,3},{2,0},{3,1},{4,6},{5,7},{6,4},{7,5},{8,10},{9,11},{10,... | collective-permute-start | bytes 2359304 | tf_op jit(solution)/shard_map/ppermute | solution.py:435
  78.0 13.6 %collective-permute-start.10 = (bf16[128,2048]{1,0:T(8,128)(2,1)S(1)}, bf16[128,2048]{1,0:T(8,128)(2,1)S(1)}, u32[]{:S(2)}, u32[]{:S(2)}) collective-permute-start(bf16[128,2048]{1,0:T(8,128)(2,1)S(1)} %collective-permute-done.8.refs_2_), channel_id=1, source_target_pairs={{8,0},{16,8},{24,16},{28,24},{20,28},{12,20},{4,12},{0,4},{9,1},{1... | collective-permute-start | bytes 1572872 | tf_op jit(solution)/shard_map/ppermute | solution.py:78
  78.0 13.6 %collective-permute-start.9 = (bf16[128,2048]{1,0:T(8,128)(2,1)S(1)}, bf16[128,2048]{1,0:T(8,128)(2,1)S(1)}, u32[]{:S(2)}, u32[]{:S(2)}) collective-permute-start(bf16[128,2048]{1,0:T(8,128)(2,1)S(1)} %collective-permute-done.7.refs_1_), channel_id=1, source_target_pairs={{0,8},{8,16},{16,24},{24,28},{28,20},{20,12},{12,4},{4,0},{1,9},{9... | collective-permute-start | bytes 1572872 | tf_op jit(solution)/shard_map/ppermute | solution.py:78
  80.0 13.7 %collective-permute-start.14 = (bf16[512,768]{1,0:T(8,128)(2,1)}, bf16[512,768]{1,0:T(8,128)(2,1)S(1)}, u32[]{:S(2)}, u32[]{:S(2)}) collective-permute-start(bf16[512,768]{1,0:T(8,128)(2,1)} %shard_map.181), channel_id=1, source_target_pairs={{0,1},{1,0},{2,3},{3,2},{4,5},{5,4},{6,7},{7,6},{8,9},{9,8},{10,11... | collective-permute-start | bytes 2359304 | tf_op jit(solution)/shard_map/ppermute | solution.py:439
  91.7 16.6 %collective-permute-start.15 = (bf16[512,768]{1,0:T(8,128)(2,1)S(1)}, bf16[512,768]{1,0:T(8,128)(2,1)S(1)}, u32[]{:S(2)}, u32[]{:S(2)}) collective-permute-start(bf16[512,768]{1,0:T(8,128)(2,1)S(1)} %collective-permute-done.11), channel_id=1, source_target_pairs={{0,1},{1,0},{2,3},{3,2},{4,5},{5,4},{6,7},{7,6},{8,9},{9,8},{10,11... | collective-permute-start | bytes 2359304 | tf_op jit(solution)/shard_map/ppermute | solution.py:439
  91.7 14.3 %collective-permute-start.12 = (bf16[128,2048]{1,0:T(8,128)(2,1)S(1)}, bf16[128,2048]{1,0:T(8,128)(2,1)S(1)}, u32[]{:S(2)}, u32[]{:S(2)}) collective-permute-start(bf16[128,2048]{1,0:T(8,128)(2,1)S(1)} %collective-permute-done.9.refs_3_), channel_id=1, source_target_pairs={{0,8},{8,16},{16,24},{24,28},{28,20},{20,12},{12,4},{4,0},{1,9},{9... | collective-permute-start | bytes 1572872 | tf_op jit(solution)/shard_map/ppermute | solution.py:78
  93.3 14.1 %collective-permute-start.13 = (bf16[128,2048]{1,0:T(8,128)(2,1)S(1)}, bf16[128,2048]{1,0:T(8,128)(2,1)S(1)}, u32[]{:S(2)}, u32[]{:S(2)}) collective-permute-start(bf16[128,2048]{1,0:T(8,128)(2,1)S(1)} %collective-permute-done.10.refs_4_), channel_id=1, source_target_pairs={{8,0},{16,8},{24,16},{28,24},{20,28},{12,20},{4,12},{0,4},{9,1},{1... | collective-permute-start | bytes 1572872 | tf_op jit(solution)/shard_map/ppermute | solution.py:78
  108.3 123.3 %all-gather.9.cloned.1.call-start = ((), (), s32[]{:S(2)}) async-start(), calls=%async_computation.7 | async-start | bytes 5242880 | tf_op jit(solution)/shard_map/all_gather | solution.py:427
  120.1 171.6 %all-gather.11.cloned.1.call-start = ((), (), s32[]{:S(2)}) async-start(), calls=%async_computation.8 | async-start | bytes 10485760 | tf_op jit(solution)/shard_map/all_gather | solution.py:427
  131.1 23.8 %collective-permute-start.18 = (bf16[64,2048]{1,0:T(8,128)(2,1)}, bf16[64,2048]{1,0:T(8,128)(2,1)S(1)}, u32[]{:S(2)}, u32[]{:S(2)}) collective-permute-start(bf16[64,2048]{1,0:T(8,128)(2,1)} %get-tuple-element.266), channel_id=1, source_target_pairs={{0,4},{4,8},{8,12},{12,16},{16,20},{20,24},{24,28},{28,0},{1,5},{5... | collective-permute-start | bytes 786440 | tf_op jit(solution)/shard_map/ppermute | solution.py:382
  132.9 22.1 %collective-permute-start.19 = (bf16[64,2048]{1,0:T(8,128)(2,1)}, bf16[64,2048]{1,0:T(8,128)(2,1)S(1)}, u32[]{:S(2)}, u32[]{:S(2)}) collective-permute-start(bf16[64,2048]{1,0:T(8,128)(2,1)} %get-tuple-element.267), channel_id=1, source_target_pairs={{0,8},{4,12},{8,16},{12,20},{16,24},{20,28},{24,0},{28,4},{1,9},{5... | collective-permute-start | bytes 786440 | tf_op jit(solution)/shard_map/ppermute | solution.py:382
  134.1 23.5 %collective-permute-start.20 = (bf16[64,2048]{1,0:T(8,128)(2,1)}, bf16[64,2048]{1,0:T(8,128)(2,1)S(1)}, u32[]{:S(2)}, u32[]{:S(2)}) collective-permute-start(bf16[64,2048]{1,0:T(8,128)(2,1)} %get-tuple-element.268), channel_id=1, source_target_pairs={{0,12},{4,16},{8,20},{12,24},{16,28},{20,0},{24,4},{28,8},{1,13},{... | collective-permute-start | bytes 786440 | tf_op jit(solution)/shard_map/ppermute | solution.py:382
  169.8 19.6 %collective-permute-start.28 = (bf16[64,2048]{1,0:T(8,128)(2,1)S(1)}, bf16[64,2048]{1,0:T(8,128)(2,1)S(1)}, u32[]{:S(2)}, u32[]{:S(2)}) collective-permute-start(bf16[64,2048]{1,0:T(8,128)(2,1)S(1)} %copy-done.106), channel_id=1, source_target_pairs={{0,16},{4,20},{8,24},{12,28},{16,0},{20,4},{24,8},{28,12},{1,17},{... | collective-permute-start | bytes 786440 | tf_op jit(solution)/shard_map/ppermute | solution.py:382
  171.7 17.7 %collective-permute-start.29 = (bf16[64,2048]{1,0:T(8,128)(2,1)S(1)}, bf16[64,2048]{1,0:T(8,128)(2,1)S(1)}, u32[]{:S(2)}, u32[]{:S(2)}) collective-permute-start(bf16[64,2048]{1,0:T(8,128)(2,1)S(1)} %copy-done.105), channel_id=1, source_target_pairs={{0,20},{4,24},{8,28},{12,0},{16,4},{20,8},{24,12},{28,16},{1,21},{... | collective-permute-start | bytes 786440 | tf_op jit(solution)/shard_map/ppermute | solution.py:382
  199.5 32.1 %collective-permute-start.31 = (bf16[128,2048]{1,0:T(8,128)(2,1)}, bf16[128,2048]{1,0:T(8,128)(2,1)S(1)}, u32[]{:S(2)}, u32[]{:S(2)}) collective-permute-start(bf16[128,2048]{1,0:T(8,128)(2,1)} %get-tuple-element.281.refs_0_), channel_id=1, source_target_pairs={{8,0},{16,8},{24,16},{28,24},{20,28},{12,20},{4,12},{0,4},{9,1},{1... | collective-permute-start | bytes 1572872 | tf_op jit(solution)/shard_map/ppermute | solution.py:78
  205.7 25.9 %collective-permute-start.30 = (bf16[128,2048]{1,0:T(8,128)(2,1)}, bf16[128,2048]{1,0:T(8,128)(2,1)S(1)}, u32[]{:S(2)}, u32[]{:S(2)}) collective-permute-start(bf16[128,2048]{1,0:T(8,128)(2,1)} %get-tuple-element.281.refs_0_), channel_id=1, source_target_pairs={{0,8},{8,16},{16,24},{24,28},{28,20},{20,12},{12,4},{4,0},{1,9},{9... | collective-permute-start | bytes 1572872 | tf_op jit(solution)/shard_map/ppermute | solution.py:78
  205.7 18.2 %collective-permute-start.32 = (bf16[64,2048]{1,0:T(8,128)(2,1)S(1)}, bf16[64,2048]{1,0:T(8,128)(2,1)S(1)}, u32[]{:S(2)}, u32[]{:S(2)}) collective-permute-start(bf16[64,2048]{1,0:T(8,128)(2,1)S(1)} %copy-done.104), channel_id=1, source_target_pairs={{0,24},{4,28},{8,0},{12,4},{16,8},{20,12},{24,16},{28,20},{1,25},{... | collective-permute-start | bytes 786440 | tf_op jit(solution)/shard_map/ppermute | solution.py:382
  208.7 19.2 %collective-permute-start.33 = (bf16[64,2048]{1,0:T(8,128)(2,1)S(1)}, bf16[64,2048]{1,0:T(8,128)(2,1)S(1)}, u32[]{:S(2)}, u32[]{:S(2)}) collective-permute-start(bf16[64,2048]{1,0:T(8,128)(2,1)S(1)} %copy-done.103), channel_id=1, source_target_pairs={{0,28},{4,0},{8,4},{12,8},{16,12},{20,16},{24,20},{28,24},{1,29},{... | collective-permute-start | bytes 786440 | tf_op jit(solution)/shard_map/ppermute | solution.py:382
  231.6 258.2 %reduce-scatter.6.cloned.1.call-start = ((), (), s32[]{:S(2)}) async-start(), calls=%async_computation.9 | async-start | bytes 5242880 | tf_op jit(solution)/shard_map/reduce_scatter | solution.py:431
  231.7 12.5 %collective-permute-start.35 = (bf16[128,2048]{1,0:T(8,128)(2,1)S(1)}, bf16[128,2048]{1,0:T(8,128)(2,1)S(1)}, u32[]{:S(2)}, u32[]{:S(2)}) collective-permute-start(bf16[128,2048]{1,0:T(8,128)(2,1)S(1)} %collective-permute-done.31.refs_2_), channel_id=1, source_target_pairs={{8,0},{16,8},{24,16},{28,24},{20,28},{12,20},{4,12},{0,4},{9,1},{1... | collective-permute-start | bytes 1572872 | tf_op jit(solution)/shard_map/ppermute | solution.py:78
  288.2 17.6 %collective-permute-start.45 = (bf16[128,2048]{1,0:T(8,128)(2,1)S(1)}, bf16[128,2048]{1,0:T(8,128)(2,1)S(1)}, u32[]{:S(2)}, u32[]{:S(2)}) collective-permute-start(bf16[128,2048]{1,0:T(8,128)(2,1)S(1)} %collective-permute-done.43.refs_4_), channel_id=1, source_target_pairs={{8,0},{16,8},{24,16},{28,24},{20,28},{12,20},{4,12},{0,4},{9,1},{1... | collective-permute-start | bytes 1572872 | tf_op jit(solution)/shard_map/ppermute | solution.py:78
  289.6 16.2 %collective-permute-start.44 = (bf16[128,2048]{1,0:T(8,128)(2,1)S(1)}, bf16[128,2048]{1,0:T(8,128)(2,1)S(1)}, u32[]{:S(2)}, u32[]{:S(2)}) collective-permute-start(bf16[128,2048]{1,0:T(8,128)(2,1)S(1)} %collective-permute-done.42.refs_3_), channel_id=1, source_target_pairs={{0,8},{8,16},{16,24},{24,28},{28,20},{20,12},{12,4},{4,0},{1,9},{9... | collective-permute-start | bytes 1572872 | tf_op jit(solution)/shard_map/ppermute | solution.py:78
  329.6 13.9 %collective-permute-start.50 = (bf16[128,2048]{1,0:T(8,128)(2,1)}, bf16[128,2048]{1,0:T(8,128)(2,1)S(1)}, u32[]{:S(2)}, u32[]{:S(2)}) collective-permute-start(bf16[128,2048]{1,0:T(8,128)(2,1)} %get-tuple-element.325), channel_id=1, source_target_pairs={{0,8},{8,16},{16,24},{24,28},{28,20},{20,12},{12,4},{4,0},{1,9},{9... | collective-permute-start | bytes 1572872 | tf_op jit(solution)/shard_map/ppermute | solution.py:121
  330.6 12.9 %collective-permute-start.51 = (bf16[128,2048]{1,0:T(8,128)(2,1)}, bf16[128,2048]{1,0:T(8,128)(2,1)S(1)}, u32[]{:S(2)}, u32[]{:S(2)}) collective-permute-start(bf16[128,2048]{1,0:T(8,128)(2,1)} %get-tuple-element.326), channel_id=1, source_target_pairs={{8,0},{16,8},{24,16},{28,24},{20,28},{12,20},{4,12},{0,4},{9,1},{1... | collective-permute-start | bytes 1572872 | tf_op jit(solution)/shard_map/ppermute | solution.py:121
  347.1 30.4 %collective-permute-start.56 = (bf16[128,2048]{1,0:T(8,128)(2,1)}, bf16[128,2048]{1,0:T(8,128)(2,1)S(1)}, u32[]{:S(2)}, u32[]{:S(2)}) collective-permute-start(bf16[128,2048]{1,0:T(8,128)(2,1)} %get-tuple-element.331), channel_id=1, source_target_pairs={{0,8},{8,16},{16,24},{24,28},{28,20},{20,12},{12,4},{4,0},{1,9},{9... | collective-permute-start | bytes 1572872 | tf_op jit(solution)/shard_map/ppermute | solution.py:121
  348.1 29.4 %collective-permute-start.57 = (bf16[128,2048]{1,0:T(8,128)(2,1)}, bf16[128,2048]{1,0:T(8,128)(2,1)S(1)}, u32[]{:S(2)}, u32[]{:S(2)}) collective-permute-start(bf16[128,2048]{1,0:T(8,128)(2,1)} %get-tuple-element.332), channel_id=1, source_target_pairs={{8,0},{16,8},{24,16},{28,24},{20,28},{12,20},{4,12},{0,4},{9,1},{1... | collective-permute-start | bytes 1572872 | tf_op jit(solution)/shard_map/ppermute | solution.py:121
  375.5 17.7 %collective-permute-start.54 = (bf16[128,2048]{1,0:T(8,128)(2,1)}, bf16[128,2048]{1,0:T(8,128)(2,1)S(1)}, u32[]{:S(2)}, u32[]{:S(2)}) collective-permute-start(bf16[128,2048]{1,0:T(8,128)(2,1)} %get-tuple-element.329), channel_id=1, source_target_pairs={{0,8},{8,16},{16,24},{24,28},{28,20},{20,12},{12,4},{4,0},{1,9},{9... | collective-permute-start | bytes 1572872 | tf_op jit(solution)/shard_map/ppermute | solution.py:121
  376.0 17.1 %collective-permute-start.55 = (bf16[128,2048]{1,0:T(8,128)(2,1)}, bf16[128,2048]{1,0:T(8,128)(2,1)S(1)}, u32[]{:S(2)}, u32[]{:S(2)}) collective-permute-start(bf16[128,2048]{1,0:T(8,128)(2,1)} %get-tuple-element.330), channel_id=1, source_target_pairs={{8,0},{16,8},{24,16},{28,24},{20,28},{12,20},{4,12},{0,4},{9,1},{1... | collective-permute-start | bytes 1572872 | tf_op jit(solution)/shard_map/ppermute | solution.py:121
  381.8 15.1 %collective-permute-start.58 = (bf16[128,2048]{1,0:T(8,128)(2,1)}, bf16[128,2048]{1,0:T(8,128)(2,1)S(1)}, u32[]{:S(2)}, u32[]{:S(2)}) collective-permute-start(bf16[128,2048]{1,0:T(8,128)(2,1)} %get-tuple-element.333), channel_id=1, source_target_pairs={{0,8},{8,16},{16,24},{24,28},{28,20},{20,12},{12,4},{4,0},{1,9},{9... | collective-permute-start | bytes 1572872 | tf_op jit(solution)/shard_map/ppermute | solution.py:121
  382.3 14.7 %collective-permute-start.59 = (bf16[128,2048]{1,0:T(8,128)(2,1)}, bf16[128,2048]{1,0:T(8,128)(2,1)S(1)}, u32[]{:S(2)}, u32[]{:S(2)}) collective-permute-start(bf16[128,2048]{1,0:T(8,128)(2,1)} %get-tuple-element.334), channel_id=1, source_target_pairs={{8,0},{16,8},{24,16},{28,24},{20,28},{12,20},{4,12},{0,4},{9,1},{1... | collective-permute-start | bytes 1572872 | tf_op jit(solution)/shard_map/ppermute | solution.py:121
  411.6 93.7 %reduce-scatter.8.cloned.1.call-start = ((), (), s32[]{:S(2)}) async-start(), calls=%async_computation.10 | async-start | bytes 5242880 | tf_op jit(solution)/shard_map/reduce_scatter | solution.py:431
  412.5 206.7 %reduce-scatter.10.cloned.1.call-start = ((), (), s32[]{:S(2)}) async-start(), calls=%async_computation.11 | async-start | bytes 5242880 | tf_op jit(solution)/shard_map/reduce_scatter | solution.py:431
  415.3 19.2 %collective-permute-start.62 = (bf16[128,2048]{1,0:T(8,128)(2,1)}, bf16[128,2048]{1,0:T(8,128)(2,1)S(1)}, u32[]{:S(2)}, u32[]{:S(2)}) collective-permute-start(bf16[128,2048]{1,0:T(8,128)(2,1)} %get-tuple-element.344), channel_id=1, source_target_pairs={{0,8},{8,16},{16,24},{24,28},{28,20},{20,12},{12,4},{4,0},{1,9},{9... | collective-permute-start | bytes 1572872 | tf_op jit(solution)/shard_map/ppermute | solution.py:121
  415.9 18.5 %collective-permute-start.63 = (bf16[128,2048]{1,0:T(8,128)(2,1)}, bf16[128,2048]{1,0:T(8,128)(2,1)S(1)}, u32[]{:S(2)}, u32[]{:S(2)}) collective-permute-start(bf16[128,2048]{1,0:T(8,128)(2,1)} %get-tuple-element.345), channel_id=1, source_target_pairs={{8,0},{16,8},{24,16},{28,24},{20,28},{12,20},{4,12},{0,4},{9,1},{1... | collective-permute-start | bytes 1572872 | tf_op jit(solution)/shard_map/ppermute | solution.py:121
  434.5 238.1 %reduce-scatter.12.cloned.1.call-start = ((), (), s32[]{:S(2)}) async-start(), calls=%async_computation.12 | async-start | bytes 3932160 | tf_op jit(solution)/shard_map/reduce_scatter | solution.py:431
  447.5 13.7 %collective-permute-start.65 = (bf16[128,2048]{1,0:T(8,128)(2,1)}, bf16[128,2048]{1,0:T(8,128)(2,1)S(1)}, u32[]{:S(2)}, u32[]{:S(2)}) collective-permute-start(bf16[128,2048]{1,0:T(8,128)(2,1)} %get-tuple-element.362.refs_0_), channel_id=1, source_target_pairs={{8,0},{16,8},{24,16},{28,24},{20,28},{12,20},{4,12},{0,4},{9,1},{1... | collective-permute-start | bytes 1572872 | tf_op jit(solution)/shard_map/ppermute | solution.py:78
  449.2 14.1 %collective-permute-start.64 = (bf16[128,2048]{1,0:T(8,128)(2,1)}, bf16[128,2048]{1,0:T(8,128)(2,1)S(1)}, u32[]{:S(2)}, u32[]{:S(2)}) collective-permute-start(bf16[128,2048]{1,0:T(8,128)(2,1)} %get-tuple-element.362.refs_0_), channel_id=1, source_target_pairs={{0,8},{8,16},{16,24},{24,28},{28,20},{20,12},{12,4},{4,0},{1,9},{9... | collective-permute-start | bytes 1572872 | tf_op jit(solution)/shard_map/ppermute | solution.py:78
  461.2 14.3 %collective-permute-start.67 = (bf16[128,2048]{1,0:T(8,128)(2,1)S(1)}, bf16[128,2048]{1,0:T(8,128)(2,1)S(1)}, u32[]{:S(2)}, u32[]{:S(2)}) collective-permute-start(bf16[128,2048]{1,0:T(8,128)(2,1)S(1)} %collective-permute-done.65.refs_2_), channel_id=1, source_target_pairs={{8,0},{16,8},{24,16},{28,24},{20,28},{12,20},{4,12},{0,4},{9,1},{1... | collective-permute-start | bytes 1572872 | tf_op jit(solution)/shard_map/ppermute | solution.py:78
  463.2 14.6 %collective-permute-start.66 = (bf16[128,2048]{1,0:T(8,128)(2,1)S(1)}, bf16[128,2048]{1,0:T(8,128)(2,1)S(1)}, u32[]{:S(2)}, u32[]{:S(2)}) collective-permute-start(bf16[128,2048]{1,0:T(8,128)(2,1)S(1)} %collective-permute-done.64.refs_1_), channel_id=1, source_target_pairs={{0,8},{8,16},{16,24},{24,28},{28,20},{20,12},{12,4},{4,0},{1,9},{9... | collective-permute-start | bytes 1572872 | tf_op jit(solution)/shard_map/ppermute | solution.py:78
  534.1 156.7 %reduce-scatter.14.cloned.1.call-start = ((), (), s32[]{:S(2)}) async-start(), calls=%async_computation.13 | async-start | bytes 1310720 | tf_op jit(solution)/shard_map/reduce_scatter | solution.py:431
  577.7 44.3 %collective-permute-start.78 = (bf16[128,2048]{1,0:T(8,128)(2,1)}, bf16[128,2048]{1,0:T(8,128)(2,1)S(1)}, u32[]{:S(2)}, u32[]{:S(2)}) collective-permute-start(bf16[128,2048]{1,0:T(8,128)(2,1)} %get-tuple-element.377), channel_id=1, source_target_pairs={{0,8},{8,16},{16,24},{24,28},{28,20},{20,12},{12,4},{4,0},{1,9},{9... | collective-permute-start | bytes 1572872 | tf_op jit(solution)/shard_map/ppermute | solution.py:121
  579.4 42.6 %collective-permute-start.79 = (bf16[128,2048]{1,0:T(8,128)(2,1)}, bf16[128,2048]{1,0:T(8,128)(2,1)S(1)}, u32[]{:S(2)}, u32[]{:S(2)}) collective-permute-start(bf16[128,2048]{1,0:T(8,128)(2,1)} %get-tuple-element.378), channel_id=1, source_target_pairs={{8,0},{16,8},{24,16},{28,24},{20,28},{12,20},{4,12},{0,4},{9,1},{1... | collective-permute-start | bytes 1572872 | tf_op jit(solution)/shard_map/ppermute | solution.py:121
  588.8 16.4 %collective-permute-start.82 = (bf16[64,1024]{1,0:T(8,128)(2,1)}, bf16[64,1024]{1,0:T(8,128)(2,1)S(1)}, u32[]{:S(2)}, u32[]{:S(2)}) collective-permute-start(bf16[64,1024]{1,0:T(8,128)(2,1)} %get-tuple-element.385), channel_id=1, source_target_pairs={{0,12},{4,16},{8,20},{12,24},{16,28},{20,0},{24,4},{28,8},{1,13},{... | collective-permute-start | bytes 393224 | tf_op jit(solution)/shard_map/ppermute | solution.py:382
  599.8 22.2 %collective-permute-start.85 = (bf16[64,1024]{1,0:T(8,128)(2,1)}, bf16[64,1024]{1,0:T(8,128)(2,1)S(1)}, u32[]{:S(2)}, u32[]{:S(2)}) collective-permute-start(bf16[64,1024]{1,0:T(8,128)(2,1)} %get-tuple-element.391), channel_id=1, source_target_pairs={{0,24},{4,28},{8,0},{12,4},{16,8},{20,12},{24,16},{28,20},{1,25},{... | collective-permute-start | bytes 393224 | tf_op jit(solution)/shard_map/ppermute | solution.py:382
  605.1 16.8 %collective-permute-start.84 = (bf16[64,1024]{1,0:T(8,128)(2,1)}, bf16[64,1024]{1,0:T(8,128)(2,1)S(1)}, u32[]{:S(2)}, u32[]{:S(2)}) collective-permute-start(bf16[64,1024]{1,0:T(8,128)(2,1)} %get-tuple-element.389), channel_id=1, source_target_pairs={{0,20},{4,24},{8,28},{12,0},{16,4},{20,8},{24,12},{28,16},{1,21},{... | collective-permute-start | bytes 393224 | tf_op jit(solution)/shard_map/ppermute | solution.py:382
  606.5 15.5 %collective-permute-start.86 = (bf16[64,1024]{1,0:T(8,128)(2,1)}, bf16[64,1024]{1,0:T(8,128)(2,1)S(1)}, u32[]{:S(2)}, u32[]{:S(2)}) collective-permute-start(bf16[64,1024]{1,0:T(8,128)(2,1)} %get-tuple-element.393), channel_id=1, source_target_pairs={{0,28},{4,0},{8,4},{12,8},{16,12},{20,16},{24,20},{28,24},{1,29},{... | collective-permute-start | bytes 393224 | tf_op jit(solution)/shard_map/ppermute | solution.py:382
  649.8 14.6 %collective-permute-start.96 = (bf16[64,1024]{1,0:T(8,128)(2,1)}, bf16[64,1024]{1,0:T(8,128)(2,1)S(1)}, u32[]{:S(2)}, u32[]{:S(2)}) collective-permute-start(bf16[64,1024]{1,0:T(8,128)(2,1)} %get-tuple-element.441), channel_id=1, source_target_pairs={{0,12},{4,16},{8,20},{12,24},{16,28},{20,0},{24,4},{28,8},{1,13},{... | collective-permute-start | bytes 393224 | tf_op jit(solution)/shard_map/ppermute | solution.py:382
  652.7 18.6 %collective-permute-start.104 = (f32[16,2048]{1,0:T(8,128)S(1)}, f32[16,2048]{1,0:T(8,128)S(1)}, u32[]{:S(2)}, u32[]{:S(2)}) collective-permute-start(f32[16,2048]{1,0:T(8,128)S(1)} %add.114), channel_id=1, source_target_pairs={{0,1},{1,0},{2,3},{3,2},{4,5},{5,4},{6,7},{7,6},{8,9},{9,8},{10,11... | collective-permute-start | bytes 393224 | tf_op jit(solution)/shard_map/ppermute | solution.py:485
  652.8 21.9 %collective-permute-start.97 = (bf16[64,1024]{1,0:T(8,128)(2,1)}, bf16[64,1024]{1,0:T(8,128)(2,1)S(1)}, u32[]{:S(2)}, u32[]{:S(2)}) collective-permute-start(bf16[64,1024]{1,0:T(8,128)(2,1)} %get-tuple-element.443), channel_id=1, source_target_pairs={{0,16},{4,20},{8,24},{12,28},{16,0},{20,4},{24,8},{28,12},{1,17},{... | collective-permute-start | bytes 393224 | tf_op jit(solution)/shard_map/ppermute | solution.py:382
  654.6 20.2 %collective-permute-start.99 = (bf16[64,1024]{1,0:T(8,128)(2,1)}, bf16[64,1024]{1,0:T(8,128)(2,1)S(1)}, u32[]{:S(2)}, u32[]{:S(2)}) collective-permute-start(bf16[64,1024]{1,0:T(8,128)(2,1)} %get-tuple-element.447), channel_id=1, source_target_pairs={{0,24},{4,28},{8,0},{12,4},{16,8},{20,12},{24,16},{28,20},{1,25},{... | collective-permute-start | bytes 393224 | tf_op jit(solution)/shard_map/ppermute | solution.py:382
  657.7 17.2 %collective-permute-start.98 = (bf16[64,1024]{1,0:T(8,128)(2,1)}, bf16[64,1024]{1,0:T(8,128)(2,1)S(1)}, u32[]{:S(2)}, u32[]{:S(2)}) collective-permute-start(bf16[64,1024]{1,0:T(8,128)(2,1)} %get-tuple-element.445), channel_id=1, source_target_pairs={{0,20},{4,24},{8,28},{12,0},{16,4},{20,8},{24,12},{28,16},{1,21},{... | collective-permute-start | bytes 393224 | tf_op jit(solution)/shard_map/ppermute | solution.py:382
  664.4 13.6 %collective-permute-start.100 = (bf16[64,1024]{1,0:T(8,128)(2,1)}, bf16[64,1024]{1,0:T(8,128)(2,1)S(1)}, u32[]{:S(2)}, u32[]{:S(2)}) collective-permute-start(bf16[64,1024]{1,0:T(8,128)(2,1)} %get-tuple-element.449), channel_id=1, source_target_pairs={{0,28},{4,0},{8,4},{12,8},{16,12},{20,16},{24,20},{28,24},{1,29},{... | collective-permute-start | bytes 393224 | tf_op jit(solution)/shard_map/ppermute | solution.py:382
  671.3 18.1 %collective-permute-start.105 = (f32[16,2048]{1,0:T(8,128)S(1)}, f32[16,2048]{1,0:T(8,128)S(1)}, u32[]{:S(2)}, u32[]{:S(2)}) collective-permute-start(f32[16,2048]{1,0:T(8,128)S(1)} %add.115), channel_id=1, source_target_pairs={{0,2},{1,3},{2,0},{3,1},{4,6},{5,7},{6,4},{7,5},{8,10},{9,11},{10,... | collective-permute-start | bytes 393224 | tf_op jit(solution)/shard_map/ppermute | solution.py:485
  674.8 13.0 %collective-permute-start.87 = (bf16[64,768]{1,0:T(8,128)(2,1)}, bf16[64,768]{1,0:T(8,128)(2,1)S(1)}, u32[]{:S(2)}, u32[]{:S(2)}) collective-permute-start(bf16[64,768]{1,0:T(8,128)(2,1)} %get-tuple-element.406), channel_id=1, source_target_pairs={{0,4},{4,8},{8,12},{12,16},{16,20},{20,24},{24,28},{28,0},{1,5},{5... | collective-permute-start | bytes 294920 | tf_op jit(solution)/shard_map/ppermute | solution.py:382
  674.9 12.9 %collective-permute-start.89 = (bf16[64,768]{1,0:T(8,128)(2,1)}, bf16[64,768]{1,0:T(8,128)(2,1)S(1)}, u32[]{:S(2)}, u32[]{:S(2)}) collective-permute-start(bf16[64,768]{1,0:T(8,128)(2,1)} %get-tuple-element.408), channel_id=1, source_target_pairs={{0,12},{4,16},{8,20},{12,24},{16,28},{20,0},{24,4},{28,8},{1,13},{... | collective-permute-start | bytes 294920 | tf_op jit(solution)/shard_map/ppermute | solution.py:382
  (170 other events, 2187.8 us)
Sparse Core Ops, SparseCore 0:
  10.1 65.7 all-gather.4
  108.4 58.2 all-gather.6
  168.2 34.4 all-gather.8
  231.7 59.8 all-gather.10
  411.7 43.4 reduce-scatter.5
  457.7 44.5 reduce-scatter.7
  504.8 44.5 reduce-scatter.9
  552.6 37.9 reduce-scatter.11
  593.8 24.8 reduce-scatter.13

commit v3 on v2

--- a/solution.py
+++ b/solution.py
@@ -104,7 +104,7 @@
         out_specs=[whole(shape, 0)] * 2,
         out_shape=[jax.ShapeDtypeStruct(shape, BF16)] * 2,
         cost_estimate=cost(moving, [jax.ShapeDtypeStruct(shape, BF16)] * 4),
-        compiler_params=room(12 * rows * partial.shape[1] * 2),
+        compiler_params=room(),
     )(*moving, partial, partial)
 
 
@@ -175,17 +175,17 @@
         ],
         out_shape=outs,
         cost_estimate=cost((*blocks, weight), outs, 2 * total * depth * columns),
-        compiler_params=room(4 * total * depth, 4 * tile * depth, 12 * total * tile),
+        compiler_params=room(),
     )(*blocks, weight)
 
 
 def ffn_specs(blocks, width):
     total, depth = sum(v.shape[0] for v in blocks), blocks[0].shape[1]
-    tile = min(256 if total <= 1024 else 128, width)
+    tile = run_of(width, 2)
     once = pl.Buffered(1)
     whole = [pl.BlockSpec(v.shape, lambda j: (0, 0), pipeline_mode=once) for v in blocks]
     joined = pl.BlockSpec((total, depth), lambda j: (0, 0), pipeline_mode=once)
-    return (total, depth, tile, whole, joined, pl.BlockSpec((total, tile), lambda j: (0, j)))
+    return (total, depth, tile, whole, joined, lambda c: pl.BlockSpec((total, c), lambda j: (0, j)))
 
 
 def join_once(refs, joined):
@@ -200,90 +200,63 @@
 def ffn_enter(blocks, weight):
     width = weight.shape[1] // 2
     total, depth, tile, whole, joined_spec, cut = ffn_specs(blocks, width)
-    count, steps = len(blocks), width // tile
+    count = len(blocks)
 
     def kernel(*refs):
-        wg_ref, wu_ref, joined, gate_ref, up_ref, hidden_ref = refs[count:]
+        w_ref, joined, both_ref, hidden_ref = refs[count:]
         join_once(refs[:count], joined)
-        gate = jnp.dot(joined[...], wg_ref[...], preferred_element_type=F32)
-        up = jnp.dot(joined[...], wu_ref[...], preferred_element_type=F32)
-        gate_ref[...] = gate
-        up_ref[...] = up
+        both = jnp.dot(joined[...], w_ref[...], preferred_element_type=F32)
+        gate, up = both[:, :tile], both[:, tile:]
+        both_ref[...] = both
         hidden_ref[...] = (gate * jax.nn.sigmoid(gate) * up).astype(BF16)
 
     outs = [
         jax.ShapeDtypeStruct((total, depth), BF16),
-        jax.ShapeDtypeStruct((total, width), F32),
-        jax.ShapeDtypeStruct((total, width), F32),
+        jax.ShapeDtypeStruct((total, 2 * width), F32),
         jax.ShapeDtypeStruct((total, width), BF16),
-    ]
-    w_specs = [
-        pl.BlockSpec((depth, tile), lambda j: (0, j)),
-        pl.BlockSpec((depth, tile), lambda j: (0, steps + j)),
     ]
     return pl.pallas_call(
         kernel,
-        grid=(steps,),
-        in_specs=whole + w_specs,
-        out_specs=[joined_spec, cut, cut, cut],
+        grid=(width // tile,),
+        in_specs=whole + [pl.BlockSpec((depth, 2 * tile), lambda j: (0, j))],
+        out_specs=[joined_spec, cut(2 * tile), cut(tile)],
         out_shape=outs,
         cost_estimate=cost((*blocks, weight), outs, 4 * total * depth * width),
-        compiler_params=room(4 * total * depth, 8 * tile * depth, 36 * total * tile),
-    )(*blocks, weight, weight)
-
-
-def ffn_back(blocks, weight, gate, up):
+        compiler_params=room(),
+    )(*blocks, weight)
+
+
+def ffn_back(blocks, weight, both):
     width = weight.shape[0]
     total, depth, tile, whole, joined_spec, cut = ffn_specs(blocks, width)
     count = len(blocks)
 
     def kernel(*refs):
-        w_ref, gate_ref, up_ref, joined, d_gate_ref, d_up_ref = refs[count:]
+        w_ref, both_ref, joined, grad_ref = refs[count:]
         join_once(refs[:count], joined)
         d_hidden = lax.dot_general(
             joined[...], w_ref[...], (((1,), (1,)), ((), ())), preferred_element_type=F32
         )
         d_hidden = d_hidden.astype(BF16).astype(F32)
-        gate = gate_ref[...]
+        gate, up = both_ref[:, :tile], both_ref[:, tile:]
         open_gate = jax.nn.sigmoid(gate)
         part = d_hidden * open_gate
-        d_up_ref[...] = (part * gate).astype(BF16)
-        d_gate_ref[...] = (part * up_ref[...] * (1.0 + gate * (1.0 - open_gate))).astype(BF16)
-
-    outs = [jax.ShapeDtypeStruct((total, depth), BF16)]
-    outs += [jax.ShapeDtypeStruct((total, width), BF16)] * 2
+        grad_ref[:, :tile] = (part * up * (1.0 + gate * (1.0 - open_gate))).astype(BF16)
+        grad_ref[:, tile:] = (part * gate).astype(BF16)
+
+    outs = [
+        jax.ShapeDtypeStruct((total, depth), BF16),
+        jax.ShapeDtypeStruct((total, 2 * width), BF16),
+    ]
     return pl.pallas_call(
         kernel,
         grid=(width // tile,),
-        in_specs=whole + [pl.BlockSpec((tile, depth), lambda j: (j, 0)), cut, cut],
-        out_specs=[joined_spec, cut, cut],
+        in_specs=whole + [pl.BlockSpec((tile, depth), lambda j: (j, 0)), cut(2 * tile)],
+        out_specs=[joined_spec, cut(2 * tile)],
         out_shape=outs,
-        cost_estimate=cost((*blocks, weight, gate, up), outs, 2 * total * depth * width),
-        compiler_params=room(4 * total * depth, 4 * tile * depth, 40 * total * tile),
-    )(*blocks, weight, gate, up)
-
-
-def ffn_leave(d_gate, d_up, weight):
-    total, width = d_gate.shape
-    depth, tile = weight.shape[0], 256
-
-    def kernel(g_ref, u_ref, w_ref, out_ref):
-        nt = (((1,), (1,)), ((), ()))
-        out = lax.dot_general(g_ref[...], w_ref[:, :width], nt, preferred_element_type=F32)
-        out += lax.dot_general(u_ref[...], w_ref[:, width:], nt, preferred_element_type=F32)
-        out_ref[...] = out.astype(BF16)
-
-    out = jax.ShapeDtypeStruct((total, depth), BF16)
-    resident = pl.BlockSpec((total, width), lambda j: (0, 0), pipeline_mode=pl.Buffered(1))
-    return pl.pallas_call(
-        kernel,
-        grid=(depth // tile,),
-        in_specs=[resident, resident, pl.BlockSpec((tile, 2 * width), lambda j: (j, 0))],
-        out_specs=pl.BlockSpec((total, tile), lambda j: (0, j)),
-        out_shape=out,
-        cost_estimate=cost((d_gate, d_up, weight), [out], 4 * total * depth * width),
-        compiler_params=room(4 * total * width, 8 * tile * width, 12 * total * tile),
-    )(d_gate, d_up, weight)
+        cost_estimate=cost((*blocks, weight, both), outs, 2 * total * depth * width),
+        compiler_params=room(),
+    )(*blocks, weight, both)
 
 
 def after(value, *others):
@@ -295,12 +268,8 @@
     return pl.CostEstimate(flops=flops, bytes_accessed=moved, transcendentals=exps)
 
 
-def room(*sizes):
+def room():
     return pltpu.CompilerParams(vmem_limit_bytes=60 * MIB)
-
-
-def bytes_of(*arrays):
-    return sum(v.size * v.dtype.itemsize for v in arrays)
 
 
 def place_call(kernel, place, ins, outs, scratch=()):
@@ -312,7 +281,7 @@
         out_shape=outs,
         scratch_shapes=scratch,
         cost_estimate=cost(ins, outs),
-        compiler_params=room(bytes_of(*ins, *outs) * 3 // 2),
+        compiler_params=room(),
     )(place.reshape(1), *ins)
 
 
@@ -322,17 +291,25 @@
 
 def lanes_at(index, width):
     return pl.ds(pl.multiple_of(index * width, width), width)
+
+
+def run_of(width, parts):
+    return min(256, max(128, width // 4)) if parts == 2 else width
 
 
 def cut_columns(weight, parts, place, n):
     rows = weight.shape[0]
     width = weight.shape[1] // parts // n
+    run = run_of(width, parts)
 
     def kernel(place_ref, w_ref, *outs):
         for k in range(n):
             dest = shifted(place_ref, k, n)
-            for p in range(parts):
-                outs[k][:, p * width : (p + 1) * width] = w_ref[:, lanes_at(p * n + dest, width)]
+            for at in range(width // run):
+                for p in range(parts):
+                    to = (at * parts + p) * run
+                    start = pl.multiple_of((p * n + dest) * width + at * run, run)
+                    outs[k][:, to : to + run] = w_ref[:, pl.ds(start, run)]
 
     piece = jax.ShapeDtypeStruct((rows, parts * width), weight.dtype)
     return place_call(kernel, place, [weight], [piece] * n)
@@ -360,21 +337,22 @@
     return place_call(kernel, place, pieces, [whole])[0]
 
 
-def join_columns(lists, parts, place, dtype):
-    n = len(lists[0])
-    rows, width = lists[0][0].shape[0], lists[0][0].shape[1] // parts
+def join_columns(pieces, parts, place, dtype):
+    n = len(pieces)
+    rows, width = pieces[0].shape[0], pieces[0].shape[1] // parts
+    run = run_of(width, parts)
 
     def kernel(place_ref, *refs):
-        for i in range(len(lists)):
-            for k in range(n):
-                source = shifted(place_ref, -k, n)
+        for k in range(n):
+            source = shifted(place_ref, -k, n)
+            for at in range(width // run):
                 for p in range(parts):
-                    cut = refs[i * n + k][:, p * width : (p + 1) * width]
-                    here = lanes_at((i * parts + p) * n + source, width)
-                    refs[-1][:, here] = cut.astype(dtype)
-
-    whole = jax.ShapeDtypeStruct((rows, len(lists) * parts * n * width), dtype)
-    return place_call(kernel, place, [v for one in lists for v in one], [whole])[0]
+                    cut = refs[k][:, (at * parts + p) * run : (at * parts + p + 1) * run]
+                    start = pl.multiple_of((p * n + source) * width + at * run, run)
+                    refs[n][:, pl.ds(start, run)] = cut.astype(dtype)
+
+    whole = jax.ShapeDtypeStruct((rows, parts * n * width), dtype)
+    return place_call(kernel, place, pieces, [whole])[0]
 
 
 def send_one(pieces, k, *ties):
@@ -395,7 +373,7 @@
     width = weight.shape[1] // parts // n
     if n <= 8:
         return send_on(cut_columns(weight, parts, lax.axis_index("ctx"), n))
-    cut = weight.reshape(rows, parts, n, width).transpose(2, 0, 1, 3)
+    cut = weight.reshape(rows, parts, n, -1, run_of(width, parts)).transpose(2, 0, 3, 1, 4)
     return [lax.all_to_all(cut.reshape(n, rows, parts * width), "ctx", 0, 0, tiled=True)]
 
 
@@ -412,15 +390,12 @@
     return [lax.all_to_all(mine.reshape(n, -1, mine.shape[1]), "ctx", 0, 0, tiled=True)]
 
 
-def take_rows(lists, parts):
-    if len(lists[0]) > 1:
-        return join_columns(lists, parts, lax.axis_index("ctx"), F32)
-    wholes = []
-    for (sent,) in lists:
-        n, rows = sent.shape[:2]
-        got = sent.reshape(n, rows, parts, -1).transpose(1, 2, 0, 3)
-        wholes.append(got.reshape(rows, -1).astype(F32))
-    return jnp.concatenate(wholes, axis=1)
+def take_rows(sent, parts):
+    if len(sent) > 1:
+        return join_columns(sent, parts, lax.axis_index("ctx"), F32)
+    n, rows, columns = sent[0].shape
+    got = sent[0].reshape(n, rows, -1, parts, run_of(columns // parts, parts))
+    return got.transpose(1, 3, 0, 2, 4).reshape(rows, -1).astype(F32)
 
 
 def gather_groups(v):
@@ -474,7 +449,8 @@
     return spread_lanes(v, m, n)
 
 
-def sum_all(v):
+def sum_all(v, beside):
+    beside, made = list(beside), []
     for axis in ("ctx", "fsdp"):
         n = lax.axis_size(axis)
         if n & (n - 1):
@@ -482,9 +458,13 @@
             continue
         step = 1
         while step < n:
-            v = v + lax.ppermute(v, axis, [(i, i ^ step) for i in range(n)])
+            got = lax.ppermute(v, axis, [(i, i ^ step) for i in range(n)])
+            if beside:
+                got, now = lax.optimization_barrier((got, beside.pop(0)))
+                made.append(now)
+            v = v + got
             step *= 2
-    return v
+    return (v, made + beside)
 
 
 LANES = 128
@@ -648,8 +628,7 @@
 
 
 def out_kernel(
-    s_ref, c_ref, y_ref, y2a_ref, y2b_ref, y2c_ref, aux0_ref, aux1_ref, static_ref,
-    out_ref, red_ref,
+    s_ref, y_ref, y2a_ref, y2b_ref, y2c_ref, aux0_ref, aux1_ref, static_ref, out_ref
 ):
     coef0 = static_ref[0:1, :] + jnp.tanh(aux0_ref[...])
     coef1 = static_ref[1:2, :] + jnp.tanh(aux1_ref[...])
@@ -657,12 +636,11 @@
     y2 = sum_of((y2a_ref, y2b_ref, y2c_ref))
     for j, total in enumerate(mixed(mid, coef1, y2)):
         out_ref[:, j * D : (j + 1) * D] = total.astype(BF16)
-    red_ref[...] = leave_grads(mid, stream_parts(c_ref), y2)
 
 
 def back_kernel(
-    order, s_ref, c_ref, y_ref, dua_ref, dub_ref, duc_ref, red_ref, aux0_ref, aux1_ref, w_ref,
-    static_ref, dmid_ref, dy_ref, hc_ref, normed_ref, dz_ref, stat_ref,
+    order, s_ref, c_ref, y_ref, y2a_ref, y2b_ref, y2c_ref, dua_ref, dub_ref, duc_ref, aux0_ref,
+    aux1_ref, w_ref, static_ref, dmid_ref, dy_ref, hc_ref, normed_ref, dz_ref, stat_ref,
 ):
     step = pl.program_id(0)
 
@@ -675,8 +653,10 @@
     coef1 = static_ref[1:2, :] + jnp.tanh(aux1)
     mid = mixed(stream_parts(s_ref), coef0, y_ref[...])
     du = unspread_lanes(sum_of((dua_ref, dub_ref, duc_ref)), *order)
+    grads = stream_parts(c_ref)
+    red = leave_grads(mid, grads, sum_of((y2a_ref, y2b_ref, y2c_ref)))
     dmid = enter_back(
-        mid, stream_parts(c_ref), aux1, coef1, red_ref[...], du, w_ref[...],
+        mid, grads, aux1, coef1, red, du, w_ref[...],
         normed_ref, dz_ref, stat_ref, step,
     )
     for j in range(STREAMS):
@@ -722,7 +702,7 @@
 
 
 def row_call(kernel, rows, ins, outs, hc=False):
-    tile = HC_ROWS
+    tile = HC_ROWS if hc else min(rows, 2 * HC_ROWS)
 
     def cut(columns):
         return pl.BlockSpec((tile, columns), lambda i: (i, 0))
@@ -750,7 +730,7 @@
         out_shape=out_shape,
         scratch_shapes=scratch,
         cost_estimate=cost([a for a, _ in ins], out_shape, 100 * rows * STREAMS * D),
-        compiler_params=pltpu.CompilerParams(vmem_limit_bytes=60 * MIB),
+        compiler_params=room(),
     )(*[a for a, _ in ins])
 
 
@@ -761,7 +741,7 @@
     return jnp.concatenate([top, mid, across - top - mid, top], axis=0).astype(BF16)
 
 
-Q_ROWS = 256
+Q_ROWS = 512
 
 
 def turn(v, cosine, sine):
@@ -855,7 +835,7 @@
         out_specs=[by_query, by_query, by_query, by_head, by_head],
         out_shape=[low, wide, low, low, low],
         cost_estimate=cost([qkv], [low] * 4, 4 * heads * total**2 * HEAD_DIM, heads * total**2),
-        compiler_params=room(20 * Q_ROWS * total, 40 * total * HEAD_DIM),
+        compiler_params=room(),
     )(qkv, qkv, qkv, *marks)
 
 
@@ -871,7 +851,7 @@
         out_shape=[low, low, low],
         scratch_shapes=[pltpu.VMEM((total, HEAD_DIM), F32)] * 2,
         cost_estimate=cost([lse], [low] * 7, 10 * heads * total**2 * HEAD_DIM, heads * total**2),
-        compiler_params=room(32 * Q_ROWS * total, 48 * total * HEAD_DIM),
+        compiler_params=room(),
     )(query, keys, values, d_out, lse, *marks)
 
 
@@ -893,7 +873,7 @@
         cosine, sine = angles(position - start)
         kpos = jnp.broadcast_to(position[None, :], (8, position.shape[0]))
         self.marks = (cosine, sine, position[:, None], start[:, None], kpos)
-        self.sent_qkv = send_columns(w_qkv, 3)
+        self.cut_qkv = cut_columns(w_qkv, 3, lax.axis_index("ctx"), n)
         self.w_out = w_out
 
     def to_tokens(self, heads_out):
@@ -929,62 +909,62 @@
         n, m = lax.axis_size("ctx"), lax.axis_size("fsdp")
         got = {}
 
+        place = lax.axis_index("ctx")
         out_ctx = lax.all_gather(self.w_out, "ctx", axis=0, tiled=True)
-        u, sent_qkv = lax.optimization_barrier((u, self.sent_qkv))
+        cut = self.cut_qkv
+        sent_qkv = [cut[0], *[send_one(cut, k) for k in (1, 2)]]
+        sent_qkv += [send_one(cut, k, u) for k in range(3, n)]
 
         def early(step, arrived):
-            if step == 0:
-                got["own"] = take_columns(sent_qkv)
+            if step == 1:
+                arrived, sent, self.marks = lax.optimization_barrier(
+                    (arrived, sent_qkv, self.marks)
+                )
+                got["own"] = take_columns(sent)
                 got["far"] = far(got["own"])
-            if step == 1:
-                arrived, got["far"] = lax.optimization_barrier((arrived, got["far"]))
+                got["cut"] = cut_columns(after(w_gate_up, got["own"]), 2, place, n)
+            if step == 2:
+                arrived, got["far"], got["out"], got["cut"] = lax.optimization_barrier(
+                    (arrived, got["far"], out_ctx, got["cut"])
+                )
                 got["near"] = [near(got["own"]), near(got["far"])]
-            if step == 2:
-                arrived, got["near"], got["out"] = lax.optimization_barrier(
-                    (arrived, got["near"], out_ctx)
-                )
-                held = [got["own"], got["near"][0], got["far"], got["near"][1]]
-                got["cols"] = in_order(held)
-            if step == 3:
-                arrived, got["cols"] = lax.optimization_barrier((arrived, got["cols"]))
             return arrived
 
         blocks = ring_gather(u, early)
-        self.qkv_cols = got["cols"]
+        blocks, got["near"] = lax.optimization_barrier((blocks, got["near"]))
+        self.qkv_cols = in_order([got["own"], got["near"][0], got["far"], got["near"][1]])
         out_all = lax.all_gather(got["out"], "fsdp", axis=0, tiled=True)
         down_rows = gather_groups(after(w_down, *blocks))
-        cut = cut_columns(after(w_gate_up, *blocks), 2, lax.axis_index("ctx"), n)
+        cut, blocks = lax.optimization_barrier((got["cut"], blocks))
+        first = [send_one(cut, k) for k in (1, 2)]
         self.u_all, qkv = joined_dot(blocks, self.qkv_cols)
-        sent = [cut[0]] + [send_one(cut, k) for k in range(1, 4)]
+        qkv, first = lax.optimization_barrier((qkv, first))
+        second = [send_one(cut, k, qkv) for k in (3, 4)]
         self.o, self.lse, self.q, self.k, self.v = attend(qkv, self.heads, self.marks)
-        o, *sent = lax.optimization_barrier((self.o, *sent))
+        o, second = lax.optimization_barrier((self.o, second))
         sent_o = self.to_tokens(o)
-        sent += [send_one(cut, k, o) for k in range(4, n)]
+        sent = [cut[0], *first, *second, *[send_one(cut, k, o) for k in range(5, n)]]
         held = out_all.reshape(m, n, -1, D)
         held = lax.dynamic_slice_in_dim(held, lax.axis_index("ctx"), 1, 1)
         self.out_rows = held.reshape(-1, D)
         y = jnp.dot(self.join_tokens(sent_o), out_all, preferred_element_type=F32)
-        y, *sent[:6] = lax.optimization_barrier((y, *sent[:6]))
+        y, *sent[:5] = lax.optimization_barrier((y, *sent[:5]))
         return (y, sent, down_rows)
 
-    def backward(self, dy, grad_gate, grad_up):
+    def backward(self, dy, dy_blocks, grad_gate_up, grad_down):
         got = {}
 
-        def early_dy(step, arrived):
-            if step == 2:
-                arrived, got["gate"] = lax.optimization_barrier((arrived, grad_gate))
-            return arrived
-
-        blocks = ring_gather(dy, early_dy)
-        dy_all, d_out = joined_dot(blocks, self.out_rows, nt=True, dtype=BF16)
-        sent_gate = send_rows(after(got["gate"], dy_all))
-        d_out, grad_up = lax.optimization_barrier((d_out, grad_up))
+        dy_all, d_out = joined_dot(dy_blocks, self.out_rows, nt=True, dtype=BF16)
+        n, place = lax.axis_size("ctx"), lax.axis_index("ctx")
+        cut = cut_rows(after(grad_gate_up, dy_all), place, n)
+        first = [send_one(cut, k) for k in range(1, 4)]
         dq, dk, dv = attend_back(self.q, self.k, self.v, d_out, self.lse, self.heads, self.marks)
+        dq, first = lax.optimization_barrier((dq, first))
+        second = [send_one(cut, k, dq) for k in range(4, n)]
         d_qkv = jnp.concatenate([dq, dk, dv], axis=1)
         partial = jnp.einsum(
             "tc,dc->td", d_qkv, self.qkv_cols, preferred_element_type=F32
         ).astype(BF16)
-
 
         def early(step, arrived):
             if step == 0:
@@ -992,20 +972,25 @@
                 g = jnp.einsum("td,tc->dc", u_all, d_qkv, preferred_element_type=F32)
                 got["qkv"] = scatter_groups(g.astype(BF16))
             if step == 1:
+                arrived, got["second"] = lax.optimization_barrier((arrived, second))
                 o, dy_now = after([self.o, dy_all], arrived)
                 g = jnp.einsum("te,td->ed", o, dy_now, preferred_element_type=F32)
-                got["out"] = scatter_groups(g.astype(BF16)).astype(F32)
+                got["out"] = g.astype(BF16)
+            if step == 2:
+                arrived, got["out"], got["down"] = lax.optimization_barrier(
+                    (arrived, got["out"], grad_down)
+                )
             return arrived
 
         du = ring_scatter(partial, self.rows, early)
-        du, sent_gate = lax.optimization_barrier((du, sent_gate))
-        sent_up = send_rows(after(grad_up, du[1]))
-        sent_qkv = send_rows(after(got["qkv"], du[1]))
+        sent_qkv = send_rows(got["qkv"])
+        du, sent_qkv = lax.optimization_barrier((du, sent_qkv))
         return (
             du,
-            lambda tie: take_rows([after(sent_qkv, tie)], 3),
-            got["out"],
-            take_rows([sent_gate, sent_up], 1),
+            lambda tie: take_rows(after(sent_qkv, tie), 3),
+            scatter_groups(got["out"]).astype(F32),
+            take_rows([cut[0], *first, *got["second"]], 2),
+            got["down"].astype(F32),
         )
 
 
@@ -1061,7 +1046,7 @@
         y = jnp.dot(self.o, self.gathered(self.w_out), preferred_element_type=F32)
         return (y, send_columns(w_gate_up, 2), gather_groups(w_down))
 
-    def backward(self, dy, grad_gate, grad_up):
+    def backward(self, dy, dy_blocks, grad_gate_up, grad_down):
         rows = self.rows
         d_out = jnp.einsum(
             "td,ed->te", dy, self.gathered(self.w_out), preferred_element_type=F32
@@ -1098,7 +1083,8 @@
             (du,),
             lambda tie: grad_qkv,
             weight_share(grad_out, self.w_out.shape[0]),
-            take_rows([send_rows(g) for g in (grad_gate, grad_up)], 1),
+            take_rows(send_rows(grad_gate_up), 2),
+            grad_down.astype(F32),
         )
 
 
@@ -1146,19 +1132,20 @@
 
     def early_u2(step, arrived):
         if step == 0:
-            got["own"] = take_columns(sent_gate_up)
+            got["own"] = take_columns(sent)
             arrived, got["own"], got["down"] = lax.optimization_barrier(
                 (arrived, got["own"], down_rows)
             )
         return arrived
 
+    u2, sent = lax.optimization_barrier((u2, sent_gate_up))
     u2_blocks = ring_gather(u2, early_u2)
     gate_up_cols, down_rows = gather_groups(got["own"]), got["down"]
     width = FF // n
-    u2_all, gate, up, hidden = ffn_enter(u2_blocks, gate_up_cols)
+    u2_all, both, hidden = ffn_enter(u2_blocks, gate_up_cols)
 
     def early_dy2(step, arrived):
-        return after(arrived, gate) if step == 2 else arrived
+        return after(arrived, both) if step == 2 else arrived
 
     dy2_blocks = ring_gather(after(dy2, *u2_blocks[-2:]), early_dy2)
     y2_partial = jnp.dot(hidden, down_rows, preferred_element_type=F32).astype(BF16)
@@ -1166,69 +1153,76 @@
 
     def early_y2(step, arrived):
         if step == 0:
-            got["dy2_all"], got["d_gate"], got["d_up"] = ffn_back(
-                after(dy2_blocks, arrived), down_rows, gate, up
-            )
+            got["dy2_all"], got["dgu"] = ffn_back(after(dy2_blocks, arrived), down_rows, both)
         if step == 1:
-            d_gate, d_up = after([got["d_gate"], got["d_up"]], arrived)
-            got["du2"] = ffn_leave(d_gate, d_up, gate_up_cols)
+            dgu = after(got["dgu"], arrived)
+            got["du2"] = jnp.einsum(
+                "tg,dg->td", dgu, gate_up_cols, preferred_element_type=F32
+            ).astype(BF16)
         return arrived
 
     y2 = ring_scatter(y2_partial, rows, early_y2)
-    for name in ("gate", "up", "down"):
-        if name == "down":
-            left, right = hidden, got["dy2_all"]
-        else:
-            left, right = u2_all, got["d_" + name]
-        left = after(left, got["du2"], *[v for k, v in got.items() if k.startswith("grad_")])
-        g = jnp.einsum("td,tg->dg", left, right, preferred_element_type=F32)
-        got["grad_" + name] = g.astype(BF16)
-
-    def leave(terms):
-        return row_call(
-            out_kernel,
-            rows,
-            [
-                (state, True), (cot, True), (y, True), *[(v, True) for v in terms],
-                (aux0, True), (aux1, True), (static, False),
-            ],
-            [(STREAMS * D, BF16), (LANES, F32)],
-        )
 
     def early_du2(step, arrived):
+        if step == 0:
+            left = after(u2_all, got["du2"])
+            g = jnp.einsum("td,tg->dg", left, got["dgu"], preferred_element_type=F32)
+            got["gate_up"] = g.astype(BF16)
         if step == 1:
-            arrived, y2_all = lax.optimization_barrier((arrived, tuple(y2)))
-            got["y2"] = y2_all
+            arrived, got["y2"] = lax.optimization_barrier((arrived, tuple(y2)))
         if step == 2:
-            arrived, got["grad_gate"], got["grad_up"] = lax.optimization_barrier(
-                (arrived, got["grad_gate"], got["grad_up"])
-            )
-            got["out"] = leave(got["y2"])
-        if step == 3:
-            arrived, got["out"], got["grad_down"] = lax.optimization_barrier(
-                (arrived, got["out"], got["grad_down"])
-            )
+            arrived, got["gate_up"] = lax.optimization_barrier((arrived, got["gate_up"]))
         return arrived
 
     du2 = ring_scatter(got["du2"], rows, early_du2)
-    if "out" not in got:
-        got["out"] = leave(y2)
-    out, red1 = got["out"]
-    grad_gate, grad_up = [scatter_groups(got[k]) for k in ("grad_gate", "grad_up")]
-    grad_down = scatter_groups(got["grad_down"]).astype(F32)
+    y2 = got["y2"] if "y2" in got else y2
+    grad_gate_up = scatter_groups(got["gate_up"])
     dmid, dy, hc1 = row_call(
         functools.partial(back_kernel, order),
         rows,
         [
-            (state, True), (cot, True), (y, True), *[(v, True) for v in du2], (red1, True),
-            (aux0, True), (aux1, True), (wpack1, False), (static, False),
+            (state, True), (cot, True), (y, True), *[(v, True) for v in y2],
+            *[(v, True) for v in du2], (aux0, True), (aux1, True), (wpack1, False),
+            (static, False),
         ],
         [(STREAMS * D, F32), (D, BF16)],
         hc=True,
     )
-    red0 = row_call(red_kernel, rows, [(state, True), (dmid, True), (y, True)], [(LANES, F32)])[0]
-    du, take_grad_qkv, grad_out, grad_gate_up = attention.backward(dy, grad_gate, grad_up)
-    du, grad_down = lax.optimization_barrier((du, grad_down))
+    left = after(hidden, dy)
+    g = jnp.einsum("tf,td->fd", left, got["dy2_all"], preferred_element_type=F32).astype(BF16)
+    terms = after(list(y2), g)
+    out = row_call(
+        out_kernel,
+        rows,
+        [
+            (state, True), (y, True), *[(v, True) for v in terms], (aux0, True), (aux1, True),
+            (static, False),
+        ],
+        [(STREAMS * D, BF16)],
+    )[0]
+    red0 = row_call(
+        red_kernel, rows, [(after(state, out), True), (dmid, True), (y, True)], [(LANES, F32)]
+    )[0]
+    held = {}
+
+    def early_dy(step, arrived):
+        if step == 1:
+            arrived, held["down"] = lax.optimization_barrier((arrived, g))
+        if step == 2:
+            arrived, held["out"] = lax.optimization_barrier((arrived, out))
+        if step == 3:
+            arrived, held["gate_up"], held["red0"] = lax.optimization_barrier(
+                (arrived, grad_gate_up, red0)
+            )
+        return arrived
+
+    dy_blocks = ring_gather(dy, early_dy)
+    out, red0 = held.get("out", out), held.get("red0", red0)
+    grad_gate_up = held.get("gate_up", grad_gate_up)
+    grad_down = scatter_groups(held.get("down", g))
+    du, take_grad_qkv, grad_out, grad_gate_up, grad_down = attention.backward(
+        dy, dy_blocks, grad_gate_up, grad_down
+    )
     grad_state, hc0 = row_call(
         functools.partial(last_kernel, own_order),
         rows,
@@ -1239,8 +1233,12 @@
         [(STREAMS * D, BF16)],
         hc=True,
     )
-    grad_qkv = take_grad_qkv(hc0)
-    hc = sum_all(jnp.concatenate([hc0, hc1], axis=0)).reshape(2, 8, D)
+    hc, beside = sum_all(
+        jnp.concatenate([hc0, hc1], axis=0),
+        (grad_down, grad_gate_up, take_grad_qkv(hc0), grad_out),
+    )
+    grad_down, grad_gate_up, grad_qkv, grad_out = beside
+    hc = hc.reshape(2, 8, D)
     grad_hc_weight = hc[:, 0:6].transpose(0, 2, 1)
     grad_hc_static = hc[:, 6, : 8 * STREAMS].reshape(2, STREAMS, 8)[:, :, 0:6]
     return (

time: 714 us -> 696 us (0.975)
  Pallas kernels: 180 us -> 160 us
  waiting for transfers between devices: 253 us -> 237 us
  starting transfers between devices: 143 us -> 158 us
  matrix products: 58.2 us -> 65.7 us
    ppermute x16, waiting for transfers between devices: 91.9 us -> 58.6 us  [ring_gather(): lax.ppermute(moving[1], 'ctx', back)]
    ppermute x16, starting transfers between devices: 12.5 us -> 38.2 us  [ring_gather(): lax.ppermute(moving[0], 'ctx', ahead)]
    ppermute x35 -> x28, starting transfers between devices: 66.9 us -> 46.4 us  [send_one(): lax.ppermute(after(pieces[k], *ties), 'ctx', [(i, (i + k) % n) for i in r...]
    pallas_call x2 -> x1, Pallas kernels: 28.3 us -> 14.2 us  [ffn_enter(): pl.pallas_call(kernel, grid=(width // tile,), in_specs=whole + [pl.BlockS...]
    ppermute x16, starting transfers between devices: 25.9 us -> 13.5 us  [ring_gather(): lax.ppermute(moving[1], 'ctx', back)]
    ppermute x12, starting transfers between devices: 13 us -> 22.1 us  [ring_scatter(): lax.ppermute(moving[0], 'ctx', ahead)]
    ppermute x35 -> x28, waiting for transfers between devices: 64.2 us -> 72.3 us  [send_one(): lax.ppermute(after(pieces[k], *ties), 'ctx', [(i, (i + k) % n) for i in r...]
    dot_general x3, matrix products: 28 us -> 35.9 us  [the longest x1 14 us: early_du2(): g = jnp.einsum('td,tg->dg', left, got['dgu'], preferred_element_type=F32)]
  transfers between devices with their start and end apart: 115 -> 107, of which waited for: 54 -> 53; matrix products, arithmetic and copies ran while one was open for 13% -> 14% of each run, Pallas kernels for 24% -> 22%
where the time goes in v3:
time: 696 us; the launch traced here: 687 us
  waiting for transfers between devices  237 us (34%)
  Pallas kernels  160 us (23%)
  starting transfers between devices  158 us (23%)
  matrix products  65.7 us (9%)
  local copies, waits for them, and re-layouts  40.6 us (6%)
  between operations  15.8 us (2%)
  other arithmetic  10.5 us (2%)
    ppermute x28, waiting for transfers between devices, send_one(): lax.ppermute(after(pieces[k], *ties), 'ctx', [(i, (i + k) % n) for i in r...  72.3 us
    ppermute x16, waiting for transfers between devices, ring_gather(): lax.ppermute(moving[1], 'ctx', back)  58.6 us
    pallas_call x6, Pallas kernels, row_call(): pl.pallas_call(kernel, grid=(rows // tile,), in_specs=in_specs, out_specs...  51 us
    ppermute x28, starting transfers between devices, send_one(): lax.ppermute(after(pieces[k], *ties), 'ctx', [(i, (i + k) % n) for i in r...  46.4 us
    ppermute x16, waiting for transfers between devices, ring_gather(): lax.ppermute(moving[0], 'ctx', ahead)  42.3 us
    ppermute x16, starting transfers between devices, ring_gather(): lax.ppermute(moving[0], 'ctx', ahead)  38.2 us
    ppermute x12, waiting for transfers between devices, ring_scatter(): lax.ppermute(moving[0], 'ctx', ahead)  27.8 us
    pallas_call x9, Pallas kernels, place_call(): pl.pallas_call(kernel, in_specs=[pl.BlockSpec(memory_space=pltpu.SMEM)] +...  24 us
  transfers between devices with their start and end apart: 107, of which 53 were waited for; matrix products, arithmetic and copies ran while one was open for 14% of the time, Pallas kernels for 22%

profile of v3, /device:TPU:0, one launch (start us, length us, event | category | flops | bytes accessed | tf_op | source)
XLA Modules:
  0.0 687.5 jit_solution(11682499571574827608)
XLA Ops:
  11.4 6.4 shard_map.179
  17.8 2.9 collective-permute-start.2
  23.0 4.9 collective-permute-start.10
  30.7 11.5 %collective-permute-done.2.refs_2_ = bf16[128,2048]{1,0:T(8,128)(2,1)S(1)} collective-permute-done((bf16[128,2048]{1,0:T(8,128)(2,1)}, bf16[128,2048]{1,0:T(8,128)(2,1)S(1)}, u32[]{:S(2)}, u32[]{:S(2)}) %collective-permute-start.2) | collective-permute-done | bytes 524320 | tf_op jit(solution)/shard_map/ppermute | solution.py:78
  43.0 6.5 collective-permute-start.1
  56.9 28.5 %collective-permute-done.7.refs_4_ = bf16[64,768]{1,0:T(8,128)(2,1)S(1)} collective-permute-done((bf16[64,768]{1,0:T(8,128)(2,1)}, bf16[64,768]{1,0:T(8,128)(2,1)S(1)}, u32[]{:S(2)}, u32[]{:S(2)}) %collective-permute-start.7) | collective-permute-done | bytes 98336 | tf_op jit(solution)/shard_map/ppermute | solution.py:360
  87.6 4.4 collective-permute-done.5.refs_2_
  98.4 3.2 shard_map.182
  101.6 6.3 collective-permute-done.11.refs_5_
  108.6 3.6 collective-permute-done.13
  116.9 6.3 collective-permute-done.15.refs_8_
  131.4 8.1 %shard_map.183 = (bf16[1024,2048]{1,0:T(8,128)(2,1)}, f32[1024,768]{1,0:T(8,128)}) custom-call(bf16[128,2048]{1,0:T(8,128)(2,1)} %get-tuple-element.330.refs_0_, bf16[128,2048]{1,0:T(8,128)(2,1)} %copy-done.90, bf16[128,2048]{1,0:T(8,128)(2,1)} %copy-done.89, bf16[128,2048]{1,0:T(8,128)(2,1)} %collective-permute-done.1.refs_3_, ...), custom_call_target="tpu_custom_call" | custom-call | flops 3221225472 | bytes 14680064 | tf_op jit(solution)/shard_map/pallas_call | solution.py:165
  147.3 10.7 %shard_map.184 = (bf16[1024,256]{1,0:T(8,128)(2,1)}, f32[1024,256]{1,0:T(8,128)}, bf16[1024,256]{1,0:T(8,128)(2,1)}, bf16[1024,256]{1,0:T(8,128)(2,1)}, bf16[1024,256]{1,0:T(8,128)(2,1)}) custom-call(f32[1024,768]{1,0:T(8,128)} %get-tuple-element.344.q_ref.k_ref.v_ref, f32[1024,768]{1,0:T(8,128)} %get-tuple-element.344.q_ref.k_ref.v_ref, ...), custom_call_target="tpu_custom_call" | custom-call | flops 1073741824 | bytes 5242880 | tf_op jit(solution)/shard_map/pallas_call | solution.py:831
  162.8 7.7 %collective-permute-start.28 = (bf16[128,256]{1,0:T(8,128)(2,1)S(1)}, bf16[128,256]{1,0:T(8,128)(2,1)S(1)}, u32[]{:S(2)}, u32[]{:S(2)}) collective-permute-start(bf16[128,256]{1,0:T(8,128)(2,1)S(1)} %get-tuple-element.552), channel_id=1, source_target_pairs={{0,28},{8,20},{16,12},{24,4},{28,0},{20,8},{12,16},{4,24},{1,29},{... | collective-permute-start | bytes 196616 | tf_op jit(solution)/shard_map/ppermute | solution.py:887
  170.6 3.9 collective-permute-start.26
  187.7 5.8 fusion.13.y_ref
  193.6 9.1 %shard_map.186 = (bf16[128,2048]{1,0:T(8,128)(2,1)}, bf16[128,2048]{1,0:T(8,128)(2,1)}, f32[128,128]{1,0:T(8,128)}) custom-call(bf16[128,8192]{1,0:T(8,128)(2,1)} %bitcast.67, bf16[128,8192]{1,0:T(8,128)(2,1)} %bitcast.73, f32[128,2048]{1,0:T(8,128)} %fusion.13.y_ref, f32[128,128]{1,0:T(8,128)} %get-tuple-element.363.aux0_ref.refs_4_, ...), custom_call_target="tpu_custom_call" | custom-call | flops 104857600 | bytes 6950912 | tf_op jit(solution)/shard_map/pallas_call | solution.py:725
  203.2 13.3 %collective-permute-start.32 = (bf16[128,2048]{1,0:T(8,128)(2,1)}, bf16[128,2048]{1,0:T(8,128)(2,1)S(1)}, u32[]{:S(2)}, u32[]{:S(2)}) collective-permute-start(bf16[128,2048]{1,0:T(8,128)(2,1)} %get-tuple-element.376.refs_0_), channel_id=1, source_target_pairs={{0,8},{8,16},{16,24},{24,28},{28,20},{20,12},{12,4},{4,0},{1,9},{9... | collective-permute-start | bytes 1572872 | tf_op jit(solution)/shard_map/ppermute | solution.py:78
  216.6 3.0 shard_map.187
  219.5 7.6 %collective-permute-done.33.refs_2_ = bf16[128,2048]{1,0:T(8,128)(2,1)S(1)} collective-permute-done((bf16[128,2048]{1,0:T(8,128)(2,1)}, bf16[128,2048]{1,0:T(8,128)(2,1)S(1)}, u32[]{:S(2)}, u32[]{:S(2)}) %collective-permute-start.33) | collective-permute-done | bytes 524320 | tf_op jit(solution)/shard_map/ppermute | solution.py:78
  228.9 3.0 collective-permute-start.34
  231.9 11.2 %collective-permute-done.34.refs_3_ = bf16[128,2048]{1,0:T(8,128)(2,1)S(1)} collective-permute-done((bf16[128,2048]{1,0:T(8,128)(2,1)S(1)}, bf16[128,2048]{1,0:T(8,128)(2,1)S(1)}, u32[]{:S(2)}, u32[]{:S(2)}) %collective-permute-start.34) | collective-permute-done | bytes 524320 | tf_op jit(solution)/shard_map/ppermute | solution.py:78
  245.5 8.3 %collective-permute-done.36.refs_5_ = bf16[128,2048]{1,0:T(8,128)(2,1)S(1)} collective-permute-done((bf16[128,2048]{1,0:T(8,128)(2,1)S(1)}, bf16[128,2048]{1,0:T(8,128)(2,1)S(1)}, u32[]{:S(2)}, u32[]{:S(2)}) %collective-permute-start.36) | collective-permute-done | bytes 524320 | tf_op jit(solution)/shard_map/ppermute | solution.py:78
  257.5 5.6 collective-permute-done.38.refs_7_
  266.0 9.5 %collective-permute-done.41.refs_2_ = bf16[128,2048]{1,0:T(8,128)(2,1)S(1)} collective-permute-done((bf16[128,2048]{1,0:T(8,128)(2,1)S(1)}, bf16[128,2048]{1,0:T(8,128)(2,1)S(1)}, u32[]{:S(2)}, u32[]{:S(2)}) %collective-permute-start.41) | collective-permute-done | bytes 524320 | tf_op jit(solution)/shard_map/ppermute | solution.py:78
  277.6 8.8 %collective-permute-done.43.refs_4_ = bf16[128,2048]{1,0:T(8,128)(2,1)S(1)} collective-permute-done((bf16[128,2048]{1,0:T(8,128)(2,1)S(1)}, bf16[128,2048]{1,0:T(8,128)(2,1)S(1)}, u32[]{:S(2)}, u32[]{:S(2)}) %collective-permute-start.43) | collective-permute-done | bytes 524320 | tf_op jit(solution)/shard_map/ppermute | solution.py:78
  290.2 14.2 %shard_map.188 = (bf16[1024,2048]{1,0:T(8,128)(2,1)}, f32[1024,2048]{1,0:T(8,128)}, bf16[1024,1024]{1,0:T(8,128)(2,1)}) custom-call(bf16[128,2048]{1,0:T(8,128)(2,1)} %get-tuple-element.376.refs_0_, bf16[128,2048]{1,0:T(8,128)(2,1)} %copy-done.92, bf16[128,2048]{1,0:T(8,128)(2,1)} %copy-done.91, bf16[128,2048]{1,0:T(8,128)(2,1)} %copy-done.93, ...), custom_call_target="tpu_custom_call" | custom-call | flops 8589934592 | bytes 27262976 | tf_op jit(solution)/shard_map/pallas_call | solution.py:218
  306.9 7.3 %convolution_convert_fusion.4.one_own.other_own.y2a_ref = bf16[1024,2048]{1,0:T(8,128)(2,1)S(1)} fusion(bf16[1024,1024]{1,0:T(8,128)(2,1)} %get-tuple-element.440, bf16[1024,2048]{1,0:T(8,128)(2,1)} %all-gather.9.cloned.1.call-done.refs_9_), kind=kOutput, calls=%fused_computation.4 | convolution fusion | flops 4297064448 | bytes 10485760 | tf_op jit(solution)/shard_map/dot_general | solution.py:1151
  318.4 4.3 collective-permute-done.49.other_ref
  329.8 11.2 %shard_map.189 = (bf16[1024,2048]{1,0:T(8,128)(2,1)}, bf16[1024,2048]{1,0:T(8,128)(2,1)}) custom-call(bf16[128,2048]{1,0:T(8,128)(2,1)} %get-tuple-element.406.refs_0_, bf16[128,2048]{1,0:T(8,128)(2,1)} %copy-done.14, bf16[128,2048]{1,0:T(8,128)(2,1)} %copy-done.13, bf16[128,2048]{1,0:T(8,128)(2,1)} %copy-done.16, bf16[128,2048]{1,0:T(8,128)(2,1)} %copy-done.15, ...), custom_call_target="tpu_custom_call" | custom-call | flops 4294967296 | bytes 25165824 | tf_op jit(solution)/shard_map/pallas_call | solution.py:251
  346.7 12.6 %convolution_convert_fusion.1.one_own.other_own.dua_ref = bf16[1024,2048]{1,0:T(8,128)(2,1)S(1)} fusion(bf16[1024,2048]{1,0:T(8,128)(2,1)} %get-tuple-element.418, bf16[2048,2048]{1,0:T(8,128)(2,1)} %all-gather.11.cloned.1.call-done.refs_9_), kind=kOutput, calls=%fused_computation.1 | convolution fusion | flops 8592031744 | bytes 16777216 | tf_op jit(solution)/shard_map/tg,dg->td/dot_general | solution.py:1159
  363.4 4.3 collective-permute-done.53.other_ref
  380.9 6.0 collective-permute-done.54.one_ref
  387.6 4.9 collective-permute-done.58.y2b_ref
  398.2 14.0 %convolution_convert_fusion = bf16[2048,2048]{1,0:T(8,128)(2,1)} fusion(bf16[1024,2048]{1,0:T(8,128)(2,1)} %get-tuple-element.433, bf16[1024,2048]{1,0:T(8,128)(2,1)} %get-tuple-element.418), kind=kOutput, calls=%fused_computation | convolution fusion | flops 8594128896 | bytes 16777216 | tf_op jit(solution)/shard_map/td,tg->dg/dot_general | solution.py:1169
  417.8 7.4 %collective-permute-done.62.dub_ref = bf16[128,2048]{1,0:T(8,128)(2,1)S(1)} collective-permute-done((bf16[128,2048]{1,0:T(8,128)(2,1)}, bf16[128,2048]{1,0:T(8,128)(2,1)S(1)}, u32[]{:S(2)}, u32[]{:S(2)}) %collective-permute-start.62) | collective-permute-done | bytes 524320 | tf_op jit(solution)/shard_map/ppermute | solution.py:121
  427.4 13.8 %shard_map.196 = (f32[128,8192]{1,0:T(8,128)}, bf16[128,2048]{1,0:T(8,128)(2,1)}, f32[8,2048]{1,0:T(8,128)}) custom-call(bf16[128,8192]{1,0:T(8,128)(2,1)} %bitcast.68, bf16[128,8192]{1,0:T(8,128)(2,1)} %bitcast.74, f32[128,2048]{1,0:T(8,128)} %fusion.13.y_ref, bf16[1024,2048]{1,0:T(8,128)(2,1)} %copy-done.2, bf16[128,2048]{1,0:T(8,128)(2,1)} %copy-done.5, ...), custom_call_target="tpu_custom_call" | custom-call | flops 104857600 | bytes 21172224 | tf_op jit(solution)/shard_map/pallas_call | solution.py:725
  443.3 11.9 %collective-permute-done.66.refs_2_ = bf16[128,2048]{1,0:T(8,128)(2,1)S(1)} collective-permute-done((bf16[128,2048]{1,0:T(8,128)(2,1)}, bf16[128,2048]{1,0:T(8,128)(2,1)S(1)}, u32[]{:S(2)}, u32[]{:S(2)}) %collective-permute-start.66) | collective-permute-done | bytes 524320 | tf_op jit(solution)/shard_map/ppermute | solution.py:78
  457.5 9.4 %convolution_convert_fusion.3 = bf16[1024,2048]{1,0:T(8,128)(2,1)} fusion(bf16[1024,1024]{1,0:T(8,128)(2,1)} %get-tuple-element.440, bf16[1024,2048]{1,0:T(8,128)(2,1)} %get-tuple-element.441), kind=kOutput, calls=%fused_computation.3 | convolution fusion | flops 4297064448 | bytes 10485760 | tf_op jit(solution)/shard_map/tf,td->fd/dot_general | solution.py:1192
  467.8 2.9 collective-permute-done.65.refs_3_
  472.9 6.9 %shard_map.197 = bf16[128,8192]{1,0:T(8,128)(2,1)} custom-call(bf16[128,8192]{1,0:T(8,128)(2,1)} %bitcast.69, f32[128,2048]{1,0:T(8,128)} %fusion.13.y_ref, bf16[1024,2048]{1,0:T(8,128)(2,1)} %copy-done.2, bf16[128,2048]{1,0:T(8,128)(2,1)} %copy-done.5, bf16[128,2048]{1,0:T(8,128)(2,1)} %copy-done.6, f32[128,128]{1,0:T(8,128)} %get-tuple-element.363.aux0_ref.refs_4_, ...), custom_call_target="tpu_custom_call" | custom-call | flops 104857600 | bytes 10620928 | tf_op jit(solution)/shard_map/pallas_call | solution.py:725
  479.8 2.9 collective-permute-done.68.refs_5_
  487.2 4.7 shard_map.198.refs_3_
  492.6 6.4 shard_map.199
  499.1 3.1 shard_map.201
  506.7 11.4 %shard_map.200 = (bf16[1024,256]{1,0:T(8,128)(2,1)}, bf16[1024,256]{1,0:T(8,128)(2,1)}, bf16[1024,256]{1,0:T(8,128)(2,1)}) custom-call(bf16[1024,256]{1,0:T(8,128)(2,1)} %get-tuple-element.449.q_ref, bf16[1024,256]{1,0:T(8,128)(2,1)} %get-tuple-element.450.k_ref, bf16[1024,256]{1,0:T(8,128)(2,1)} %get-tuple-element.451.v_ref, ...), custom_call_target="tpu_custom_call" | custom-call | flops 2684354560 | bytes 4718592 | tf_op jit(solution)/shard_map/pallas_call | solution.py:846
  524.1 7.2 %convolution_convert_fusion.2.one_own.other_own.refs_0_ = bf16[1024,2048]{1,0:T(8,128)(2,1)} fusion(bf16[1024,768]{1,0:T(8,128)(2,1)S(1)} %constant_dynamic-update-slice_fusion, bf16[2048,768]{1,0:T(8,128)(2,1)} %bitcast.16.refs_9_), kind=kOutput, calls=%fused_computation.2 | convolution fusion | flops 3223322624 | bytes 8912896 | tf_op jit(solution)/shard_map/tc,dc->td/dot_general | solution.py:965
  531.3 5.0 convolution_convert_fusion.5
  539.6 6.0 collective-permute-done.76.other_ref
  549.5 4.1 collective-permute-start.77
  553.5 4.3 collective-permute-start.80
  560.5 13.2 %collective-permute-done.80.refs_5_ = bf16[64,2048]{1,0:T(8,128)(2,1)S(1)} collective-permute-done((bf16[64,2048]{1,0:T(8,128)(2,1)S(1)}, bf16[64,2048]{1,0:T(8,128)(2,1)S(1)}, u32[]{:S(2)}, u32[]{:S(2)}) %collective-permute-start.80) | collective-permute-done | bytes 262176 | tf_op jit(solution)/shard_map/ppermute | solution.py:360
  573.7 4.7 collective-permute-done.81.refs_6_
  582.6 10.9 %collective-permute-start.83 = (bf16[128,2048]{1,0:T(8,128)(2,1)}, bf16[128,2048]{1,0:T(8,128)(2,1)S(1)}, u32[]{:S(2)}, u32[]{:S(2)}) collective-permute-start(bf16[128,2048]{1,0:T(8,128)(2,1)} %get-tuple-element.482), channel_id=1, source_target_pairs={{0,8},{8,16},{16,24},{24,28},{28,20},{20,12},{12,4},{4,0},{1,9},{9... | collective-permute-start | bytes 1572872 | tf_op jit(solution)/shard_map/ppermute | solution.py:121
  593.5 4.5 convolution_convert_fusion.6
  598.0 5.3 collective-permute-done.83.one_ref
  615.1 4.2 collective-permute-start.89
  619.2 9.6 %collective-permute-done.88.refs_2_ = bf16[64,768]{1,0:T(8,128)(2,1)S(1)} collective-permute-done((bf16[64,768]{1,0:T(8,128)(2,1)}, bf16[64,768]{1,0:T(8,128)(2,1)S(1)}, u32[]{:S(2)}, u32[]{:S(2)}) %collective-permute-start.88) | collective-permute-done | bytes 98336 | tf_op jit(solution)/shard_map/ppermute | solution.py:360
  634.7 3.0 collective-permute-start.93
  641.5 10.1 %shard_map.206 = (bf16[128,8192]{1,0:T(8,128)(2,1)}, f32[8,2048]{1,0:T(8,128)}) custom-call(bf16[128,8192]{1,0:T(8,128)(2,1)} %bitcast.71, f32[128,8192]{1,0:T(8,128)} %get-tuple-element.448.dmid_ref, bf16[1024,2048]{1,0:T(8,128)(2,1)} %convolution_convert_fusion.2.one_own.other_own.refs_0_, bf16[128,2048]{1,0:T(8,128)(2,1)} %copy-done.18, ...), custom_call_target="tpu_custom_call" | custom-call | flops 104857600 | bytes 14356480 | tf_op jit(solution)/shard_map/pallas_call | solution.py:725
  652.5 3.0 collective-permute-start.94
  658.8 3.8 shard_map.207
  667.4 3.4 collective-permute-done.96
  673.4 5.2 collective-permute-done.98
  (487 shorter events, 204.8 us)
Async XLA Ops:
  7.2 105.0 %all-gather.5.cloned.1.call-start = ((), (), s32[]{:S(2)}) async-start(), calls=%async_computation.4 | async-start | bytes 2359296 | tf_op jit(solution)/shard_map/all_gather | solution.py:913
  8.0 179.8 %all-gather.7.cloned.1.call-start = ((), (), s32[]{:S(2)}) async-start(), calls=%async_computation.5 | async-start | bytes 10485760 | tf_op jit(solution)/shard_map/all_gather | solution.py:936
  17.8 24.4 %collective-permute-start.2 = (bf16[128,2048]{1,0:T(8,128)(2,1)}, bf16[128,2048]{1,0:T(8,128)(2,1)S(1)}, u32[]{:S(2)}, u32[]{:S(2)}) collective-permute-start(bf16[128,2048]{1,0:T(8,128)(2,1)} %get-tuple-element.330.refs_0_), channel_id=1, source_target_pairs={{8,0},{16,8},{24,16},{28,24},{20,28},{12,20},{4,12},{0,4},{9,1},{1... | collective-permute-start | bytes 1572872 | tf_op jit(solution)/shard_map/ppermute | solution.py:78
  20.7 22.3 %collective-permute-start = (bf16[128,2048]{1,0:T(8,128)(2,1)}, bf16[128,2048]{1,0:T(8,128)(2,1)S(1)}, u32[]{:S(2)}, u32[]{:S(2)}) collective-permute-start(bf16[128,2048]{1,0:T(8,128)(2,1)} %get-tuple-element.330.refs_0_), channel_id=1, source_target_pairs={{0,8},{8,16},{16,24},{24,28},{28,20},{20,12},{12,4},{4,0},{1,9},{9... | collective-permute-start | bytes 1572872 | tf_op jit(solution)/shard_map/ppermute | solution.py:78
  23.0 26.6 %collective-permute-start.10 = (bf16[64,768]{1,0:T(8,128)(2,1)}, bf16[64,768]{1,0:T(8,128)(2,1)S(1)}, u32[]{:S(2)}, u32[]{:S(2)}) collective-permute-start(bf16[64,768]{1,0:T(8,128)(2,1)} %get-tuple-element.290), channel_id=1, source_target_pairs={{0,28},{4,0},{8,4},{12,8},{16,12},{20,16},{24,20},{28,24},{1,29},{... | collective-permute-start | bytes 294920 | tf_op jit(solution)/shard_map/ppermute | solution.py:360
  27.9 26.3 %collective-permute-start.9 = (bf16[64,768]{1,0:T(8,128)(2,1)}, bf16[64,768]{1,0:T(8,128)(2,1)S(1)}, u32[]{:S(2)}, u32[]{:S(2)}) collective-permute-start(bf16[64,768]{1,0:T(8,128)(2,1)} %get-tuple-element.288), channel_id=1, source_target_pairs={{0,24},{4,28},{8,0},{12,4},{16,8},{20,12},{24,16},{28,20},{1,25},{... | collective-permute-start | bytes 294920 | tf_op jit(solution)/shard_map/ppermute | solution.py:360
  28.4 26.0 %collective-permute-start.8 = (bf16[64,768]{1,0:T(8,128)(2,1)}, bf16[64,768]{1,0:T(8,128)(2,1)S(1)}, u32[]{:S(2)}, u32[]{:S(2)}) collective-permute-start(bf16[64,768]{1,0:T(8,128)(2,1)} %get-tuple-element.286), channel_id=1, source_target_pairs={{0,20},{4,24},{8,28},{12,0},{16,4},{20,8},{24,12},{28,16},{1,21},{... | collective-permute-start | bytes 294920 | tf_op jit(solution)/shard_map/ppermute | solution.py:360
  42.2 49.8 %collective-permute-start.3 = (bf16[128,2048]{1,0:T(8,128)(2,1)S(1)}, bf16[128,2048]{1,0:T(8,128)(2,1)}, u32[]{:S(2)}, u32[]{:S(2)}) collective-permute-start(bf16[128,2048]{1,0:T(8,128)(2,1)S(1)} %collective-permute-done.2.refs_2_), channel_id=1, source_target_pairs={{8,0},{16,8},{24,16},{28,24},{20,28},{12,20},{4,12},{0,4},{9,1},{1... | collective-permute-start | bytes 1572872 | tf_op jit(solution)/shard_map/ppermute | solution.py:78
  43.0 49.0 %collective-permute-start.1 = (bf16[128,2048]{1,0:T(8,128)(2,1)S(1)}, bf16[128,2048]{1,0:T(8,128)(2,1)}, u32[]{:S(2)}, u32[]{:S(2)}) collective-permute-start(bf16[128,2048]{1,0:T(8,128)(2,1)S(1)} %collective-permute-done.refs_1_), channel_id=1, source_target_pairs={{0,8},{8,16},{16,24},{24,28},{28,20},{20,12},{12,4},{4,0},{1,9},{9... | collective-permute-start | bytes 1572872 | tf_op jit(solution)/shard_map/ppermute | solution.py:78
  49.6 35.8 %collective-permute-start.7 = (bf16[64,768]{1,0:T(8,128)(2,1)}, bf16[64,768]{1,0:T(8,128)(2,1)S(1)}, u32[]{:S(2)}, u32[]{:S(2)}) collective-permute-start(bf16[64,768]{1,0:T(8,128)(2,1)} %get-tuple-element.284), channel_id=1, source_target_pairs={{0,16},{4,20},{8,24},{12,28},{16,0},{20,4},{24,8},{28,12},{1,17},{... | collective-permute-start | bytes 294920 | tf_op jit(solution)/shard_map/ppermute | solution.py:360
  54.2 33.4 %collective-permute-start.6 = (bf16[64,768]{1,0:T(8,128)(2,1)}, bf16[64,768]{1,0:T(8,128)(2,1)S(1)}, u32[]{:S(2)}, u32[]{:S(2)}) collective-permute-start(bf16[64,768]{1,0:T(8,128)(2,1)} %get-tuple-element.282), channel_id=1, source_target_pairs={{0,12},{4,16},{8,20},{12,24},{16,28},{20,0},{24,4},{28,8},{1,13},{... | collective-permute-start | bytes 294920 | tf_op jit(solution)/shard_map/ppermute | solution.py:360
  54.4 33.2 %collective-permute-start.4 = (bf16[64,768]{1,0:T(8,128)(2,1)}, bf16[64,768]{1,0:T(8,128)(2,1)S(1)}, u32[]{:S(2)}, u32[]{:S(2)}) collective-permute-start(bf16[64,768]{1,0:T(8,128)(2,1)} %get-tuple-element.279), channel_id=1, source_target_pairs={{0,4},{4,8},{8,12},{12,16},{16,20},{20,24},{24,28},{28,0},{1,5},{5... | collective-permute-start | bytes 294920 | tf_op jit(solution)/shard_map/ppermute | solution.py:360
  94.8 17.4 %collective-permute-start.13 = (bf16[512,768]{1,0:T(8,128)(2,1)}, bf16[512,768]{1,0:T(8,128)(2,1)S(1)}, u32[]{:S(2)}, u32[]{:S(2)}) collective-permute-start(bf16[512,768]{1,0:T(8,128)(2,1)} %shard_map.181), channel_id=1, source_target_pairs={{0,2},{1,3},{2,0},{3,1},{4,6},{5,7},{6,4},{7,5},{8,10},{9,11},{10,... | collective-permute-start | bytes 2359304 | tf_op jit(solution)/shard_map/ppermute | solution.py:410
  96.4 12.3 %collective-permute-start.12 = (bf16[128,2048]{1,0:T(8,128)(2,1)}, bf16[128,2048]{1,0:T(8,128)(2,1)S(1)}, u32[]{:S(2)}, u32[]{:S(2)}) collective-permute-start(bf16[128,2048]{1,0:T(8,128)(2,1)} %collective-permute-done.3.refs_4_), channel_id=1, source_target_pairs={{8,0},{16,8},{24,16},{28,24},{20,28},{12,20},{4,12},{0,4},{9,1},{1... | collective-permute-start | bytes 1572872 | tf_op jit(solution)/shard_map/ppermute | solution.py:78
  112.2 107.3 %all-gather.9.cloned.1.call-start = ((), (), s32[]{:S(2)}) async-start(), calls=%async_computation.6 | async-start | bytes 5242880 | tf_op jit(solution)/shard_map/all_gather | solution.py:402
  112.4 12.2 %collective-permute-start.17 = (bf16[512,768]{1,0:T(8,128)(2,1)S(1)}, bf16[512,768]{1,0:T(8,128)(2,1)S(1)}, u32[]{:S(2)}, u32[]{:S(2)}) collective-permute-start(bf16[512,768]{1,0:T(8,128)(2,1)S(1)} %collective-permute-done.13), channel_id=1, source_target_pairs={{0,1},{1,0},{2,3},{3,2},{4,5},{5,4},{6,7},{7,6},{8,9},{9,8},{10,11... | collective-permute-start | bytes 2359304 | tf_op jit(solution)/shard_map/ppermute | solution.py:414
  124.6 165.5 %all-gather.11.cloned.1.call-start = ((), (), s32[]{:S(2)}) async-start(), calls=%async_computation.7 | async-start | bytes 10485760 | tf_op jit(solution)/shard_map/all_gather | solution.py:402
  139.6 21.2 %collective-permute-start.20 = (bf16[64,2048]{1,0:T(8,128)(2,1)S(1)}, bf16[64,2048]{1,0:T(8,128)(2,1)S(1)}, u32[]{:S(2)}, u32[]{:S(2)}) collective-permute-start(bf16[64,2048]{1,0:T(8,128)(2,1)S(1)} %copy-done.99), channel_id=1, source_target_pairs={{0,12},{4,16},{8,20},{12,24},{16,28},{20,0},{24,4},{28,8},{1,13},{... | collective-permute-start | bytes 786440 | tf_op jit(solution)/shard_map/ppermute | solution.py:360
  142.5 18.5 %collective-permute-start.21 = (bf16[64,2048]{1,0:T(8,128)(2,1)S(1)}, bf16[64,2048]{1,0:T(8,128)(2,1)S(1)}, u32[]{:S(2)}, u32[]{:S(2)}) collective-permute-start(bf16[64,2048]{1,0:T(8,128)(2,1)S(1)} %copy-done.98), channel_id=1, source_target_pairs={{0,16},{4,20},{8,24},{12,28},{16,0},{20,4},{24,8},{28,12},{1,17},{... | collective-permute-start | bytes 786440 | tf_op jit(solution)/shard_map/ppermute | solution.py:360
  162.8 14.5 %collective-permute-start.28 = (bf16[128,256]{1,0:T(8,128)(2,1)S(1)}, bf16[128,256]{1,0:T(8,128)(2,1)S(1)}, u32[]{:S(2)}, u32[]{:S(2)}) collective-permute-start(bf16[128,256]{1,0:T(8,128)(2,1)S(1)} %get-tuple-element.552), channel_id=1, source_target_pairs={{0,28},{8,20},{16,12},{24,4},{28,0},{20,8},{12,16},{4,24},{1,29},{... | collective-permute-start | bytes 196616 | tf_op jit(solution)/shard_map/ppermute | solution.py:887
  180.3 22.4 %collective-permute-start.29 = (bf16[64,2048]{1,0:T(8,128)(2,1)S(1)}, bf16[64,2048]{1,0:T(8,128)(2,1)S(1)}, u32[]{:S(2)}, u32[]{:S(2)}) collective-permute-start(bf16[64,2048]{1,0:T(8,128)(2,1)S(1)} %copy-done.97), channel_id=1, source_target_pairs={{0,20},{4,24},{8,28},{12,0},{16,4},{20,8},{24,12},{28,16},{1,21},{... | collective-permute-start | bytes 786440 | tf_op jit(solution)/shard_map/ppermute | solution.py:360
  181.0 21.7 %collective-permute-start.30 = (bf16[64,2048]{1,0:T(8,128)(2,1)S(1)}, bf16[64,2048]{1,0:T(8,128)(2,1)S(1)}, u32[]{:S(2)}, u32[]{:S(2)}) collective-permute-start(bf16[64,2048]{1,0:T(8,128)(2,1)S(1)} %copy-done.96), channel_id=1, source_target_pairs={{0,24},{4,28},{8,0},{12,4},{16,8},{20,12},{24,16},{28,20},{1,25},{... | collective-permute-start | bytes 786440 | tf_op jit(solution)/shard_map/ppermute | solution.py:360
  183.1 19.5 %collective-permute-start.31 = (bf16[64,2048]{1,0:T(8,128)(2,1)S(1)}, bf16[64,2048]{1,0:T(8,128)(2,1)S(1)}, u32[]{:S(2)}, u32[]{:S(2)}) collective-permute-start(bf16[64,2048]{1,0:T(8,128)(2,1)S(1)} %copy-done.95), channel_id=1, source_target_pairs={{0,28},{4,0},{8,4},{12,8},{16,12},{20,16},{24,20},{28,24},{1,29},{... | collective-permute-start | bytes 786440 | tf_op jit(solution)/shard_map/ppermute | solution.py:360
  202.7 24.4 %collective-permute-start.33 = (bf16[128,2048]{1,0:T(8,128)(2,1)}, bf16[128,2048]{1,0:T(8,128)(2,1)S(1)}, u32[]{:S(2)}, u32[]{:S(2)}) collective-permute-start(bf16[128,2048]{1,0:T(8,128)(2,1)} %get-tuple-element.376.refs_0_), channel_id=1, source_target_pairs={{8,0},{16,8},{24,16},{28,24},{20,28},{12,20},{4,12},{0,4},{9,1},{1... | collective-permute-start | bytes 1572872 | tf_op jit(solution)/shard_map/ppermute | solution.py:78
  203.2 25.6 %collective-permute-start.32 = (bf16[128,2048]{1,0:T(8,128)(2,1)}, bf16[128,2048]{1,0:T(8,128)(2,1)S(1)}, u32[]{:S(2)}, u32[]{:S(2)}) collective-permute-start(bf16[128,2048]{1,0:T(8,128)(2,1)} %get-tuple-element.376.refs_0_), channel_id=1, source_target_pairs={{0,8},{8,16},{16,24},{24,28},{28,20},{20,12},{12,4},{4,0},{1,9},{9... | collective-permute-start | bytes 1572872 | tf_op jit(solution)/shard_map/ppermute | solution.py:78
  228.9 263.0 %reduce-scatter.5.cloned.1.call-start = ((), (), s32[]{:S(2)}) async-start(), calls=%async_computation.8 | async-start | bytes 10485760 | tf_op jit(solution)/shard_map/reduce_scatter | solution.py:406
  228.9 14.2 %collective-permute-start.34 = (bf16[128,2048]{1,0:T(8,128)(2,1)S(1)}, bf16[128,2048]{1,0:T(8,128)(2,1)S(1)}, u32[]{:S(2)}, u32[]{:S(2)}) collective-permute-start(bf16[128,2048]{1,0:T(8,128)(2,1)S(1)} %collective-permute-done.32.refs_1_), channel_id=1, source_target_pairs={{0,8},{8,16},{16,24},{24,28},{28,20},{20,12},{12,4},{4,0},{1,9},{9... | collective-permute-start | bytes 1572872 | tf_op jit(solution)/shard_map/ppermute | solution.py:78
  231.9 13.6 %collective-permute-start.35 = (bf16[128,2048]{1,0:T(8,128)(2,1)S(1)}, bf16[128,2048]{1,0:T(8,128)(2,1)S(1)}, u32[]{:S(2)}, u32[]{:S(2)}) collective-permute-start(bf16[128,2048]{1,0:T(8,128)(2,1)S(1)} %collective-permute-done.33.refs_2_), channel_id=1, source_target_pairs={{8,0},{16,8},{24,16},{28,24},{20,28},{12,20},{4,12},{0,4},{9,1},{1... | collective-permute-start | bytes 1572872 | tf_op jit(solution)/shard_map/ppermute | solution.py:78
  264.2 13.1 %collective-permute-start.40 = (bf16[128,2048]{1,0:T(8,128)(2,1)S(1)}, bf16[128,2048]{1,0:T(8,128)(2,1)S(1)}, u32[]{:S(2)}, u32[]{:S(2)}) collective-permute-start(bf16[128,2048]{1,0:T(8,128)(2,1)S(1)} %copy-done.12), channel_id=1, source_target_pairs={{0,8},{8,16},{16,24},{24,28},{28,20},{20,12},{12,4},{4,0},{1,9},{9... | collective-permute-start | bytes 1572872 | tf_op jit(solution)/shard_map/ppermute | solution.py:78
  277.3 12.7 %collective-permute-start.42 = (bf16[128,2048]{1,0:T(8,128)(2,1)S(1)}, bf16[128,2048]{1,0:T(8,128)(2,1)S(1)}, u32[]{:S(2)}, u32[]{:S(2)}) collective-permute-start(bf16[128,2048]{1,0:T(8,128)(2,1)S(1)} %collective-permute-done.40.refs_1_), channel_id=1, source_target_pairs={{0,8},{8,16},{16,24},{24,28},{28,20},{20,12},{12,4},{4,0},{1,9},{9... | collective-permute-start | bytes 1572872 | tf_op jit(solution)/shard_map/ppermute | solution.py:78
  286.4 18.0 %collective-permute-start.45 = (bf16[128,2048]{1,0:T(8,128)(2,1)S(1)}, bf16[128,2048]{1,0:T(8,128)(2,1)S(1)}, u32[]{:S(2)}, u32[]{:S(2)}) collective-permute-start(bf16[128,2048]{1,0:T(8,128)(2,1)S(1)} %collective-permute-done.43.refs_4_), channel_id=1, source_target_pairs={{8,0},{16,8},{24,16},{28,24},{20,28},{12,20},{4,12},{0,4},{9,1},{1... | collective-permute-start | bytes 1572872 | tf_op jit(solution)/shard_map/ppermute | solution.py:78
  290.1 14.3 %collective-permute-start.44 = (bf16[128,2048]{1,0:T(8,128)(2,1)S(1)}, bf16[128,2048]{1,0:T(8,128)(2,1)S(1)}, u32[]{:S(2)}, u32[]{:S(2)}) collective-permute-start(bf16[128,2048]{1,0:T(8,128)(2,1)S(1)} %collective-permute-done.42.refs_3_), channel_id=1, source_target_pairs={{0,8},{8,16},{16,24},{24,28},{28,20},{20,12},{12,4},{4,0},{1,9},{9... | collective-permute-start | bytes 1572872 | tf_op jit(solution)/shard_map/ppermute | solution.py:78
  327.8 13.3 %collective-permute-start.50 = (bf16[128,2048]{1,0:T(8,128)(2,1)}, bf16[128,2048]{1,0:T(8,128)(2,1)S(1)}, u32[]{:S(2)}, u32[]{:S(2)}) collective-permute-start(bf16[128,2048]{1,0:T(8,128)(2,1)} %get-tuple-element.416), channel_id=1, source_target_pairs={{0,8},{8,16},{16,24},{24,28},{28,20},{20,12},{12,4},{4,0},{1,9},{9... | collective-permute-start | bytes 1572872 | tf_op jit(solution)/shard_map/ppermute | solution.py:121
  327.9 13.2 %collective-permute-start.51 = (bf16[128,2048]{1,0:T(8,128)(2,1)}, bf16[128,2048]{1,0:T(8,128)(2,1)S(1)}, u32[]{:S(2)}, u32[]{:S(2)}) collective-permute-start(bf16[128,2048]{1,0:T(8,128)(2,1)} %get-tuple-element.417), channel_id=1, source_target_pairs={{8,0},{16,8},{24,16},{28,24},{20,28},{12,20},{4,12},{0,4},{9,1},{1... | collective-permute-start | bytes 1572872 | tf_op jit(solution)/shard_map/ppermute | solution.py:121
  344.7 29.9 %collective-permute-start.56 = (bf16[128,2048]{1,0:T(8,128)(2,1)}, bf16[128,2048]{1,0:T(8,128)(2,1)S(1)}, u32[]{:S(2)}, u32[]{:S(2)}) collective-permute-start(bf16[128,2048]{1,0:T(8,128)(2,1)} %get-tuple-element.421), channel_id=1, source_target_pairs={{0,8},{8,16},{16,24},{24,28},{28,20},{20,12},{12,4},{4,0},{1,9},{9... | collective-permute-start | bytes 1572872 | tf_op jit(solution)/shard_map/ppermute | solution.py:121
  345.4 29.3 %collective-permute-start.57 = (bf16[128,2048]{1,0:T(8,128)(2,1)}, bf16[128,2048]{1,0:T(8,128)(2,1)S(1)}, u32[]{:S(2)}, u32[]{:S(2)}) collective-permute-start(bf16[128,2048]{1,0:T(8,128)(2,1)} %get-tuple-element.422), channel_id=1, source_target_pairs={{8,0},{16,8},{24,16},{28,24},{20,28},{12,20},{4,12},{0,4},{9,1},{1... | collective-permute-start | bytes 1572872 | tf_op jit(solution)/shard_map/ppermute | solution.py:121
  372.6 14.3 %collective-permute-start.54 = (bf16[128,2048]{1,0:T(8,128)(2,1)}, bf16[128,2048]{1,0:T(8,128)(2,1)S(1)}, u32[]{:S(2)}, u32[]{:S(2)}) collective-permute-start(bf16[128,2048]{1,0:T(8,128)(2,1)} %get-tuple-element.419), channel_id=1, source_target_pairs={{0,8},{8,16},{16,24},{24,28},{28,20},{20,12},{12,4},{4,0},{1,9},{9... | collective-permute-start | bytes 1572872 | tf_op jit(solution)/shard_map/ppermute | solution.py:121
  372.9 14.7 %collective-permute-start.55 = (bf16[128,2048]{1,0:T(8,128)(2,1)}, bf16[128,2048]{1,0:T(8,128)(2,1)S(1)}, u32[]{:S(2)}, u32[]{:S(2)}) collective-permute-start(bf16[128,2048]{1,0:T(8,128)(2,1)} %get-tuple-element.420), channel_id=1, source_target_pairs={{8,0},{16,8},{24,16},{28,24},{20,28},{12,20},{4,12},{0,4},{9,1},{1... | collective-permute-start | bytes 1572872 | tf_op jit(solution)/shard_map/ppermute | solution.py:121
  378.8 13.6 %collective-permute-start.58 = (bf16[128,2048]{1,0:T(8,128)(2,1)}, bf16[128,2048]{1,0:T(8,128)(2,1)S(1)}, u32[]{:S(2)}, u32[]{:S(2)}) collective-permute-start(bf16[128,2048]{1,0:T(8,128)(2,1)} %get-tuple-element.423), channel_id=1, source_target_pairs={{0,8},{8,16},{16,24},{24,28},{28,20},{20,12},{12,4},{4,0},{1,9},{9... | collective-permute-start | bytes 1572872 | tf_op jit(solution)/shard_map/ppermute | solution.py:121
  379.1 14.1 %collective-permute-start.59 = (bf16[128,2048]{1,0:T(8,128)(2,1)}, bf16[128,2048]{1,0:T(8,128)(2,1)S(1)}, u32[]{:S(2)}, u32[]{:S(2)}) collective-permute-start(bf16[128,2048]{1,0:T(8,128)(2,1)} %get-tuple-element.424), channel_id=1, source_target_pairs={{8,0},{16,8},{24,16},{28,24},{20,28},{12,20},{4,12},{0,4},{9,1},{1... | collective-permute-start | bytes 1572872 | tf_op jit(solution)/shard_map/ppermute | solution.py:121
  396.0 16.2 %collective-permute-start.60 = (bf16[128,2048]{1,0:T(8,128)(2,1)}, bf16[128,2048]{1,0:T(8,128)(2,1)S(1)}, u32[]{:S(2)}, u32[]{:S(2)}) collective-permute-start(bf16[128,2048]{1,0:T(8,128)(2,1)} %get-tuple-element.430), channel_id=1, source_target_pairs={{0,8},{8,16},{16,24},{24,28},{28,20},{20,12},{12,4},{4,0},{1,9},{9... | collective-permute-start | bytes 1572872 | tf_op jit(solution)/shard_map/ppermute | solution.py:121
  397.5 14.7 %collective-permute-start.61 = (bf16[128,2048]{1,0:T(8,128)(2,1)}, bf16[128,2048]{1,0:T(8,128)(2,1)S(1)}, u32[]{:S(2)}, u32[]{:S(2)}) collective-permute-start(bf16[128,2048]{1,0:T(8,128)(2,1)} %get-tuple-element.431), channel_id=1, source_target_pairs={{8,0},{16,8},{24,16},{28,24},{20,28},{12,20},{4,12},{0,4},{9,1},{1... | collective-permute-start | bytes 1572872 | tf_op jit(solution)/shard_map/ppermute | solution.py:121
  413.2 184.8 %reduce-scatter.7.cloned.1.call-start = ((), (), s32[]{:S(2)}) async-start(), calls=%async_computation.9 | async-start | bytes 5242880 | tf_op jit(solution)/shard_map/reduce_scatter | solution.py:406
  441.2 14.0 %collective-permute-start.66 = (bf16[128,2048]{1,0:T(8,128)(2,1)}, bf16[128,2048]{1,0:T(8,128)(2,1)S(1)}, u32[]{:S(2)}, u32[]{:S(2)}) collective-permute-start(bf16[128,2048]{1,0:T(8,128)(2,1)} %get-tuple-element.439.refs_0_), channel_id=1, source_target_pairs={{8,0},{16,8},{24,16},{28,24},{20,28},{12,20},{4,12},{0,4},{9,1},{1... | collective-permute-start | bytes 1572872 | tf_op jit(solution)/shard_map/ppermute | solution.py:78
  441.9 14.0 %collective-permute-start.64 = (bf16[128,2048]{1,0:T(8,128)(2,1)}, bf16[128,2048]{1,0:T(8,128)(2,1)S(1)}, u32[]{:S(2)}, u32[]{:S(2)}) collective-permute-start(bf16[128,2048]{1,0:T(8,128)(2,1)} %get-tuple-element.439.refs_0_), channel_id=1, source_target_pairs={{0,8},{8,16},{16,24},{24,28},{28,20},{20,12},{12,4},{4,0},{1,9},{9... | collective-permute-start | bytes 1572872 | tf_op jit(solution)/shard_map/ppermute | solution.py:78
  455.3 12.6 %collective-permute-start.67 = (bf16[128,2048]{1,0:T(8,128)(2,1)S(1)}, bf16[128,2048]{1,0:T(8,128)(2,1)S(1)}, u32[]{:S(2)}, u32[]{:S(2)}) collective-permute-start(bf16[128,2048]{1,0:T(8,128)(2,1)S(1)} %collective-permute-done.66.refs_2_), channel_id=1, source_target_pairs={{8,0},{16,8},{24,16},{28,24},{20,28},{12,20},{4,12},{0,4},{9,1},{1... | collective-permute-start | bytes 1572872 | tf_op jit(solution)/shard_map/ppermute | solution.py:78
  456.0 14.8 %collective-permute-start.65 = (bf16[128,2048]{1,0:T(8,128)(2,1)S(1)}, bf16[128,2048]{1,0:T(8,128)(2,1)S(1)}, u32[]{:S(2)}, u32[]{:S(2)}) collective-permute-start(bf16[128,2048]{1,0:T(8,128)(2,1)S(1)} %collective-permute-done.64.refs_1_), channel_id=1, source_target_pairs={{0,8},{8,16},{16,24},{24,28},{28,20},{20,12},{12,4},{4,0},{1,9},{9... | collective-permute-start | bytes 1572872 | tf_op jit(solution)/shard_map/ppermute | solution.py:78
  470.8 140.1 %reduce-scatter.9.cloned.1.call-start = ((), (), s32[]{:S(2)}) async-start(), calls=%async_computation.10 | async-start | bytes 3932160 | tf_op jit(solution)/shard_map/reduce_scatter | solution.py:406
  502.2 15.9 %collective-permute-start.73 = (bf16[64,2048]{1,0:T(8,128)(2,1)}, bf16[64,2048]{1,0:T(8,128)(2,1)S(1)}, u32[]{:S(2)}, u32[]{:S(2)}) collective-permute-start(bf16[64,2048]{1,0:T(8,128)(2,1)} %get-tuple-element.465), channel_id=1, source_target_pairs={{0,8},{4,12},{8,16},{12,20},{16,24},{20,28},{24,0},{28,4},{1,9},{5... | collective-permute-start | bytes 786440 | tf_op jit(solution)/shard_map/ppermute | solution.py:360
  503.2 15.0 %collective-permute-start.72 = (bf16[64,2048]{1,0:T(8,128)(2,1)}, bf16[64,2048]{1,0:T(8,128)(2,1)S(1)}, u32[]{:S(2)}, u32[]{:S(2)}) collective-permute-start(bf16[64,2048]{1,0:T(8,128)(2,1)} %get-tuple-element.464), channel_id=1, source_target_pairs={{0,4},{4,8},{8,12},{12,16},{16,20},{20,24},{24,28},{28,0},{1,5},{5... | collective-permute-start | bytes 786440 | tf_op jit(solution)/shard_map/ppermute | solution.py:360
  504.1 16.7 %collective-permute-start.74 = (bf16[64,2048]{1,0:T(8,128)(2,1)}, bf16[64,2048]{1,0:T(8,128)(2,1)S(1)}, u32[]{:S(2)}, u32[]{:S(2)}) collective-permute-start(bf16[64,2048]{1,0:T(8,128)(2,1)} %get-tuple-element.466), channel_id=1, source_target_pairs={{0,12},{4,16},{8,20},{12,24},{16,28},{20,0},{24,4},{28,8},{1,13},{... | collective-permute-start | bytes 786440 | tf_op jit(solution)/shard_map/ppermute | solution.py:360
  536.3 134.6 %reduce-scatter.11.cloned.1.call-start = ((), (), s32[]{:S(2)}) async-start(), calls=%async_computation.11 | async-start | bytes 1310720 | tf_op jit(solution)/shard_map/reduce_scatter | solution.py:406
  539.5 20.5 %collective-permute-start.79 = (bf16[64,2048]{1,0:T(8,128)(2,1)S(1)}, bf16[64,2048]{1,0:T(8,128)(2,1)S(1)}, u32[]{:S(2)}, u32[]{:S(2)}) collective-permute-start(bf16[64,2048]{1,0:T(8,128)(2,1)S(1)} %copy-done.105), channel_id=1, source_target_pairs={{0,16},{4,20},{8,24},{12,28},{16,0},{20,4},{24,8},{28,12},{1,17},{... | collective-permute-start | bytes 786440 | tf_op jit(solution)/shard_map/ppermute | solution.py:360
  549.5 28.9 %collective-permute-start.77 = (bf16[128,2048]{1,0:T(8,128)(2,1)}, bf16[128,2048]{1,0:T(8,128)(2,1)S(1)}, u32[]{:S(2)}, u32[]{:S(2)}) collective-permute-start(bf16[128,2048]{1,0:T(8,128)(2,1)} %get-tuple-element.470), channel_id=1, source_target_pairs={{0,8},{8,16},{16,24},{24,28},{28,20},{20,12},{12,4},{4,0},{1,9},{9... | collective-permute-start | bytes 1572872 | tf_op jit(solution)/shard_map/ppermute | solution.py:121
  553.5 24.9 %collective-permute-start.78 = (bf16[128,2048]{1,0:T(8,128)(2,1)}, bf16[128,2048]{1,0:T(8,128)(2,1)S(1)}, u32[]{:S(2)}, u32[]{:S(2)}) collective-permute-start(bf16[128,2048]{1,0:T(8,128)(2,1)} %get-tuple-element.471), channel_id=1, source_target_pairs={{8,0},{16,8},{24,16},{28,24},{20,28},{12,20},{4,12},{0,4},{9,1},{1... | collective-permute-start | bytes 1572872 | tf_op jit(solution)/shard_map/ppermute | solution.py:121
  553.5 20.2 %collective-permute-start.80 = (bf16[64,2048]{1,0:T(8,128)(2,1)S(1)}, bf16[64,2048]{1,0:T(8,128)(2,1)S(1)}, u32[]{:S(2)}, u32[]{:S(2)}) collective-permute-start(bf16[64,2048]{1,0:T(8,128)(2,1)S(1)} %copy-done.104), channel_id=1, source_target_pairs={{0,20},{4,24},{8,28},{12,0},{16,4},{20,8},{24,12},{28,16},{1,21},{... | collective-permute-start | bytes 786440 | tf_op jit(solution)/shard_map/ppermute | solution.py:360
  557.8 20.6 %collective-permute-start.81 = (bf16[64,2048]{1,0:T(8,128)(2,1)S(1)}, bf16[64,2048]{1,0:T(8,128)(2,1)S(1)}, u32[]{:S(2)}, u32[]{:S(2)}) collective-permute-start(bf16[64,2048]{1,0:T(8,128)(2,1)S(1)} %copy-done.103), channel_id=1, source_target_pairs={{0,24},{4,28},{8,0},{12,4},{16,8},{20,12},{24,16},{28,20},{1,25},{... | collective-permute-start | bytes 786440 | tf_op jit(solution)/shard_map/ppermute | solution.py:360
  560.1 18.3 %collective-permute-start.82 = (bf16[64,2048]{1,0:T(8,128)(2,1)S(1)}, bf16[64,2048]{1,0:T(8,128)(2,1)S(1)}, u32[]{:S(2)}, u32[]{:S(2)}) collective-permute-start(bf16[64,2048]{1,0:T(8,128)(2,1)S(1)} %copy-done.102), channel_id=1, source_target_pairs={{0,28},{4,0},{8,4},{12,8},{16,12},{20,16},{24,20},{28,24},{1,29},{... | collective-permute-start | bytes 786440 | tf_op jit(solution)/shard_map/ppermute | solution.py:360
  582.6 20.6 %collective-permute-start.83 = (bf16[128,2048]{1,0:T(8,128)(2,1)}, bf16[128,2048]{1,0:T(8,128)(2,1)S(1)}, u32[]{:S(2)}, u32[]{:S(2)}) collective-permute-start(bf16[128,2048]{1,0:T(8,128)(2,1)} %get-tuple-element.482), channel_id=1, source_target_pairs={{0,8},{8,16},{16,24},{24,28},{28,20},{20,12},{12,4},{4,0},{1,9},{9... | collective-permute-start | bytes 1572872 | tf_op jit(solution)/shard_map/ppermute | solution.py:121
  608.8 25.9 %collective-permute-start.85 = (bf16[128,2048]{1,0:T(8,128)(2,1)}, bf16[128,2048]{1,0:T(8,128)(2,1)S(1)}, u32[]{:S(2)}, u32[]{:S(2)}) collective-permute-start(bf16[128,2048]{1,0:T(8,128)(2,1)} %get-tuple-element.489), channel_id=1, source_target_pairs={{0,8},{8,16},{16,24},{24,28},{28,20},{20,12},{12,4},{4,0},{1,9},{9... | collective-permute-start | bytes 1572872 | tf_op jit(solution)/shard_map/ppermute | solution.py:121
  609.3 28.4 %collective-permute-start.86 = (bf16[128,2048]{1,0:T(8,128)(2,1)}, bf16[128,2048]{1,0:T(8,128)(2,1)S(1)}, u32[]{:S(2)}, u32[]{:S(2)}) collective-permute-start(bf16[128,2048]{1,0:T(8,128)(2,1)} %get-tuple-element.490), channel_id=1, source_target_pairs={{8,0},{16,8},{24,16},{28,24},{20,28},{12,20},{4,12},{0,4},{9,1},{1... | collective-permute-start | bytes 1572872 | tf_op jit(solution)/shard_map/ppermute | solution.py:121
  612.9 15.8 %collective-permute-start.88 = (bf16[64,768]{1,0:T(8,128)(2,1)}, bf16[64,768]{1,0:T(8,128)(2,1)S(1)}, u32[]{:S(2)}, u32[]{:S(2)}) collective-permute-start(bf16[64,768]{1,0:T(8,128)(2,1)} %get-tuple-element.495), channel_id=1, source_target_pairs={{0,8},{4,12},{8,16},{12,20},{16,24},{20,28},{24,0},{28,4},{1,9},{5... | collective-permute-start | bytes 294920 | tf_op jit(solution)/shard_map/ppermute | solution.py:360
  614.6 16.0 %collective-permute-start.87 = (bf16[64,768]{1,0:T(8,128)(2,1)}, bf16[64,768]{1,0:T(8,128)(2,1)S(1)}, u32[]{:S(2)}, u32[]{:S(2)}) collective-permute-start(bf16[64,768]{1,0:T(8,128)(2,1)} %get-tuple-element.494), channel_id=1, source_target_pairs={{0,4},{4,8},{8,12},{12,16},{16,20},{20,24},{24,28},{28,0},{1,5},{5... | collective-permute-start | bytes 294920 | tf_op jit(solution)/shard_map/ppermute | solution.py:360
  615.1 17.6 %collective-permute-start.89 = (bf16[64,768]{1,0:T(8,128)(2,1)}, bf16[64,768]{1,0:T(8,128)(2,1)S(1)}, u32[]{:S(2)}, u32[]{:S(2)}) collective-permute-start(bf16[64,768]{1,0:T(8,128)(2,1)} %get-tuple-element.496), channel_id=1, source_target_pairs={{0,12},{4,16},{8,20},{12,24},{16,28},{20,0},{24,4},{28,8},{1,13},{... | collective-permute-start | bytes 294920 | tf_op jit(solution)/shard_map/ppermute | solution.py:360
  (156 other events, 2078.0 us)
Sparse Core Ops, SparseCore 0:
  10.2 70.5 all-gather.4
  112.3 55.5 all-gather.6
  169.5 34.4 all-gather.8
  229.0 59.4 all-gather.10
  412.4 71.6 reduce-scatter.4
  486.6 44.4 reduce-scatter.6
  536.4 35.7 reduce-scatter.8
  605.5 25.3 reduce-scatter.10

commit v4 on v3

--- a/solution.py
+++ b/solution.py
@@ -968,10 +968,12 @@
 
         def early(step, arrived):
             if step == 0:
-                u_all = after(self.u_all, partial)
+                u_all = after(self.u_all, arrived)
                 g = jnp.einsum("td,tc->dc", u_all, d_qkv, preferred_element_type=F32)
-                got["qkv"] = scatter_groups(g.astype(BF16))
+                got["qkv"] = g.astype(BF16)
             if step == 1:
+                arrived, got["qkv"] = lax.optimization_barrier((arrived, got["qkv"]))
+                got["qkv"] = scatter_groups(got["qkv"])
                 arrived, got["second"] = lax.optimization_barrier((arrived, second))
                 o, dy_now = after([self.o, dy_all], arrived)
                 g = jnp.einsum("te,td->ed", o, dy_now, preferred_element_type=F32)

time: 696 us -> 700 us (level)
    unnamed x230 -> x228, local copies, waits for them, and re-layouts: 20.4 us -> 20.7 us
  transfers between devices with their start and end apart: 107 -> 107, of which waited for: 53 -> 54; matrix products, arithmetic and copies ran while one was open for 14% -> 14% of each run, Pallas kernels for 22% -> 22%
where the time goes in v4:
time: 700 us; the launch traced here: 691 us
  waiting for transfers between devices  243 us (35%)
  Pallas kernels  160 us (23%)
  starting transfers between devices  155 us (22%)
  matrix products  66.8 us (10%)
  local copies, waits for them, and re-layouts  39.9 us (6%)
  between operations  15.7 us (2%)
  other arithmetic  10.5 us (2%)
    ppermute x28, waiting for transfers between devices, send_one(): lax.ppermute(after(pieces[k], *ties), 'ctx', [(i, (i + k) % n) for i in r...  76.1 us
    ppermute x16, waiting for transfers between devices, ring_gather(): lax.ppermute(moving[1], 'ctx', back)  57.7 us
    pallas_call x6, Pallas kernels, row_call(): pl.pallas_call(kernel, grid=(rows // tile,), in_specs=in_specs, out_specs...  51 us
    ppermute x16, waiting for transfers between devices, ring_gather(): lax.ppermute(moving[0], 'ctx', ahead)  41.9 us
    ppermute x28, starting transfers between devices, send_one(): lax.ppermute(after(pieces[k], *ties), 'ctx', [(i, (i + k) % n) for i in r...  41.1 us
    ppermute x16, starting transfers between devices, ring_gather(): lax.ppermute(moving[0], 'ctx', ahead)  37.2 us
    ppermute x12, waiting for transfers between devices, ring_scatter(): lax.ppermute(moving[0], 'ctx', ahead)  30.7 us
    ppermute x12, starting transfers between devices, ring_scatter(): lax.ppermute(moving[0], 'ctx', ahead)  24.5 us
  transfers between devices with their start and end apart: 107, of which 54 were waited for; matrix products, arithmetic and copies ran while one was open for 14% of the time, Pallas kernels for 22%

profile of v4, /device:TPU:0, one launch (start us, length us, event | category | flops | bytes accessed | tf_op | source)
XLA Modules:
  0.0 691.3 jit_solution(12672992861594181891)
XLA Ops:
  11.4 6.4 shard_map.179
  23.0 4.9 collective-permute-start.10
  30.7 11.5 %collective-permute-done.2.refs_2_ = bf16[128,2048]{1,0:T(8,128)(2,1)S(1)} collective-permute-done((bf16[128,2048]{1,0:T(8,128)(2,1)}, bf16[128,2048]{1,0:T(8,128)(2,1)S(1)}, u32[]{:S(2)}, u32[]{:S(2)}) %collective-permute-start.2) | collective-permute-done | bytes 524320 | tf_op jit(solution)/shard_map/ppermute | solution.py:78
  43.0 6.5 collective-permute-start.1
  56.9 28.5 %collective-permute-done.7.refs_4_ = bf16[64,768]{1,0:T(8,128)(2,1)S(1)} collective-permute-done((bf16[64,768]{1,0:T(8,128)(2,1)}, bf16[64,768]{1,0:T(8,128)(2,1)S(1)}, u32[]{:S(2)}, u32[]{:S(2)}) %collective-permute-start.7) | collective-permute-done | bytes 98336 | tf_op jit(solution)/shard_map/ppermute | solution.py:360
  87.6 4.4 collective-permute-done.5.refs_2_
  98.4 3.2 shard_map.182
  101.6 6.3 collective-permute-done.11.refs_5_
  108.6 3.6 collective-permute-done.13
  116.9 6.3 collective-permute-done.15.refs_8_
  131.5 8.1 %shard_map.183 = (bf16[1024,2048]{1,0:T(8,128)(2,1)}, f32[1024,768]{1,0:T(8,128)}) custom-call(bf16[128,2048]{1,0:T(8,128)(2,1)} %get-tuple-element.333.refs_0_, bf16[128,2048]{1,0:T(8,128)(2,1)} %copy-done.91, bf16[128,2048]{1,0:T(8,128)(2,1)} %copy-done.90, bf16[128,2048]{1,0:T(8,128)(2,1)} %collective-permute-done.1.refs_3_, ...), custom_call_target="tpu_custom_call" | custom-call | flops 3221225472 | bytes 14680064 | tf_op jit(solution)/shard_map/pallas_call | solution.py:165
  147.2 10.7 %shard_map.184 = (bf16[1024,256]{1,0:T(8,128)(2,1)}, f32[1024,256]{1,0:T(8,128)}, bf16[1024,256]{1,0:T(8,128)(2,1)}, bf16[1024,256]{1,0:T(8,128)(2,1)}, bf16[1024,256]{1,0:T(8,128)(2,1)}) custom-call(f32[1024,768]{1,0:T(8,128)} %get-tuple-element.347.q_ref.k_ref.v_ref, f32[1024,768]{1,0:T(8,128)} %get-tuple-element.347.q_ref.k_ref.v_ref, ...), custom_call_target="tpu_custom_call" | custom-call | flops 1073741824 | bytes 5242880 | tf_op jit(solution)/shard_map/pallas_call | solution.py:831
  162.8 7.7 %collective-permute-start.28 = (bf16[128,256]{1,0:T(8,128)(2,1)S(1)}, bf16[128,256]{1,0:T(8,128)(2,1)S(1)}, u32[]{:S(2)}, u32[]{:S(2)}) collective-permute-start(bf16[128,256]{1,0:T(8,128)(2,1)S(1)} %get-tuple-element.558), channel_id=1, source_target_pairs={{0,28},{8,20},{16,12},{24,4},{28,0},{20,8},{12,16},{4,24},{1,29},{... | collective-permute-start | bytes 196616 | tf_op jit(solution)/shard_map/ppermute | solution.py:887
  170.6 3.9 collective-permute-start.26
  187.7 5.8 fusion.13.y_ref
  193.6 9.1 %shard_map.186 = (bf16[128,2048]{1,0:T(8,128)(2,1)}, bf16[128,2048]{1,0:T(8,128)(2,1)}, f32[128,128]{1,0:T(8,128)}) custom-call(bf16[128,8192]{1,0:T(8,128)(2,1)} %bitcast.67, bf16[128,8192]{1,0:T(8,128)(2,1)} %bitcast.73, f32[128,2048]{1,0:T(8,128)} %fusion.13.y_ref, f32[128,128]{1,0:T(8,128)} %get-tuple-element.366.aux0_ref.refs_4_, ...), custom_call_target="tpu_custom_call" | custom-call | flops 104857600 | bytes 6950912 | tf_op jit(solution)/shard_map/pallas_call | solution.py:725
  203.2 13.3 %collective-permute-start.32 = (bf16[128,2048]{1,0:T(8,128)(2,1)}, bf16[128,2048]{1,0:T(8,128)(2,1)S(1)}, u32[]{:S(2)}, u32[]{:S(2)}) collective-permute-start(bf16[128,2048]{1,0:T(8,128)(2,1)} %get-tuple-element.379.refs_0_), channel_id=1, source_target_pairs={{0,8},{8,16},{16,24},{24,28},{28,20},{20,12},{12,4},{4,0},{1,9},{9... | collective-permute-start | bytes 1572872 | tf_op jit(solution)/shard_map/ppermute | solution.py:78
  216.6 3.0 shard_map.187
  219.5 7.3 %collective-permute-done.33.refs_2_ = bf16[128,2048]{1,0:T(8,128)(2,1)S(1)} collective-permute-done((bf16[128,2048]{1,0:T(8,128)(2,1)}, bf16[128,2048]{1,0:T(8,128)(2,1)S(1)}, u32[]{:S(2)}, u32[]{:S(2)}) %collective-permute-start.33) | collective-permute-done | bytes 524320 | tf_op jit(solution)/shard_map/ppermute | solution.py:78
  228.5 3.4 collective-permute-start.34
  232.0 11.4 %collective-permute-done.34.refs_3_ = bf16[128,2048]{1,0:T(8,128)(2,1)S(1)} collective-permute-done((bf16[128,2048]{1,0:T(8,128)(2,1)S(1)}, bf16[128,2048]{1,0:T(8,128)(2,1)S(1)}, u32[]{:S(2)}, u32[]{:S(2)}) %collective-permute-start.34) | collective-permute-done | bytes 524320 | tf_op jit(solution)/shard_map/ppermute | solution.py:78
  245.5 9.2 %collective-permute-done.36.refs_5_ = bf16[128,2048]{1,0:T(8,128)(2,1)S(1)} collective-permute-done((bf16[128,2048]{1,0:T(8,128)(2,1)S(1)}, bf16[128,2048]{1,0:T(8,128)(2,1)S(1)}, u32[]{:S(2)}, u32[]{:S(2)}) %collective-permute-start.36) | collective-permute-done | bytes 524320 | tf_op jit(solution)/shard_map/ppermute | solution.py:78
  257.4 6.3 collective-permute-done.38.refs_7_
  266.0 10.0 %collective-permute-done.41.refs_2_ = bf16[128,2048]{1,0:T(8,128)(2,1)S(1)} collective-permute-done((bf16[128,2048]{1,0:T(8,128)(2,1)S(1)}, bf16[128,2048]{1,0:T(8,128)(2,1)S(1)}, u32[]{:S(2)}, u32[]{:S(2)}) %collective-permute-start.41) | collective-permute-done | bytes 524320 | tf_op jit(solution)/shard_map/ppermute | solution.py:78
  278.0 9.1 %collective-permute-done.43.refs_4_ = bf16[128,2048]{1,0:T(8,128)(2,1)S(1)} collective-permute-done((bf16[128,2048]{1,0:T(8,128)(2,1)S(1)}, bf16[128,2048]{1,0:T(8,128)(2,1)S(1)}, u32[]{:S(2)}, u32[]{:S(2)}) %collective-permute-start.43) | collective-permute-done | bytes 524320 | tf_op jit(solution)/shard_map/ppermute | solution.py:78
  289.7 14.1 %shard_map.188 = (bf16[1024,2048]{1,0:T(8,128)(2,1)}, f32[1024,2048]{1,0:T(8,128)}, bf16[1024,1024]{1,0:T(8,128)(2,1)}) custom-call(bf16[128,2048]{1,0:T(8,128)(2,1)} %get-tuple-element.379.refs_0_, bf16[128,2048]{1,0:T(8,128)(2,1)} %copy-done.93, bf16[128,2048]{1,0:T(8,128)(2,1)} %copy-done.92, bf16[128,2048]{1,0:T(8,128)(2,1)} %copy-done.94, ...), custom_call_target="tpu_custom_call" | custom-call | flops 8589934592 | bytes 27262976 | tf_op jit(solution)/shard_map/pallas_call | solution.py:218
  306.4 7.3 %convolution_convert_fusion.4.one_own.other_own.y2a_ref = bf16[1024,2048]{1,0:T(8,128)(2,1)S(1)} fusion(bf16[1024,1024]{1,0:T(8,128)(2,1)} %get-tuple-element.443, bf16[1024,2048]{1,0:T(8,128)(2,1)} %all-gather.9.cloned.1.call-done.refs_9_), kind=kOutput, calls=%fused_computation.4 | convolution fusion | flops 4297064448 | bytes 10485760 | tf_op jit(solution)/shard_map/dot_general | solution.py:1153
  317.9 4.6 collective-permute-done.49.other_ref
  329.2 11.3 %shard_map.189 = (bf16[1024,2048]{1,0:T(8,128)(2,1)}, bf16[1024,2048]{1,0:T(8,128)(2,1)}) custom-call(bf16[128,2048]{1,0:T(8,128)(2,1)} %get-tuple-element.409.refs_0_, bf16[128,2048]{1,0:T(8,128)(2,1)} %copy-done.15, bf16[128,2048]{1,0:T(8,128)(2,1)} %copy-done.14, bf16[128,2048]{1,0:T(8,128)(2,1)} %copy-done.17, bf16[128,2048]{1,0:T(8,128)(2,1)} %copy-done.16, ...), custom_call_target="tpu_custom_call" | custom-call | flops 4294967296 | bytes 25165824 | tf_op jit(solution)/shard_map/pallas_call | solution.py:251
  346.1 12.6 %convolution_convert_fusion.1.one_own.other_own.dua_ref = bf16[1024,2048]{1,0:T(8,128)(2,1)S(1)} fusion(bf16[1024,2048]{1,0:T(8,128)(2,1)} %get-tuple-element.421, bf16[2048,2048]{1,0:T(8,128)(2,1)} %all-gather.11.cloned.1.call-done.refs_9_), kind=kOutput, calls=%fused_computation.1 | convolution fusion | flops 8592031744 | bytes 16777216 | tf_op jit(solution)/shard_map/tg,dg->td/dot_general | solution.py:1161
  362.8 4.3 collective-permute-done.53.other_ref
  380.0 6.6 collective-permute-done.54.one_ref
  387.4 5.0 collective-permute-done.58.y2b_ref
  398.2 14.0 %convolution_convert_fusion = bf16[2048,2048]{1,0:T(8,128)(2,1)} fusion(bf16[1024,2048]{1,0:T(8,128)(2,1)} %get-tuple-element.436, bf16[1024,2048]{1,0:T(8,128)(2,1)} %get-tuple-element.421), kind=kOutput, calls=%fused_computation | convolution fusion | flops 8594128896 | bytes 16777216 | tf_op jit(solution)/shard_map/td,tg->dg/dot_general | solution.py:1171
  417.8 7.4 %collective-permute-done.62.dub_ref = bf16[128,2048]{1,0:T(8,128)(2,1)S(1)} collective-permute-done((bf16[128,2048]{1,0:T(8,128)(2,1)}, bf16[128,2048]{1,0:T(8,128)(2,1)S(1)}, u32[]{:S(2)}, u32[]{:S(2)}) %collective-permute-start.62) | collective-permute-done | bytes 524320 | tf_op jit(solution)/shard_map/ppermute | solution.py:121
  427.6 13.8 %shard_map.196 = (f32[128,8192]{1,0:T(8,128)}, bf16[128,2048]{1,0:T(8,128)(2,1)}, f32[8,2048]{1,0:T(8,128)}) custom-call(bf16[128,8192]{1,0:T(8,128)(2,1)} %bitcast.68, bf16[128,8192]{1,0:T(8,128)(2,1)} %bitcast.74, f32[128,2048]{1,0:T(8,128)} %fusion.13.y_ref, bf16[1024,2048]{1,0:T(8,128)(2,1)} %copy-done.2, bf16[128,2048]{1,0:T(8,128)(2,1)} %copy-done.6, ...), custom_call_target="tpu_custom_call" | custom-call | flops 104857600 | bytes 21172224 | tf_op jit(solution)/shard_map/pallas_call | solution.py:725
  443.5 11.7 %collective-permute-done.66.refs_2_ = bf16[128,2048]{1,0:T(8,128)(2,1)S(1)} collective-permute-done((bf16[128,2048]{1,0:T(8,128)(2,1)}, bf16[128,2048]{1,0:T(8,128)(2,1)S(1)}, u32[]{:S(2)}, u32[]{:S(2)}) %collective-permute-start.66) | collective-permute-done | bytes 524320 | tf_op jit(solution)/shard_map/ppermute | solution.py:78
  457.5 9.4 %convolution_convert_fusion.3 = bf16[1024,2048]{1,0:T(8,128)(2,1)} fusion(bf16[1024,1024]{1,0:T(8,128)(2,1)} %get-tuple-element.443, bf16[1024,2048]{1,0:T(8,128)(2,1)} %get-tuple-element.444), kind=kOutput, calls=%fused_computation.3 | convolution fusion | flops 4297064448 | bytes 10485760 | tf_op jit(solution)/shard_map/tf,td->fd/dot_general | solution.py:1194
  467.6 2.9 collective-permute-done.65.refs_3_
  472.7 6.9 %shard_map.197 = bf16[128,8192]{1,0:T(8,128)(2,1)} custom-call(bf16[128,8192]{1,0:T(8,128)(2,1)} %bitcast.69, f32[128,2048]{1,0:T(8,128)} %fusion.13.y_ref, bf16[1024,2048]{1,0:T(8,128)(2,1)} %copy-done.2, bf16[128,2048]{1,0:T(8,128)(2,1)} %copy-done.6, bf16[128,2048]{1,0:T(8,128)(2,1)} %copy-done.7, f32[128,128]{1,0:T(8,128)} %get-tuple-element.366.aux0_ref.refs_4_, ...), custom_call_target="tpu_custom_call" | custom-call | flops 104857600 | bytes 10620928 | tf_op jit(solution)/shard_map/pallas_call | solution.py:725
  479.6 3.0 collective-permute-done.68.refs_5_
  487.1 4.7 shard_map.198.refs_3_
  492.5 6.3 shard_map.199
  498.9 3.0 shard_map.201
  506.7 11.4 %shard_map.200 = (bf16[1024,256]{1,0:T(8,128)(2,1)}, bf16[1024,256]{1,0:T(8,128)(2,1)}, bf16[1024,256]{1,0:T(8,128)(2,1)}) custom-call(bf16[1024,256]{1,0:T(8,128)(2,1)} %get-tuple-element.452.q_ref, bf16[1024,256]{1,0:T(8,128)(2,1)} %get-tuple-element.453.k_ref, bf16[1024,256]{1,0:T(8,128)(2,1)} %get-tuple-element.454.v_ref, ...), custom_call_target="tpu_custom_call" | custom-call | flops 2684354560 | bytes 4718592 | tf_op jit(solution)/shard_map/pallas_call | solution.py:846
  524.1 5.7 convolution_convert_fusion.2.one_own.other_own.refs_0_
  534.0 5.3 collective-permute-done.76.other_ref
  544.5 7.4 %convolution_convert_fusion.5 = bf16[2048,768]{1,0:T(8,128)(2,1)} fusion(bf16[1024,2048]{1,0:T(8,128)(2,1)} %get-tuple-element.476, bf16[1024,768]{1,0:T(8,128)(2,1)S(1)} %constant_dynamic-update-slice_fusion), kind=kOutput, calls=%fused_computation.5 | convolution fusion | flops 3222798336 | bytes 8912896 | tf_op jit(solution)/shard_map/td,tc->dc/dot_general | solution.py:972
  561.3 12.5 %collective-permute-done.79.refs_4_ = bf16[64,2048]{1,0:T(8,128)(2,1)S(1)} collective-permute-done((bf16[64,2048]{1,0:T(8,128)(2,1)}, bf16[64,2048]{1,0:T(8,128)(2,1)S(1)}, u32[]{:S(2)}, u32[]{:S(2)}) %collective-permute-start.79) | collective-permute-done | bytes 262176 | tf_op jit(solution)/shard_map/ppermute | solution.py:360
  579.2 11.9 %collective-permute-start.83 = (bf16[128,2048]{1,0:T(8,128)(2,1)}, bf16[128,2048]{1,0:T(8,128)(2,1)S(1)}, u32[]{:S(2)}, u32[]{:S(2)}) collective-permute-start(bf16[128,2048]{1,0:T(8,128)(2,1)} %get-tuple-element.489), channel_id=1, source_target_pairs={{0,8},{8,16},{16,24},{24,28},{28,20},{20,12},{12,4},{4,0},{1,9},{9... | collective-permute-start | bytes 1572872 | tf_op jit(solution)/shard_map/ppermute | solution.py:121
  591.1 4.6 convolution_convert_fusion.6
  595.7 6.1 collective-permute-done.83.one_ref
  601.7 3.0 collective-permute-done.84.other_ref
  617.7 10.4 %collective-permute-done.88.refs_2_ = bf16[64,768]{1,0:T(8,128)(2,1)S(1)} collective-permute-done((bf16[64,768]{1,0:T(8,128)(2,1)}, bf16[64,768]{1,0:T(8,128)(2,1)S(1)}, u32[]{:S(2)}, u32[]{:S(2)}) %collective-permute-start.88) | collective-permute-done | bytes 98336 | tf_op jit(solution)/shard_map/ppermute | solution.py:360
  628.1 3.4 collective-permute-done.87.refs_1_
  631.5 3.1 collective-permute-done.89.refs_3_
  635.9 3.2 collective-permute-start.93
  640.5 3.4 collective-permute-done.93.refs_7_
  643.8 10.1 %shard_map.206 = (bf16[128,8192]{1,0:T(8,128)(2,1)}, f32[8,2048]{1,0:T(8,128)}) custom-call(bf16[128,8192]{1,0:T(8,128)(2,1)} %bitcast.71, f32[128,8192]{1,0:T(8,128)} %get-tuple-element.451.dmid_ref, bf16[1024,2048]{1,0:T(8,128)(2,1)} %copy-done.3, bf16[128,2048]{1,0:T(8,128)(2,1)} %copy-done.19, bf16[128,2048]{1,0:T(8,128)(2,1)} %copy-done.21, ...), custom_call_target="tpu_custom_call" | custom-call | flops 104857600 | bytes 14356480 | tf_op jit(solution)/shard_map/pallas_call | solution.py:725
  654.9 3.0 collective-permute-start.94
  661.2 3.8 shard_map.207
  669.8 3.4 collective-permute-done.96
  675.1 3.3 collective-permute-start.98
  678.4 4.1 collective-permute-done.98
  (485 shorter events, 207.9 us)
Async XLA Ops:
  7.2 105.0 %all-gather.5.cloned.1.call-start = ((), (), s32[]{:S(2)}) async-start(), calls=%async_computation.4 | async-start | bytes 2359296 | tf_op jit(solution)/shard_map/all_gather | solution.py:913
  8.0 179.8 %all-gather.7.cloned.1.call-start = ((), (), s32[]{:S(2)}) async-start(), calls=%async_computation.5 | async-start | bytes 10485760 | tf_op jit(solution)/shard_map/all_gather | solution.py:936
  17.8 24.4 %collective-permute-start.2 = (bf16[128,2048]{1,0:T(8,128)(2,1)}, bf16[128,2048]{1,0:T(8,128)(2,1)S(1)}, u32[]{:S(2)}, u32[]{:S(2)}) collective-permute-start(bf16[128,2048]{1,0:T(8,128)(2,1)} %get-tuple-element.333.refs_0_), channel_id=1, source_target_pairs={{8,0},{16,8},{24,16},{28,24},{20,28},{12,20},{4,12},{0,4},{9,1},{1... | collective-permute-start | bytes 1572872 | tf_op jit(solution)/shard_map/ppermute | solution.py:78
  20.7 22.3 %collective-permute-start = (bf16[128,2048]{1,0:T(8,128)(2,1)}, bf16[128,2048]{1,0:T(8,128)(2,1)S(1)}, u32[]{:S(2)}, u32[]{:S(2)}) collective-permute-start(bf16[128,2048]{1,0:T(8,128)(2,1)} %get-tuple-element.333.refs_0_), channel_id=1, source_target_pairs={{0,8},{8,16},{16,24},{24,28},{28,20},{20,12},{12,4},{4,0},{1,9},{9... | collective-permute-start | bytes 1572872 | tf_op jit(solution)/shard_map/ppermute | solution.py:78
  23.0 26.5 %collective-permute-start.10 = (bf16[64,768]{1,0:T(8,128)(2,1)}, bf16[64,768]{1,0:T(8,128)(2,1)S(1)}, u32[]{:S(2)}, u32[]{:S(2)}) collective-permute-start(bf16[64,768]{1,0:T(8,128)(2,1)} %get-tuple-element.293), channel_id=1, source_target_pairs={{0,28},{4,0},{8,4},{12,8},{16,12},{20,16},{24,20},{28,24},{1,29},{... | collective-permute-start | bytes 294920 | tf_op jit(solution)/shard_map/ppermute | solution.py:360
  27.9 26.2 %collective-permute-start.9 = (bf16[64,768]{1,0:T(8,128)(2,1)}, bf16[64,768]{1,0:T(8,128)(2,1)S(1)}, u32[]{:S(2)}, u32[]{:S(2)}) collective-permute-start(bf16[64,768]{1,0:T(8,128)(2,1)} %get-tuple-element.291), channel_id=1, source_target_pairs={{0,24},{4,28},{8,0},{12,4},{16,8},{20,12},{24,16},{28,20},{1,25},{... | collective-permute-start | bytes 294920 | tf_op jit(solution)/shard_map/ppermute | solution.py:360
  28.4 26.0 %collective-permute-start.8 = (bf16[64,768]{1,0:T(8,128)(2,1)}, bf16[64,768]{1,0:T(8,128)(2,1)S(1)}, u32[]{:S(2)}, u32[]{:S(2)}) collective-permute-start(bf16[64,768]{1,0:T(8,128)(2,1)} %get-tuple-element.289), channel_id=1, source_target_pairs={{0,20},{4,24},{8,28},{12,0},{16,4},{20,8},{24,12},{28,16},{1,21},{... | collective-permute-start | bytes 294920 | tf_op jit(solution)/shard_map/ppermute | solution.py:360
  42.2 49.8 %collective-permute-start.3 = (bf16[128,2048]{1,0:T(8,128)(2,1)S(1)}, bf16[128,2048]{1,0:T(8,128)(2,1)}, u32[]{:S(2)}, u32[]{:S(2)}) collective-permute-start(bf16[128,2048]{1,0:T(8,128)(2,1)S(1)} %collective-permute-done.2.refs_2_), channel_id=1, source_target_pairs={{8,0},{16,8},{24,16},{28,24},{20,28},{12,20},{4,12},{0,4},{9,1},{1... | collective-permute-start | bytes 1572872 | tf_op jit(solution)/shard_map/ppermute | solution.py:78
  43.0 49.0 %collective-permute-start.1 = (bf16[128,2048]{1,0:T(8,128)(2,1)S(1)}, bf16[128,2048]{1,0:T(8,128)(2,1)}, u32[]{:S(2)}, u32[]{:S(2)}) collective-permute-start(bf16[128,2048]{1,0:T(8,128)(2,1)S(1)} %collective-permute-done.refs_1_), channel_id=1, source_target_pairs={{0,8},{8,16},{16,24},{24,28},{28,20},{20,12},{12,4},{4,0},{1,9},{9... | collective-permute-start | bytes 1572872 | tf_op jit(solution)/shard_map/ppermute | solution.py:78
  49.6 35.8 %collective-permute-start.7 = (bf16[64,768]{1,0:T(8,128)(2,1)}, bf16[64,768]{1,0:T(8,128)(2,1)S(1)}, u32[]{:S(2)}, u32[]{:S(2)}) collective-permute-start(bf16[64,768]{1,0:T(8,128)(2,1)} %get-tuple-element.287), channel_id=1, source_target_pairs={{0,16},{4,20},{8,24},{12,28},{16,0},{20,4},{24,8},{28,12},{1,17},{... | collective-permute-start | bytes 294920 | tf_op jit(solution)/shard_map/ppermute | solution.py:360
  54.2 33.4 %collective-permute-start.6 = (bf16[64,768]{1,0:T(8,128)(2,1)}, bf16[64,768]{1,0:T(8,128)(2,1)S(1)}, u32[]{:S(2)}, u32[]{:S(2)}) collective-permute-start(bf16[64,768]{1,0:T(8,128)(2,1)} %get-tuple-element.285), channel_id=1, source_target_pairs={{0,12},{4,16},{8,20},{12,24},{16,28},{20,0},{24,4},{28,8},{1,13},{... | collective-permute-start | bytes 294920 | tf_op jit(solution)/shard_map/ppermute | solution.py:360
  54.4 33.2 %collective-permute-start.4 = (bf16[64,768]{1,0:T(8,128)(2,1)}, bf16[64,768]{1,0:T(8,128)(2,1)S(1)}, u32[]{:S(2)}, u32[]{:S(2)}) collective-permute-start(bf16[64,768]{1,0:T(8,128)(2,1)} %get-tuple-element.282), channel_id=1, source_target_pairs={{0,4},{4,8},{8,12},{12,16},{16,20},{20,24},{24,28},{28,0},{1,5},{5... | collective-permute-start | bytes 294920 | tf_op jit(solution)/shard_map/ppermute | solution.py:360
  94.8 17.4 %collective-permute-start.13 = (bf16[512,768]{1,0:T(8,128)(2,1)}, bf16[512,768]{1,0:T(8,128)(2,1)S(1)}, u32[]{:S(2)}, u32[]{:S(2)}) collective-permute-start(bf16[512,768]{1,0:T(8,128)(2,1)} %shard_map.181), channel_id=1, source_target_pairs={{0,2},{1,3},{2,0},{3,1},{4,6},{5,7},{6,4},{7,5},{8,10},{9,11},{10,... | collective-permute-start | bytes 2359304 | tf_op jit(solution)/shard_map/ppermute | solution.py:410
  96.4 12.3 %collective-permute-start.12 = (bf16[128,2048]{1,0:T(8,128)(2,1)}, bf16[128,2048]{1,0:T(8,128)(2,1)S(1)}, u32[]{:S(2)}, u32[]{:S(2)}) collective-permute-start(bf16[128,2048]{1,0:T(8,128)(2,1)} %collective-permute-done.3.refs_4_), channel_id=1, source_target_pairs={{8,0},{16,8},{24,16},{28,24},{20,28},{12,20},{4,12},{0,4},{9,1},{1... | collective-permute-start | bytes 1572872 | tf_op jit(solution)/shard_map/ppermute | solution.py:78
  112.2 107.3 %all-gather.9.cloned.1.call-start = ((), (), s32[]{:S(2)}) async-start(), calls=%async_computation.6 | async-start | bytes 5242880 | tf_op jit(solution)/shard_map/all_gather | solution.py:402
  112.4 12.2 %collective-permute-start.17 = (bf16[512,768]{1,0:T(8,128)(2,1)S(1)}, bf16[512,768]{1,0:T(8,128)(2,1)S(1)}, u32[]{:S(2)}, u32[]{:S(2)}) collective-permute-start(bf16[512,768]{1,0:T(8,128)(2,1)S(1)} %collective-permute-done.13), channel_id=1, source_target_pairs={{0,1},{1,0},{2,3},{3,2},{4,5},{5,4},{6,7},{7,6},{8,9},{9,8},{10,11... | collective-permute-start | bytes 2359304 | tf_op jit(solution)/shard_map/ppermute | solution.py:414
  124.6 165.1 %all-gather.11.cloned.1.call-start = ((), (), s32[]{:S(2)}) async-start(), calls=%async_computation.7 | async-start | bytes 10485760 | tf_op jit(solution)/shard_map/all_gather | solution.py:402
  127.5 12.0 %collective-permute-start.18 = (bf16[64,2048]{1,0:T(8,128)(2,1)S(1)}, bf16[64,2048]{1,0:T(8,128)(2,1)S(1)}, u32[]{:S(2)}, u32[]{:S(2)}) collective-permute-start(bf16[64,2048]{1,0:T(8,128)(2,1)S(1)} %copy-done.104), channel_id=1, source_target_pairs={{0,4},{4,8},{8,12},{12,16},{16,20},{20,24},{24,28},{28,0},{1,5},{5... | collective-permute-start | bytes 786440 | tf_op jit(solution)/shard_map/ppermute | solution.py:360
  139.6 21.2 %collective-permute-start.20 = (bf16[64,2048]{1,0:T(8,128)(2,1)S(1)}, bf16[64,2048]{1,0:T(8,128)(2,1)S(1)}, u32[]{:S(2)}, u32[]{:S(2)}) collective-permute-start(bf16[64,2048]{1,0:T(8,128)(2,1)S(1)} %copy-done.100), channel_id=1, source_target_pairs={{0,12},{4,16},{8,20},{12,24},{16,28},{20,0},{24,4},{28,8},{1,13},{... | collective-permute-start | bytes 786440 | tf_op jit(solution)/shard_map/ppermute | solution.py:360
  142.5 18.5 %collective-permute-start.21 = (bf16[64,2048]{1,0:T(8,128)(2,1)S(1)}, bf16[64,2048]{1,0:T(8,128)(2,1)S(1)}, u32[]{:S(2)}, u32[]{:S(2)}) collective-permute-start(bf16[64,2048]{1,0:T(8,128)(2,1)S(1)} %copy-done.99), channel_id=1, source_target_pairs={{0,16},{4,20},{8,24},{12,28},{16,0},{20,4},{24,8},{28,12},{1,17},{... | collective-permute-start | bytes 786440 | tf_op jit(solution)/shard_map/ppermute | solution.py:360
  162.8 14.6 %collective-permute-start.28 = (bf16[128,256]{1,0:T(8,128)(2,1)S(1)}, bf16[128,256]{1,0:T(8,128)(2,1)S(1)}, u32[]{:S(2)}, u32[]{:S(2)}) collective-permute-start(bf16[128,256]{1,0:T(8,128)(2,1)S(1)} %get-tuple-element.558), channel_id=1, source_target_pairs={{0,28},{8,20},{16,12},{24,4},{28,0},{20,8},{12,16},{4,24},{1,29},{... | collective-permute-start | bytes 196616 | tf_op jit(solution)/shard_map/ppermute | solution.py:887
  180.3 22.4 %collective-permute-start.29 = (bf16[64,2048]{1,0:T(8,128)(2,1)S(1)}, bf16[64,2048]{1,0:T(8,128)(2,1)S(1)}, u32[]{:S(2)}, u32[]{:S(2)}) collective-permute-start(bf16[64,2048]{1,0:T(8,128)(2,1)S(1)} %copy-done.98), channel_id=1, source_target_pairs={{0,20},{4,24},{8,28},{12,0},{16,4},{20,8},{24,12},{28,16},{1,21},{... | collective-permute-start | bytes 786440 | tf_op jit(solution)/shard_map/ppermute | solution.py:360
  181.0 21.7 %collective-permute-start.30 = (bf16[64,2048]{1,0:T(8,128)(2,1)S(1)}, bf16[64,2048]{1,0:T(8,128)(2,1)S(1)}, u32[]{:S(2)}, u32[]{:S(2)}) collective-permute-start(bf16[64,2048]{1,0:T(8,128)(2,1)S(1)} %copy-done.97), channel_id=1, source_target_pairs={{0,24},{4,28},{8,0},{12,4},{16,8},{20,12},{24,16},{28,20},{1,25},{... | collective-permute-start | bytes 786440 | tf_op jit(solution)/shard_map/ppermute | solution.py:360
  183.2 19.5 %collective-permute-start.31 = (bf16[64,2048]{1,0:T(8,128)(2,1)S(1)}, bf16[64,2048]{1,0:T(8,128)(2,1)S(1)}, u32[]{:S(2)}, u32[]{:S(2)}) collective-permute-start(bf16[64,2048]{1,0:T(8,128)(2,1)S(1)} %copy-done.96), channel_id=1, source_target_pairs={{0,28},{4,0},{8,4},{12,8},{16,12},{20,16},{24,20},{28,24},{1,29},{... | collective-permute-start | bytes 786440 | tf_op jit(solution)/shard_map/ppermute | solution.py:360
  202.7 24.1 %collective-permute-start.33 = (bf16[128,2048]{1,0:T(8,128)(2,1)}, bf16[128,2048]{1,0:T(8,128)(2,1)S(1)}, u32[]{:S(2)}, u32[]{:S(2)}) collective-permute-start(bf16[128,2048]{1,0:T(8,128)(2,1)} %get-tuple-element.379.refs_0_), channel_id=1, source_target_pairs={{8,0},{16,8},{24,16},{28,24},{20,28},{12,20},{4,12},{0,4},{9,1},{1... | collective-permute-start | bytes 1572872 | tf_op jit(solution)/shard_map/ppermute | solution.py:78
  203.2 25.2 %collective-permute-start.32 = (bf16[128,2048]{1,0:T(8,128)(2,1)}, bf16[128,2048]{1,0:T(8,128)(2,1)S(1)}, u32[]{:S(2)}, u32[]{:S(2)}) collective-permute-start(bf16[128,2048]{1,0:T(8,128)(2,1)} %get-tuple-element.379.refs_0_), channel_id=1, source_target_pairs={{0,8},{8,16},{16,24},{24,28},{28,20},{20,12},{12,4},{4,0},{1,9},{9... | collective-permute-start | bytes 1572872 | tf_op jit(solution)/shard_map/ppermute | solution.py:78
  228.5 263.3 %reduce-scatter.5.cloned.1.call-start = ((), (), s32[]{:S(2)}) async-start(), calls=%async_computation.8 | async-start | bytes 10485760 | tf_op jit(solution)/shard_map/reduce_scatter | solution.py:406
  228.5 14.8 %collective-permute-start.34 = (bf16[128,2048]{1,0:T(8,128)(2,1)S(1)}, bf16[128,2048]{1,0:T(8,128)(2,1)S(1)}, u32[]{:S(2)}, u32[]{:S(2)}) collective-permute-start(bf16[128,2048]{1,0:T(8,128)(2,1)S(1)} %collective-permute-done.32.refs_1_), channel_id=1, source_target_pairs={{0,8},{8,16},{16,24},{24,28},{28,20},{20,12},{12,4},{4,0},{1,9},{9... | collective-permute-start | bytes 1572872 | tf_op jit(solution)/shard_map/ppermute | solution.py:78
  232.0 13.5 %collective-permute-start.35 = (bf16[128,2048]{1,0:T(8,128)(2,1)S(1)}, bf16[128,2048]{1,0:T(8,128)(2,1)S(1)}, u32[]{:S(2)}, u32[]{:S(2)}) collective-permute-start(bf16[128,2048]{1,0:T(8,128)(2,1)S(1)} %collective-permute-done.33.refs_2_), channel_id=1, source_target_pairs={{8,0},{16,8},{24,16},{28,24},{20,28},{12,20},{4,12},{0,4},{9,1},{1... | collective-permute-start | bytes 1572872 | tf_op jit(solution)/shard_map/ppermute | solution.py:78
  265.0 12.6 %collective-permute-start.40 = (bf16[128,2048]{1,0:T(8,128)(2,1)S(1)}, bf16[128,2048]{1,0:T(8,128)(2,1)S(1)}, u32[]{:S(2)}, u32[]{:S(2)}) collective-permute-start(bf16[128,2048]{1,0:T(8,128)(2,1)S(1)} %copy-done.13), channel_id=1, source_target_pairs={{0,8},{8,16},{16,24},{24,28},{28,20},{20,12},{12,4},{4,0},{1,9},{9... | collective-permute-start | bytes 1572872 | tf_op jit(solution)/shard_map/ppermute | solution.py:78
  287.1 16.8 %collective-permute-start.45 = (bf16[128,2048]{1,0:T(8,128)(2,1)S(1)}, bf16[128,2048]{1,0:T(8,128)(2,1)S(1)}, u32[]{:S(2)}, u32[]{:S(2)}) collective-permute-start(bf16[128,2048]{1,0:T(8,128)(2,1)S(1)} %collective-permute-done.43.refs_4_), channel_id=1, source_target_pairs={{8,0},{16,8},{24,16},{28,24},{20,28},{12,20},{4,12},{0,4},{9,1},{1... | collective-permute-start | bytes 1572872 | tf_op jit(solution)/shard_map/ppermute | solution.py:78
  289.4 14.5 %collective-permute-start.44 = (bf16[128,2048]{1,0:T(8,128)(2,1)S(1)}, bf16[128,2048]{1,0:T(8,128)(2,1)S(1)}, u32[]{:S(2)}, u32[]{:S(2)}) collective-permute-start(bf16[128,2048]{1,0:T(8,128)(2,1)S(1)} %collective-permute-done.42.refs_3_), channel_id=1, source_target_pairs={{0,8},{8,16},{16,24},{24,28},{28,20},{20,12},{12,4},{4,0},{1,9},{9... | collective-permute-start | bytes 1572872 | tf_op jit(solution)/shard_map/ppermute | solution.py:78
  327.1 13.3 %collective-permute-start.50 = (bf16[128,2048]{1,0:T(8,128)(2,1)}, bf16[128,2048]{1,0:T(8,128)(2,1)S(1)}, u32[]{:S(2)}, u32[]{:S(2)}) collective-permute-start(bf16[128,2048]{1,0:T(8,128)(2,1)} %get-tuple-element.419), channel_id=1, source_target_pairs={{0,8},{8,16},{16,24},{24,28},{28,20},{20,12},{12,4},{4,0},{1,9},{9... | collective-permute-start | bytes 1572872 | tf_op jit(solution)/shard_map/ppermute | solution.py:121
  327.8 12.7 %collective-permute-start.51 = (bf16[128,2048]{1,0:T(8,128)(2,1)}, bf16[128,2048]{1,0:T(8,128)(2,1)S(1)}, u32[]{:S(2)}, u32[]{:S(2)}) collective-permute-start(bf16[128,2048]{1,0:T(8,128)(2,1)} %get-tuple-element.420), channel_id=1, source_target_pairs={{8,0},{16,8},{24,16},{28,24},{20,28},{12,20},{4,12},{0,4},{9,1},{1... | collective-permute-start | bytes 1572872 | tf_op jit(solution)/shard_map/ppermute | solution.py:121
  344.1 29.7 %collective-permute-start.56 = (bf16[128,2048]{1,0:T(8,128)(2,1)}, bf16[128,2048]{1,0:T(8,128)(2,1)S(1)}, u32[]{:S(2)}, u32[]{:S(2)}) collective-permute-start(bf16[128,2048]{1,0:T(8,128)(2,1)} %get-tuple-element.424), channel_id=1, source_target_pairs={{0,8},{8,16},{16,24},{24,28},{28,20},{20,12},{12,4},{4,0},{1,9},{9... | collective-permute-start | bytes 1572872 | tf_op jit(solution)/shard_map/ppermute | solution.py:121
  345.4 28.4 %collective-permute-start.57 = (bf16[128,2048]{1,0:T(8,128)(2,1)}, bf16[128,2048]{1,0:T(8,128)(2,1)S(1)}, u32[]{:S(2)}, u32[]{:S(2)}) collective-permute-start(bf16[128,2048]{1,0:T(8,128)(2,1)} %get-tuple-element.425), channel_id=1, source_target_pairs={{8,0},{16,8},{24,16},{28,24},{20,28},{12,20},{4,12},{0,4},{9,1},{1... | collective-permute-start | bytes 1572872 | tf_op jit(solution)/shard_map/ppermute | solution.py:121
  371.7 14.8 %collective-permute-start.54 = (bf16[128,2048]{1,0:T(8,128)(2,1)}, bf16[128,2048]{1,0:T(8,128)(2,1)S(1)}, u32[]{:S(2)}, u32[]{:S(2)}) collective-permute-start(bf16[128,2048]{1,0:T(8,128)(2,1)} %get-tuple-element.422), channel_id=1, source_target_pairs={{0,8},{8,16},{16,24},{24,28},{28,20},{20,12},{12,4},{4,0},{1,9},{9... | collective-permute-start | bytes 1572872 | tf_op jit(solution)/shard_map/ppermute | solution.py:121
  372.3 15.1 %collective-permute-start.55 = (bf16[128,2048]{1,0:T(8,128)(2,1)}, bf16[128,2048]{1,0:T(8,128)(2,1)S(1)}, u32[]{:S(2)}, u32[]{:S(2)}) collective-permute-start(bf16[128,2048]{1,0:T(8,128)(2,1)} %get-tuple-element.423), channel_id=1, source_target_pairs={{8,0},{16,8},{24,16},{28,24},{20,28},{12,20},{4,12},{0,4},{9,1},{1... | collective-permute-start | bytes 1572872 | tf_op jit(solution)/shard_map/ppermute | solution.py:121
  378.0 14.4 %collective-permute-start.58 = (bf16[128,2048]{1,0:T(8,128)(2,1)}, bf16[128,2048]{1,0:T(8,128)(2,1)S(1)}, u32[]{:S(2)}, u32[]{:S(2)}) collective-permute-start(bf16[128,2048]{1,0:T(8,128)(2,1)} %get-tuple-element.426), channel_id=1, source_target_pairs={{0,8},{8,16},{16,24},{24,28},{28,20},{20,12},{12,4},{4,0},{1,9},{9... | collective-permute-start | bytes 1572872 | tf_op jit(solution)/shard_map/ppermute | solution.py:121
  378.6 14.6 %collective-permute-start.59 = (bf16[128,2048]{1,0:T(8,128)(2,1)}, bf16[128,2048]{1,0:T(8,128)(2,1)S(1)}, u32[]{:S(2)}, u32[]{:S(2)}) collective-permute-start(bf16[128,2048]{1,0:T(8,128)(2,1)} %get-tuple-element.427), channel_id=1, source_target_pairs={{8,0},{16,8},{24,16},{28,24},{20,28},{12,20},{4,12},{0,4},{9,1},{1... | collective-permute-start | bytes 1572872 | tf_op jit(solution)/shard_map/ppermute | solution.py:121
  396.0 16.2 %collective-permute-start.60 = (bf16[128,2048]{1,0:T(8,128)(2,1)}, bf16[128,2048]{1,0:T(8,128)(2,1)S(1)}, u32[]{:S(2)}, u32[]{:S(2)}) collective-permute-start(bf16[128,2048]{1,0:T(8,128)(2,1)} %get-tuple-element.433), channel_id=1, source_target_pairs={{0,8},{8,16},{16,24},{24,28},{28,20},{20,12},{12,4},{4,0},{1,9},{9... | collective-permute-start | bytes 1572872 | tf_op jit(solution)/shard_map/ppermute | solution.py:121
  397.6 14.7 %collective-permute-start.61 = (bf16[128,2048]{1,0:T(8,128)(2,1)}, bf16[128,2048]{1,0:T(8,128)(2,1)S(1)}, u32[]{:S(2)}, u32[]{:S(2)}) collective-permute-start(bf16[128,2048]{1,0:T(8,128)(2,1)} %get-tuple-element.434), channel_id=1, source_target_pairs={{8,0},{16,8},{24,16},{28,24},{20,28},{12,20},{4,12},{0,4},{9,1},{1... | collective-permute-start | bytes 1572872 | tf_op jit(solution)/shard_map/ppermute | solution.py:121
  413.2 182.5 %reduce-scatter.7.cloned.1.call-start = ((), (), s32[]{:S(2)}) async-start(), calls=%async_computation.9 | async-start | bytes 5242880 | tf_op jit(solution)/shard_map/reduce_scatter | solution.py:406
  441.4 13.8 %collective-permute-start.66 = (bf16[128,2048]{1,0:T(8,128)(2,1)}, bf16[128,2048]{1,0:T(8,128)(2,1)S(1)}, u32[]{:S(2)}, u32[]{:S(2)}) collective-permute-start(bf16[128,2048]{1,0:T(8,128)(2,1)} %get-tuple-element.442.refs_0_), channel_id=1, source_target_pairs={{8,0},{16,8},{24,16},{28,24},{20,28},{12,20},{4,12},{0,4},{9,1},{1... | collective-permute-start | bytes 1572872 | tf_op jit(solution)/shard_map/ppermute | solution.py:78
  442.0 13.8 %collective-permute-start.64 = (bf16[128,2048]{1,0:T(8,128)(2,1)}, bf16[128,2048]{1,0:T(8,128)(2,1)S(1)}, u32[]{:S(2)}, u32[]{:S(2)}) collective-permute-start(bf16[128,2048]{1,0:T(8,128)(2,1)} %get-tuple-element.442.refs_0_), channel_id=1, source_target_pairs={{0,8},{8,16},{16,24},{24,28},{28,20},{20,12},{12,4},{4,0},{1,9},{9... | collective-permute-start | bytes 1572872 | tf_op jit(solution)/shard_map/ppermute | solution.py:78
  455.2 12.4 %collective-permute-start.67 = (bf16[128,2048]{1,0:T(8,128)(2,1)S(1)}, bf16[128,2048]{1,0:T(8,128)(2,1)S(1)}, u32[]{:S(2)}, u32[]{:S(2)}) collective-permute-start(bf16[128,2048]{1,0:T(8,128)(2,1)S(1)} %collective-permute-done.66.refs_2_), channel_id=1, source_target_pairs={{8,0},{16,8},{24,16},{28,24},{20,28},{12,20},{4,12},{0,4},{9,1},{1... | collective-permute-start | bytes 1572872 | tf_op jit(solution)/shard_map/ppermute | solution.py:78
  455.8 14.7 %collective-permute-start.65 = (bf16[128,2048]{1,0:T(8,128)(2,1)S(1)}, bf16[128,2048]{1,0:T(8,128)(2,1)S(1)}, u32[]{:S(2)}, u32[]{:S(2)}) collective-permute-start(bf16[128,2048]{1,0:T(8,128)(2,1)S(1)} %collective-permute-done.64.refs_1_), channel_id=1, source_target_pairs={{0,8},{8,16},{16,24},{24,28},{28,20},{20,12},{12,4},{4,0},{1,9},{9... | collective-permute-start | bytes 1572872 | tf_op jit(solution)/shard_map/ppermute | solution.py:78
  470.5 140.0 %reduce-scatter.9.cloned.1.call-start = ((), (), s32[]{:S(2)}) async-start(), calls=%async_computation.10 | async-start | bytes 3932160 | tf_op jit(solution)/shard_map/reduce_scatter | solution.py:406
  501.9 16.2 %collective-permute-start.73 = (bf16[64,2048]{1,0:T(8,128)(2,1)}, bf16[64,2048]{1,0:T(8,128)(2,1)S(1)}, u32[]{:S(2)}, u32[]{:S(2)}) collective-permute-start(bf16[64,2048]{1,0:T(8,128)(2,1)} %get-tuple-element.468), channel_id=1, source_target_pairs={{0,8},{4,12},{8,16},{12,20},{16,24},{20,28},{24,0},{28,4},{1,9},{5... | collective-permute-start | bytes 786440 | tf_op jit(solution)/shard_map/ppermute | solution.py:360
  502.8 15.3 %collective-permute-start.72 = (bf16[64,2048]{1,0:T(8,128)(2,1)}, bf16[64,2048]{1,0:T(8,128)(2,1)S(1)}, u32[]{:S(2)}, u32[]{:S(2)}) collective-permute-start(bf16[64,2048]{1,0:T(8,128)(2,1)} %get-tuple-element.467), channel_id=1, source_target_pairs={{0,4},{4,8},{8,12},{12,16},{16,20},{20,24},{24,28},{28,0},{1,5},{5... | collective-permute-start | bytes 786440 | tf_op jit(solution)/shard_map/ppermute | solution.py:360
  504.1 16.7 %collective-permute-start.74 = (bf16[64,2048]{1,0:T(8,128)(2,1)}, bf16[64,2048]{1,0:T(8,128)(2,1)S(1)}, u32[]{:S(2)}, u32[]{:S(2)}) collective-permute-start(bf16[64,2048]{1,0:T(8,128)(2,1)} %get-tuple-element.469), channel_id=1, source_target_pairs={{0,12},{4,16},{8,20},{12,24},{16,28},{20,0},{24,4},{28,8},{1,13},{... | collective-permute-start | bytes 786440 | tf_op jit(solution)/shard_map/ppermute | solution.py:360
  542.5 12.2 %collective-permute-start.77 = (bf16[128,2048]{1,0:T(8,128)(2,1)}, bf16[128,2048]{1,0:T(8,128)(2,1)S(1)}, u32[]{:S(2)}, u32[]{:S(2)}) collective-permute-start(bf16[128,2048]{1,0:T(8,128)(2,1)} %get-tuple-element.473), channel_id=1, source_target_pairs={{0,8},{8,16},{16,24},{24,28},{28,20},{20,12},{12,4},{4,0},{1,9},{9... | collective-permute-start | bytes 1572872 | tf_op jit(solution)/shard_map/ppermute | solution.py:121
  555.8 117.5 %reduce-scatter.11.cloned.1.call-start = ((), (), s32[]{:S(2)}) async-start(), calls=%async_computation.11 | async-start | bytes 1310720 | tf_op jit(solution)/shard_map/reduce_scatter | solution.py:406
  555.9 17.9 %collective-permute-start.79 = (bf16[64,2048]{1,0:T(8,128)(2,1)}, bf16[64,2048]{1,0:T(8,128)(2,1)S(1)}, u32[]{:S(2)}, u32[]{:S(2)}) collective-permute-start(bf16[64,2048]{1,0:T(8,128)(2,1)} %get-tuple-element.480), channel_id=1, source_target_pairs={{0,16},{4,20},{8,24},{12,28},{16,0},{20,4},{24,8},{28,12},{1,17},{... | collective-permute-start | bytes 786440 | tf_op jit(solution)/shard_map/ppermute | solution.py:360
  556.3 17.5 %collective-permute-start.80 = (bf16[64,2048]{1,0:T(8,128)(2,1)S(1)}, bf16[64,2048]{1,0:T(8,128)(2,1)S(1)}, u32[]{:S(2)}, u32[]{:S(2)}) collective-permute-start(bf16[64,2048]{1,0:T(8,128)(2,1)S(1)} %copy-done.105), channel_id=1, source_target_pairs={{0,20},{4,24},{8,28},{12,0},{16,4},{20,8},{24,12},{28,16},{1,21},{... | collective-permute-start | bytes 786440 | tf_op jit(solution)/shard_map/ppermute | solution.py:360
  559.0 14.8 %collective-permute-start.81 = (bf16[64,2048]{1,0:T(8,128)(2,1)S(1)}, bf16[64,2048]{1,0:T(8,128)(2,1)S(1)}, u32[]{:S(2)}, u32[]{:S(2)}) collective-permute-start(bf16[64,2048]{1,0:T(8,128)(2,1)S(1)} %copy-done.103), channel_id=1, source_target_pairs={{0,24},{4,28},{8,0},{12,4},{16,8},{20,12},{24,16},{28,20},{1,25},{... | collective-permute-start | bytes 786440 | tf_op jit(solution)/shard_map/ppermute | solution.py:360
  559.1 17.4 %collective-permute-start.82 = (bf16[64,2048]{1,0:T(8,128)(2,1)S(1)}, bf16[64,2048]{1,0:T(8,128)(2,1)S(1)}, u32[]{:S(2)}, u32[]{:S(2)}) collective-permute-start(bf16[64,2048]{1,0:T(8,128)(2,1)S(1)} %copy-done.101), channel_id=1, source_target_pairs={{0,28},{4,0},{8,4},{12,8},{16,12},{20,16},{24,20},{28,24},{1,29},{... | collective-permute-start | bytes 786440 | tf_op jit(solution)/shard_map/ppermute | solution.py:360
  579.2 22.6 %collective-permute-start.83 = (bf16[128,2048]{1,0:T(8,128)(2,1)}, bf16[128,2048]{1,0:T(8,128)(2,1)S(1)}, u32[]{:S(2)}, u32[]{:S(2)}) collective-permute-start(bf16[128,2048]{1,0:T(8,128)(2,1)} %get-tuple-element.489), channel_id=1, source_target_pairs={{0,8},{8,16},{16,24},{24,28},{28,20},{20,12},{12,4},{4,0},{1,9},{9... | collective-permute-start | bytes 1572872 | tf_op jit(solution)/shard_map/ppermute | solution.py:121
  591.1 13.7 %collective-permute-start.84 = (bf16[128,2048]{1,0:T(8,128)(2,1)}, bf16[128,2048]{1,0:T(8,128)(2,1)S(1)}, u32[]{:S(2)}, u32[]{:S(2)}) collective-permute-start(bf16[128,2048]{1,0:T(8,128)(2,1)} %get-tuple-element.490), channel_id=1, source_target_pairs={{8,0},{16,8},{24,16},{28,24},{20,28},{12,20},{4,12},{0,4},{9,1},{1... | collective-permute-start | bytes 1572872 | tf_op jit(solution)/shard_map/ppermute | solution.py:121
  608.2 27.7 %collective-permute-start.85 = (bf16[128,2048]{1,0:T(8,128)(2,1)}, bf16[128,2048]{1,0:T(8,128)(2,1)S(1)}, u32[]{:S(2)}, u32[]{:S(2)}) collective-permute-start(bf16[128,2048]{1,0:T(8,128)(2,1)} %get-tuple-element.496), channel_id=1, source_target_pairs={{0,8},{8,16},{16,24},{24,28},{28,20},{20,12},{12,4},{4,0},{1,9},{9... | collective-permute-start | bytes 1572872 | tf_op jit(solution)/shard_map/ppermute | solution.py:121
  609.9 29.1 %collective-permute-start.86 = (bf16[128,2048]{1,0:T(8,128)(2,1)}, bf16[128,2048]{1,0:T(8,128)(2,1)S(1)}, u32[]{:S(2)}, u32[]{:S(2)}) collective-permute-start(bf16[128,2048]{1,0:T(8,128)(2,1)} %get-tuple-element.497), channel_id=1, source_target_pairs={{8,0},{16,8},{24,16},{28,24},{20,28},{12,20},{4,12},{0,4},{9,1},{1... | collective-permute-start | bytes 1572872 | tf_op jit(solution)/shard_map/ppermute | solution.py:121
  612.6 15.5 %collective-permute-start.88 = (bf16[64,768]{1,0:T(8,128)(2,1)}, bf16[64,768]{1,0:T(8,128)(2,1)S(1)}, u32[]{:S(2)}, u32[]{:S(2)}) collective-permute-start(bf16[64,768]{1,0:T(8,128)(2,1)} %get-tuple-element.501), channel_id=1, source_target_pairs={{0,8},{4,12},{8,16},{12,20},{16,24},{20,28},{24,0},{28,4},{1,9},{5... | collective-permute-start | bytes 294920 | tf_op jit(solution)/shard_map/ppermute | solution.py:360
  614.0 17.4 %collective-permute-start.87 = (bf16[64,768]{1,0:T(8,128)(2,1)}, bf16[64,768]{1,0:T(8,128)(2,1)S(1)}, u32[]{:S(2)}, u32[]{:S(2)}) collective-permute-start(bf16[64,768]{1,0:T(8,128)(2,1)} %get-tuple-element.500), channel_id=1, source_target_pairs={{0,4},{4,8},{8,12},{12,16},{16,20},{20,24},{24,28},{28,0},{1,5},{5... | collective-permute-start | bytes 294920 | tf_op jit(solution)/shard_map/ppermute | solution.py:360
  616.3 18.3 %collective-permute-start.89 = (bf16[64,768]{1,0:T(8,128)(2,1)}, bf16[64,768]{1,0:T(8,128)(2,1)S(1)}, u32[]{:S(2)}, u32[]{:S(2)}) collective-permute-start(bf16[64,768]{1,0:T(8,128)(2,1)} %get-tuple-element.502), channel_id=1, source_target_pairs={{0,12},{4,16},{8,20},{12,24},{16,28},{20,0},{24,4},{28,8},{1,13},{... | collective-permute-start | bytes 294920 | tf_op jit(solution)/shard_map/ppermute | solution.py:360
  (155 other events, 1973.0 us)
Sparse Core Ops, SparseCore 0:
  10.2 70.5 all-gather.4
  112.4 55.5 all-gather.6
  169.5 34.4 all-gather.8
  228.6 59.7 all-gather.10
  412.4 71.6 reduce-scatter.4
  486.7 44.5 reduce-scatter.6
  556.0 36.2 reduce-scatter.8
  604.9 27.8 reduce-scatter.10
